TPU v7x, 128 devices: a whole 4x4x4 slice. The times are simulated.
128 devices in a mesh: rows: 4 (over z_lo, core), blk: 32 (over x, y, z_hi).
Axes of the slice: x: 4, y: 4, z: 4 (z_hi: 2, z_lo: 2; z = z_hi * 2 + z_lo), core: 2. Of those that a mesh axis runs over, the one named last changes fastest.
Arguments:
- tokens: bfloat16 [8, 2048, 1024], P('rows', 'blk'), may hold values from -6 to 6
- lengths: int32 [8], P('rows'), may hold values from 128 to 2048, as said below
- routes: int32 [8, 2048, 8], P('rows', 'blk'), may hold values from 0 to 31, all different within a row; in each aligned block of 64 rows (0 to 63, 64 to 127, ..., all dimensions but the last counted through in order) at most 24 rows name the same one
- gates: float32 [8, 2048, 8], P('rows', 'blk'), may hold values from 0.05 to 0.25
- gain_attn: float32 [1024], replicated, may hold values from 0.5 to 1.5
- w_qkv: bfloat16 [1024, 2048], replicated, may hold values from -0.1875 to 0.1875
- w_out: bfloat16 [1024, 1024], replicated, may hold values from -0.75 to 0.75
- gain_moe: float32 [1024], replicated, may hold values from 0.5 to 1.5
- w_gate_up: bfloat16 [32, 1024, 1024], P('blk'), may hold values from -0.1875 to 0.1875
- w_down: bfloat16 [32, 512, 1024], P('blk'), may hold values from -1 to 1
- cotangent: bfloat16 [8, 2048, 1024], P('rows', 'blk'), may hold values from -6 to 6
Outputs:
- mixed_out: bfloat16 [8, 2048, 1024], P('rows', 'blk')
- grad_tokens: float32 [8, 2048, 1024], P('rows', 'blk')
- grad_gain_attn: float32 [1024], replicated
- grad_qkv: float32 [1024, 2048], replicated
- grad_out: float32 [1024, 1024], replicated
- grad_gain_moe: float32 [1024], replicated
- grad_gate_up: float32 [32, 1024, 1024], P('blk')
- grad_down: float32 [32, 512, 1024], P('blk')
Inputs may be any that keep to these rules, and one draw needn't show every extreme that they name: `routes`: within each aligned block of 64 tokens of one sequence, no expert is named by more than 24 tokens; a token names 8 different experts. `lengths`: in each group of 2 consecutive sequences one, drawn from the seed, has length 2048; the others are shorter.
All inputs are finite; a program needn't handle non-finite values.
Results may differ from a plain program's by a relative error of at most 0.02.
Values may be sent and summed in bfloat16 or wider, within the bound.
No kernel may reach another device: no remote copies, remote signals or barrier semaphores. Data moves between devices by JAX's collectives and lax.ppermute only.
A program may use at most 128 MiB of HBM per device.

v0:
```python
import jax
import jax.numpy as jnp
from jax import lax
from jax.sharding import PartitionSpec as P

HEADS = 16
KV_HEADS = 8
HEAD = 64
FF_EXP = 512
TOP = 8


EPS = 1e-06
ROPE_BASE = 10000.0


def norm_rows(vectors, gain_vec):
    inverse = lax.rsqrt(jnp.mean(vectors * vectors, axis=-1, keepdims=True) + EPS)
    scaled = vectors * inverse
    return (scaled * gain_vec, scaled, inverse)


def norm_back(incoming, gain_vec, scaled, inverse):
    grad_scaled = incoming * gain_vec
    grad_input = inverse * (
        grad_scaled - scaled * jnp.mean(grad_scaled * scaled, axis=-1, keepdims=True)
    )
    grad_gain = jnp.sum((incoming * scaled).reshape(-1, scaled.shape[-1]), axis=0)
    return (grad_input, grad_gain)


def rope_tables(positions):
    half_head = HEAD // 2
    frequency = ROPE_BASE ** (-jnp.arange(half_head, dtype=jnp.float32) / half_head)
    angles = positions.astype(jnp.float32)[:, None] * frequency[None, :]
    return (jnp.cos(angles)[:, None, :], jnp.sin(angles)[:, None, :])


def rotate(vectors, cosine, sine_table):
    half_head = HEAD // 2
    front_half = vectors[..., :half_head]
    back_half = vectors[..., half_head:]
    return jnp.concatenate(
        [
            front_half * cosine - back_half * sine_table,
            back_half * cosine + front_half * sine_table,
        ],
        -1,
    )


def rotate_back(incoming, cosine, sine_table):
    half_head = HEAD // 2
    front_half = incoming[..., :half_head]
    back_half = incoming[..., half_head:]
    return jnp.concatenate(
        [
            front_half * cosine + back_half * sine_table,
            back_half * cosine - front_half * sine_table,
        ],
        -1,
    )


def contract_rows(left, right):
    return lax.dot_general(
        left, right, (((0,), (0,)), ((), ())), preferred_element_type=jnp.float32
    )


def times_transposed(left, right):
    return lax.dot_general(
        left, right, (((1,), (1,)), ((), ())), preferred_element_type=jnp.float32
    )


def shards(
    tokens, lengths, routes, gates, gain_attn, w_qkv, w_out, gain_moe, w_gate_up, w_down, cotangent
):
    cycle_size = lax.axis_size("blk")
    cycle_index = lax.axis_index("blk")
    seq_count, local_len, model_width = tokens.shape
    local_experts = w_gate_up.shape[0]
    expert_count = local_experts * cycle_size
    q_width = HEADS * HEAD
    kv_width = KV_HEADS * HEAD
    groups = HEADS // KV_HEADS
    score_scale = HEAD ** (-0.5)
    capacity = min(local_len, max(2, 3 * local_len * TOP // (2 * expert_count)))
    first_row = cycle_index * local_len
    cosine, sine_table = rope_tables(first_row + jnp.arange(local_len, dtype=jnp.int32))
    inputs = tokens.astype(jnp.float32)
    normed_f, scaled_attn, inverse_attn = norm_rows(inputs, gain_attn)
    normed = normed_f.astype(jnp.bfloat16)
    projected = jnp.dot(normed.reshape(-1, model_width), w_qkv, preferred_element_type=jnp.float32)
    projected = projected.reshape(seq_count, local_len, -1)
    queries = rotate(
        projected[..., :q_width].reshape(seq_count, local_len, HEADS, HEAD), cosine, sine_table
    ).astype(jnp.bfloat16)
    key_rows = rotate(
        projected[..., q_width : q_width + kv_width].reshape(seq_count, local_len, KV_HEADS, HEAD),
        cosine,
        sine_table,
    ).astype(jnp.bfloat16)
    value_rows = projected[..., q_width + kv_width :].astype(jnp.bfloat16)
    pairs_local = jnp.concatenate(
        [key_rows.reshape(seq_count, local_len, kv_width), value_rows], -1
    )
    pairs_all = lax.all_gather(pairs_local, "blk", axis=1, tiled=True)
    grouped = queries.reshape(seq_count, local_len, KV_HEADS, groups, HEAD)

    def scores_of(query_part, all_keys, seq_length):
        scores = (
            jnp.einsum("tkgd,jkd->kgtj", query_part, all_keys, preferred_element_type=jnp.float32)
            * score_scale
        )
        query_pos = first_row + jnp.arange(query_part.shape[0], dtype=jnp.int32)
        key_pos = jnp.arange(all_keys.shape[0], dtype=jnp.int32)
        allowed = (key_pos[None, :] <= query_pos[:, None]) & (key_pos[None, :] < seq_length)
        return jnp.where(allowed, scores, -1e30)

    def attend(operands):
        query_part, pairs, seq_length = operands
        all_keys = pairs[:, :kv_width].reshape(-1, KV_HEADS, HEAD)
        all_values = pairs[:, kv_width:].reshape(-1, KV_HEADS, HEAD)
        scores = scores_of(query_part, all_keys, seq_length)
        row_max = jnp.max(scores, axis=-1, keepdims=True)
        exp_scores = jnp.exp(scores - row_max)
        row_total = jnp.sum(exp_scores, axis=-1, keepdims=True)
        soft_weights = (exp_scores / row_total).astype(jnp.bfloat16)
        attended = jnp.einsum(
            "kgtj,jkd->tkgd", soft_weights, all_values, preferred_element_type=jnp.float32
        )
        return (
            attended.astype(jnp.bfloat16).reshape(query_part.shape[0], q_width),
            (row_max + jnp.log(row_total))[..., 0],
        )

    attended, log_totals = lax.map(attend, (grouped, pairs_all, lengths))
    branch = jnp.dot(attended.reshape(-1, q_width), w_out, preferred_element_type=jnp.float32)
    residual = inputs + branch.reshape(seq_count, local_len, model_width)
    normed_moe_f, scaled_moe, inverse_moe = norm_rows(residual, gain_moe)
    normed_moe = normed_moe_f.astype(jnp.bfloat16)
    expert_ids = jnp.arange(expert_count, dtype=jnp.int32)
    matches = routes[..., None] == expert_ids
    chosen = jnp.sum(matches.astype(jnp.int32), axis=2)
    picked_gate = jnp.sum(jnp.where(matches, gates[..., None], 0.0), axis=2)
    ranking = jnp.cumsum(chosen, axis=1) - chosen
    slot_ids = jnp.arange(capacity, dtype=jnp.int32)
    placed = (chosen.transpose(2, 0, 1)[:, :, None, :] == 1) & (
        ranking.transpose(2, 0, 1)[:, :, None, :] == slot_ids[None, None, :, None]
    )
    dispatch = placed.astype(jnp.bfloat16)
    combine = jnp.where(placed, picked_gate.transpose(2, 0, 1)[:, :, None, :], 0.0)
    outgoing = jnp.einsum(
        "esmt,std->esmd", dispatch, normed_moe, preferred_element_type=jnp.float32
    ).astype(jnp.bfloat16)
    outgoing = outgoing.reshape(cycle_size, local_experts, seq_count, capacity, model_width)
    arrived_rows = lax.all_to_all(outgoing, "blk", split_axis=0, concat_axis=0, tiled=True)
    pre_act = jnp.einsum(
        "nesmd,edf->nesmf", arrived_rows, w_gate_up, preferred_element_type=jnp.float32
    )
    hidden_rows = (jax.nn.silu(pre_act[..., :FF_EXP]) * pre_act[..., FF_EXP:]).astype(jnp.bfloat16)
    produced = jnp.einsum(
        "nesmf,efd->nesmd", hidden_rows, w_down, preferred_element_type=jnp.float32
    ).astype(jnp.bfloat16)
    sent_back = lax.all_to_all(produced, "blk", split_axis=0, concat_axis=0, tiled=True)
    returned_f = sent_back.reshape(expert_count, seq_count, capacity, model_width).astype(
        jnp.float32
    )
    expert_sum = jnp.einsum("esmt,esmd->std", combine, returned_f, precision=lax.Precision.HIGHEST)
    mixed_out = (residual + expert_sum).astype(jnp.bfloat16)
    grad_mixed = cotangent.astype(jnp.float32)
    grad_expert = jnp.einsum(
        "esmt,std->esmd", combine, grad_mixed, precision=lax.Precision.HIGHEST
    ).astype(jnp.bfloat16)
    grad_expert = grad_expert.reshape(cycle_size, local_experts, seq_count, capacity, model_width)
    grad_produced = lax.all_to_all(grad_expert, "blk", split_axis=0, concat_axis=0, tiled=True)
    gate_pre = pre_act[..., :FF_EXP]
    up_pre = pre_act[..., FF_EXP:]
    sigmoid_gate = jax.nn.sigmoid(gate_pre)
    activated = gate_pre * sigmoid_gate
    grad_down = jnp.einsum(
        "nesmf,nesmd->efd", hidden_rows, grad_produced, preferred_element_type=jnp.float32
    )
    grad_hidden = jnp.einsum(
        "nesmd,efd->nesmf", grad_produced, w_down, preferred_element_type=jnp.float32
    )
    grad_gate_pre = grad_hidden * up_pre * sigmoid_gate * (1.0 + gate_pre * (1.0 - sigmoid_gate))
    grad_up_pre = grad_hidden * activated
    grad_pre = jnp.concatenate([grad_gate_pre, grad_up_pre], -1).astype(jnp.bfloat16)
    grad_gate_up = jnp.einsum(
        "nesmd,nesmf->edf", arrived_rows, grad_pre, preferred_element_type=jnp.float32
    )
    grad_rows = jnp.einsum(
        "nesmf,edf->nesmd", grad_pre, w_gate_up, preferred_element_type=jnp.float32
    ).astype(jnp.bfloat16)
    grad_back = lax.all_to_all(grad_rows, "blk", split_axis=0, concat_axis=0, tiled=True)
    grad_back = grad_back.reshape(expert_count, seq_count, capacity, model_width)
    grad_normed_moe = jnp.einsum(
        "esmt,esmd->std", dispatch, grad_back, preferred_element_type=jnp.float32
    )
    grad_from_moe, grad_gain_moe = norm_back(grad_normed_moe, gain_moe, scaled_moe, inverse_moe)
    grad_residual = grad_mixed + grad_from_moe
    grad_branch = grad_residual.astype(jnp.bfloat16).reshape(-1, model_width)
    grad_out = contract_rows(attended.reshape(-1, q_width), grad_branch)
    grad_attended = times_transposed(grad_branch, w_out).astype(jnp.bfloat16)
    grad_attended = grad_attended.reshape(seq_count, local_len, KV_HEADS, groups, HEAD)

    def attend_back(operands):
        query_part, pairs, seq_length, log_total, grad_part = operands
        all_keys = pairs[:, :kv_width].reshape(-1, KV_HEADS, HEAD)
        all_values = pairs[:, kv_width:].reshape(-1, KV_HEADS, HEAD)
        scores = scores_of(query_part, all_keys, seq_length)
        soft_weights = jnp.exp(scores - log_total[..., None])
        rounded = soft_weights.astype(jnp.bfloat16)
        grad_values = jnp.einsum(
            "kgtj,tkgd->jkd", rounded, grad_part, preferred_element_type=jnp.float32
        )
        grad_weights = jnp.einsum(
            "tkgd,jkd->kgtj", grad_part, all_values, preferred_element_type=jnp.float32
        )
        row_inner = jnp.sum(grad_weights * soft_weights, axis=-1, keepdims=True)
        grad_scores = (soft_weights * (grad_weights - row_inner)).astype(jnp.bfloat16)
        grad_query = (
            jnp.einsum("kgtj,jkd->tkgd", grad_scores, all_keys, preferred_element_type=jnp.float32)
            * score_scale
        )
        grad_keys = (
            jnp.einsum(
                "kgtj,tkgd->jkd", grad_scores, query_part, preferred_element_type=jnp.float32
            )
            * score_scale
        )
        key_count = all_keys.shape[0]
        return (
            grad_query,
            jnp.concatenate(
                [grad_keys.reshape(key_count, kv_width), grad_values.reshape(key_count, kv_width)],
                -1,
            ),
        )

    grad_queries, grad_pairs = lax.map(
        attend_back, (grouped, pairs_all, lengths, log_totals, grad_attended)
    )
    grad_pairs_local = lax.psum_scatter(
        grad_pairs.astype(jnp.bfloat16), "blk", scatter_dimension=1, tiled=True
    ).astype(jnp.float32)
    grad_queries = rotate_back(
        grad_queries.reshape(seq_count, local_len, HEADS, HEAD), cosine, sine_table
    )
    grad_keys_local = rotate_back(
        grad_pairs_local[..., :kv_width].reshape(seq_count, local_len, KV_HEADS, HEAD),
        cosine,
        sine_table,
    )
    grad_proj = jnp.concatenate(
        [
            grad_queries.reshape(seq_count, local_len, q_width),
            grad_keys_local.reshape(seq_count, local_len, kv_width),
            grad_pairs_local[..., kv_width:],
        ],
        -1,
    ).astype(jnp.bfloat16)
    grad_proj = grad_proj.reshape(seq_count * local_len, -1)
    grad_qkv = contract_rows(normed.reshape(-1, model_width), grad_proj)
    grad_normed = times_transposed(grad_proj, w_qkv).reshape(seq_count, local_len, model_width)
    grad_from_attn, grad_gain_attn = norm_back(grad_normed, gain_attn, scaled_attn, inverse_attn)
    grad_tokens = grad_residual + grad_from_attn
    summed_gain_attn, summed_qkv, summed_out, summed_gain_moe = lax.psum(
        (grad_gain_attn, grad_qkv, grad_out, grad_gain_moe), ("rows", "blk")
    )
    summed_gate_up, summed_down = (
        lax.psum(grad_gate_up.astype(jnp.bfloat16), "rows").astype(jnp.float32),
        lax.psum(grad_down.astype(jnp.bfloat16), "rows").astype(jnp.float32),
    )
    return (
        mixed_out,
        grad_tokens,
        summed_gain_attn,
        summed_qkv,
        summed_out,
        summed_gain_moe,
        summed_gate_up,
        summed_down,
    )


def solution(mesh):
    return jax.shard_map(
        shards,
        mesh=mesh,
        in_specs=(
            P("rows", "blk", None),
            P("rows"),
            P("rows", "blk", None),
            P("rows", "blk", None),
            P(),
            P(),
            P(),
            P(),
            P("blk", None, None),
            P("blk", None, None),
            P("rows", "blk", None),
        ),
        out_specs=(
            P("rows", "blk", None),
            P("rows", "blk", None),
            P(),
            P(),
            P(),
            P(),
            P("blk", None, None),
            P("blk", None, None),
        ),
        check_vma=False,
    )
```

profile of v0, /device:TPU:1, one launch (start us, length us, event | category | flops | bytes accessed | tf_op | source)
XLA Modules:
  0.0 886.7 jit_solution(9838131638784037380)
XLA Ops:
  8.5 3.1 fusion.38
  20.5 101.8 %all-gather.2.cloned.1.call-done = bf16[2,2048,1024]{2,1,0:T(8,128)(2,1)} async-done(((bf16[2,64,1024]{2,1,0:T(8,128)(2,1)}), bf16[2,2048,1024]{2,1,0:T(8,128)(2,1)}) %all-gather.2.cloned.1.call-update) | async-done | bytes 8388624 | tf_op jit(solution)/shard_map/all_gather | solution.py:109
  122.3 11.6 %copy.75 = bf16[2,2048,1024]{1,2,0:T(8,128)(2,1)} copy(bf16[2,2048,1024]{2,1,0:T(8,128)(2,1)} %all-gather.2.cloned.1.call-done) | data formatting | bytes 16777216 | tf_op jit(solution)/shard_map/while | solution.py:139
  133.9 22.3 %while.24 = (s32[]{:T(128)}, bf16[2,64,1024]{1,2,0:T(8,128)(2,1)S(1)}, f32[2,8,2,64]{3,2,1,0:T(2,128)S(1)}, bf16[2,2048,1024]{1,2,0:T(8,128)(2,1)}, s32[]{:T(128...) while((s32[]{:T(128)}, bf16[2,64,1024]{1,2,0:T(8,128)(2,1)S(1)}, ...), condition=%wide.region_4.5_spmd, body=%wide.region_1.4_spmd.sunk | while | flops 562365504 | bytes 47628920 | solution.py:139
  135.3 2.5 dynamic-slice_bitcast_fusion.6
  142.2 2.7 fusion.177
  146.5 2.5 dynamic-slice_bitcast_fusion.6
  153.4 2.7 fusion.177
  160.4 3.4 copy.80
  163.8 5.9 all-to-all-start
  170.5 2.9 convert_bitcast_fusion.1
  175.5 34.5 %all-to-all-done = bf16[32,1,2,24,1024]{4,3,2,1,0:T(8,128)(2,1)} async-done(((bf16[32,1,2,24,1024]{4,3,2,1,0:T(8,128)(2,1)}), bf16[32,1,2,24,1024]{4,3,2,1,0:T(8,128)(2,1)}, u32[]{:S(2)}, u32[]{:S(2)}) %all-to-all-start) | async-done | bytes 3145760 | tf_op jit(solution)/shard_map/all_to_all | solution.py:159
  210.0 6.0 all-to-all-start.2
  216.0 7.3 fusion.59
  223.3 30.3 %all-to-all-done.2 = bf16[32,1,2,24,1024]{4,3,2,1,0:T(8,128)(2,1)} async-done(((bf16[32,1,2,24,1024]{4,3,2,1,0:T(8,128)(2,1)}), bf16[32,1,2,24,1024]{4,3,2,1,0:T(8,128)(2,1)}, u32[]{:S(2)}, u32[]{:S(2)}) %all-to-all-start.2) | async-done | bytes 3145760 | tf_op jit(solution)/shard_map/all_to_all | solution.py:178
  253.5 8.4 fusion.73
  263.6 4.9 convert_bitcast_fusion
  268.5 7.4 all-to-all-start.3
  276.0 40.8 %all-to-all-done.3 = bf16[32,1,2,24,1024]{4,3,2,1,0:T(8,128)(2,1)} async-done(((bf16[32,1,2,24,1024]{4,3,2,1,0:T(8,128)(2,1)}), bf16[32,1,2,24,1024]{4,3,2,1,0:T(8,128)(2,1)}, u32[]{:S(2)}, u32[]{:S(2)}) %all-to-all-start.3) | async-done | bytes 3145760 | tf_op jit(solution)/shard_map/all_to_all | solution.py:198
  316.7 4.6 multiply_reduce_fusion
  323.5 64.7 %while.25 = (s32[]{:T(128)}, f32[2,64,8,2,64]{1,4,3,2,0:T(8,128)}, bf16[2,2048,1024]{2,1,0:T(8,128)(2,1)}, bf16[2,2048,1024]{1,2,0:T(8,128)(2,1)}, s32[]{:T(128)...) while((s32[]{:T(128)}, f32[2,64,8,2,64]{1,4,3,2,0:T(8,128)}, ...), condition=%wide.region_12.13_spmd, body=%wide.region_10.12_spmd.sunk | while | flops 1384449024 | bytes 151029456 | solution.py:244
  323.7 2.5 dynamic-slice_bitcast_fusion.7
  329.4 3.0 fusion.189
  332.4 2.4 fusion.190
  336.8 2.6 fusion.192
  341.8 6.4 copy.153
  348.2 4.8 constant_dynamic-update-slice_fusion.5
  353.0 2.9 fusion.191
  355.9 2.5 dynamic-slice_bitcast_fusion.7
  361.6 3.0 fusion.189
  364.7 2.4 fusion.190
  369.0 2.6 fusion.192
  374.0 6.4 copy.153
  380.4 4.8 constant_dynamic-update-slice_fusion.5
  385.3 2.9 fusion.191
  389.6 4.8 fusion.74
  394.4 7.0 fusion.62
  405.0 2.8 convolution_bitcast_fusion.1
  407.7 163.5 %reduce-scatter.2.cloned.1.call-done = bf16[2,64,1024]{2,1,0:T(8,128)(2,1)} async-done(((bf16[2,2048,1024]{2,1,0:T(8,128)(2,1)}), bf16[2,64,1024]{2,1,0:T(8,128)(2,1)}) %reduce-scatter.2.cloned.1.call-update) | async-done | bytes 262160 | tf_op jit(solution)/shard_map/reduce_scatter | solution.py:247
  573.1 4.8 convolution_bitcast_fusion
  579.0 3.2 convert_bitcast_fusion.2
  582.3 36.6 %all_to_all.20 = bf16[32,1,2,24,1024]{4,3,2,1,0:T(8,128)(2,1)S(1)} all-to-all(bf16[32,1,2,24,1024]{4,3,2,1,0:T(8,128)(2,1)S(1)} %convert_bitcast_fusion.2), channel_id=1, replica_groups=mesh['rows'=4,'blk'=32] {'blk'}, dimensions={0} | all-to-all | bytes 6291456 | tf_op jit(solution)/shard_map/all_to_all | solution.py:167
  618.9 4.0 fusion.89
  622.9 70.8 %all-reduce.8.cloned.1.call-done = (bf16[1,1024,1024]{2,1,0:T(8,128)(2,1)}, bf16[1,512,1024]{2,1,0:T(8,128)(2,1)}) async-done(((bf16[1,1024,1024]{2,1,0:T(8,128)(2,1)}, bf16[1,512,1024]{2,1,0:T(8,128)(2,1)}), (bf16[1,1024,1024]{2,1,0:T(8,128)(2,1)}, bf16[1,512,1024]{2,1,0:T(8,128)(2,1)})) %all-reduce.8.cloned.1.call-update) | async-done | bytes 3145744 | tf_op jit(solution)/shard_map/psum | solution.py:275
  693.7 4.2 convert_element_type.151
  701.2 67.0 %all-reduce = (f32[1024]{0:T(1024)}, f32[1024]{0:T(1024)}) all-reduce(f32[1024]{0:T(1024)S(1)} %get-tuple-element.148, f32[1024]{0:T(1024)S(1)} %copy-done.43), channel_id=1, replica_groups=mesh['rows'=4,'blk'=32] {'rows','blk'}, use_global_device_ids=true, to_apply=%region_16.17 | all-reduce | flops 2048 | bytes 16384 | tf_op jit(solution)/shard_map/psum | solution.py:271
  769.3 100.4 %all-reduce.6.cloned.1.call-done = (f32[1024,2048]{1,0:T(8,128)}, f32[1024,1024]{1,0:T(8,128)}) async-done(((f32[1024,2048]{1,0:T(8,128)}, f32[1024,1024]{1,0:T(8,128)}), (f32[1024,2048]{1,0:T(8,128)}, f32[1024,1024]{1,0:T(8,128)})) %all-reduce.6.cloned.1.call-update) | async-done | bytes 12582928 | tf_op jit(solution)/shard_map/psum | solution.py:271
  869.7 8.0 copy.182
  (207 shorter events, 61.7 us)
Async XLA Ops:
  7.2 208.8 %copy-start = (bf16[1,1024,1024]{2,1,0:T(8,128)(2,1)S(1)}, bf16[1,1024,1024]{2,1,0:T(8,128)(2,1)}, u32[]{:S(2)}) copy-start(bf16[1,1024,1024]{2,1,0:T(8,128)(2,1)} %param.23) | copy-start | bytes 6291460
  7.2 115.1 %all-gather.2.cloned.1.call-start = ((), (), s32[]{:S(2)}) async-start(), calls=%async_computation.5 | async-start | bytes 8650752 | tf_op jit(solution)/shard_map/all_gather | solution.py:109
  8.5 3.1 copy-start.31
  12.9 4.7 copy-start.22
  12.9 4.7 copy-start.24
  14.4 4.4 copy-start.35
  19.1 297.7 %copy-start.27 = (s32[32,2,64]{2,0,1:T(8,128)}, s32[32,2,64]{2,0,1:T(8,128)S(1)}, u32[]{:S(2)}) copy-start(s32[32,2,64]{2,0,1:T(8,128)S(1)} %copy.79) | copy-start | bytes 49156
  20.5 296.3 %copy-start.33 = (pred[32,2,64]{2,0,1:T(8,128)(4,1)}, pred[32,2,64]{2,0,1:T(8,128)(4,1)S(1)}, u32[]{:S(2)}) copy-start(pred[32,2,64]{2,0,1:T(8,128)(4,1)S(1)} %compare_bitcast_fusion) | copy-start | bytes 12292
  20.5 113.4 %copy-start.16 = (bf16[2,64,1024]{1,2,0:T(8,128)(2,1)S(1)}, bf16[2,64,1024]{1,2,0:T(8,128)(2,1)}, u32[]{:S(2)}) copy-start(bf16[2,64,1024]{1,2,0:T(8,128)(2,1)} %custom-call) | copy-start | bytes 786436
  20.5 113.4 %copy-start.45 = (s32[2]{0:T(128)S(1)}, s32[2]{0:T(128)}, u32[]{:S(2)}) copy-start(s32[2]{0:T(128)} %param.16) | copy-start | bytes 28
  133.9 23.1 %copy-start.5 = (bf16[2,64,1024]{2,1,0:T(8,128)(2,1)S(1)}, bf16[2,64,1024]{2,1,0:T(8,128)(2,1)}, u32[]{:S(2)}) copy-start(bf16[2,64,1024]{2,1,0:T(8,128)(2,1)} %param.15) | copy-start | bytes 786436
  157.0 2.4 copy-start.36
  159.3 162.0 %copy-start.8 = (f32[2,64,1024]{2,1,0:T(8,128)}, f32[2,64,1024]{2,1,0:T(8,128)S(1)}, u32[]{:S(2)}) copy-start(f32[2,64,1024]{2,1,0:T(8,128)S(1)} %get-tuple-element.214) | copy-start | bytes 1572868
  159.3 162.0 %copy-start.38 = (f32[2,64]{1,0:T(2,128)}, f32[2,64]{1,0:T(2,128)S(1)}, u32[]{:S(2)}) copy-start(f32[2,64]{1,0:T(2,128)S(1)} %add_rsqrt_fusion) | copy-start | bytes 1540
  163.8 6.0 copy-start.42
  163.8 6.7 copy-start.12
  163.8 46.2 %all-to-all-start = ((bf16[32,1,2,24,1024]{4,3,2,1,0:T(8,128)(2,1)}), bf16[32,1,2,24,1024]{4,3,2,1,0:T(8,128)(2,1)}, u32[]{:S(2)}, u32[]{:S(2)}) async-start(bf16[32,1,2,24,1024]{4,3,2,1,0:T(8,128)(2,1)} %copy.80), calls=%async_computation | async-start | bytes 6291456 | tf_op jit(solution)/shard_map/all_to_all | solution.py:159
  210.0 43.6 %all-to-all-start.2 = ((bf16[32,1,2,24,1024]{4,3,2,1,0:T(8,128)(2,1)}), bf16[32,1,2,24,1024]{4,3,2,1,0:T(8,128)(2,1)}, u32[]{:S(2)}, u32[]{:S(2)}) async-start(bf16[32,1,2,24,1024]{4,3,2,1,0:T(8,128)(2,1)} %copy.84), calls=%async_computation.2 | async-start | bytes 6291456 | tf_op jit(solution)/shard_map/all_to_all | solution.py:178
  268.5 48.2 %all-to-all-start.3 = ((bf16[32,1,2,24,1024]{4,3,2,1,0:T(8,128)(2,1)}), bf16[32,1,2,24,1024]{4,3,2,1,0:T(8,128)(2,1)}, u32[]{:S(2)}, u32[]{:S(2)}) async-start(bf16[32,1,2,24,1024]{4,3,2,1,0:T(8,128)(2,1)} %convert_bitcast_fusion), calls=%async_computation.3 | async-start | bytes 6291456 | tf_op jit(solution)/shard_map/all_to_all | solution.py:198
  275.9 46.4 %copy-start.4 = (bf16[1024,1024]{1,0:T(8,128)(2,1)S(1)}, bf16[1024,1024]{1,0:T(8,128)(2,1)}, u32[]{:S(2)}) copy-start(bf16[1024,1024]{1,0:T(8,128)(2,1)} %param.21) | copy-start | bytes 6291460
  275.9 295.4 %reduce-scatter.2.cloned.1.call-start = ((), (), s32[]{:S(2)}) async-start(), calls=%async_computation.6 | async-start | bytes 8650752 | tf_op jit(solution)/shard_map/reduce_scatter | solution.py:247
  321.3 2.1 copy-start.40
  334.8 2.0 copy-start.2
  348.2 4.8 copy-start.3
  367.0 2.0 copy-start.2
  380.4 4.8 copy-start.3
  388.2 305.5 %all-reduce.8.cloned.1.call-start = ((), (), s32[]{:S(2)}) async-start(), calls=%async_computation.8 | async-start | bytes 6291456 | tf_op jit(solution)/shard_map/psum | solution.py:275
  389.6 4.8 copy-start.48
  389.6 4.8 copy-start.50
  401.4 2.4 copy-start.23
  401.4 2.4 copy-start.25
  401.5 468.2 %all-reduce.6.cloned.1.call-start = ((), (), s32[]{:S(2)}) async-start(), calls=%async_computation.7 | async-start | bytes 25165824 | tf_op jit(solution)/shard_map/psum | solution.py:271
  407.7 165.3 %copy-start.6 = (bf16[2,64,1024]{2,1,0:T(8,128)(2,1)S(1)}, bf16[2,64,1024]{2,1,0:T(8,128)(2,1)}, u32[]{:S(2)}) copy-start(bf16[2,64,1024]{2,1,0:T(8,128)(2,1)} %param.15) | copy-start | bytes 786436
  407.7 165.3 %copy-start.26 = (f32[1024]{0:T(1024)S(1)}, f32[1024]{0:T(1024)}, u32[]{:S(2)}) copy-start(f32[1024]{0:T(1024)} %param.19) | copy-start | bytes 12292
  407.7 165.3 %copy-start.32 = (f32[2,64]{1,0:T(2,128)S(1)}, f32[2,64]{1,0:T(2,128)}, u32[]{:S(2)}) copy-start(f32[2,64]{1,0:T(2,128)} %copy-done.31) | copy-start | bytes 1540
  582.2 36.6 %copy-start.9 = (f32[2,64,1024]{2,1,0:T(8,128)S(1)}, f32[2,64,1024]{2,1,0:T(8,128)}, u32[]{:S(2)}) copy-start(f32[2,64,1024]{2,1,0:T(8,128)} %copy-done.8) | copy-start | bytes 1572868
  582.3 36.6 %copy-start.28 = (s32[32,2,64]{2,0,1:T(8,128)S(1)}, s32[32,2,64]{2,0,1:T(8,128)}, u32[]{:S(2)}) copy-start(s32[32,2,64]{2,0,1:T(8,128)} %copy-done.27) | copy-start | bytes 49156
  582.3 36.6 %copy-start.30 = (f32[2,64,32]{1,2,0:T(8,128)S(1)}, f32[2,64,32]{1,2,0:T(8,128)}, u32[]{:S(2)}) copy-start(f32[2,64,32]{1,2,0:T(8,128)} %copy-done.29) | copy-start | bytes 49156
  582.3 36.6 %copy-start.34 = (pred[32,2,64]{2,0,1:T(8,128)(4,1)S(1)}, pred[32,2,64]{2,0,1:T(8,128)(4,1)}, u32[]{:S(2)}) copy-start(pred[32,2,64]{2,0,1:T(8,128)(4,1)} %copy-done.33) | copy-start | bytes 12292
  693.7 4.2 copy-start.21
  693.7 5.8 copy-start.7
  699.5 68.7 %copy-start.13 = (bf16[2,64,1024]{2,1,0:T(8,128)(2,1)S(1)}, bf16[2,64,1024]{2,1,0:T(8,128)(2,1)}, u32[]{:S(2)}) copy-start(bf16[2,64,1024]{2,1,0:T(8,128)(2,1)} %param.25) | copy-start | bytes 786436
  699.5 68.7 %copy-start.20 = (f32[2,64,1024]{2,1,0:T(8,128)S(1)}, f32[2,64,1024]{2,1,0:T(8,128)}, u32[]{:S(2)}) copy-start(f32[2,64,1024]{2,1,0:T(8,128)} %copy-done.19) | copy-start | bytes 1572868
  699.5 68.7 %copy-start.37 = (f32[1024]{0:T(1024)S(1)}, f32[1024]{0:T(1024)}, u32[]{:S(2)}) copy-start(f32[1024]{0:T(1024)} %param.22) | copy-start | bytes 12292
  699.5 68.7 %copy-start.39 = (f32[2,64]{1,0:T(2,128)S(1)}, f32[2,64]{1,0:T(2,128)}, u32[]{:S(2)}) copy-start(f32[2,64]{1,0:T(2,128)} %copy-done.38) | copy-start | bytes 1540
  699.5 68.7 %copy-start.41 = (f32[2,64]{1,0:T(2,128)S(1)}, f32[2,64]{1,0:T(2,128)}, u32[]{:S(2)}) copy-start(f32[2,64]{1,0:T(2,128)} %copy-done.40) | copy-start | bytes 1540
  869.7 8.0 copy-start.10
  869.7 10.1 %copy-start.1 = (bf16[1,1024,1024]{2,1,0:T(8,128)(2,1)S(1)}, bf16[1,1024,1024]{2,1,0:T(8,128)(2,1)}, u32[]{:S(2)}) copy-start(bf16[1,1024,1024]{2,1,0:T(8,128)(2,1)} %param.23) | copy-start | bytes 6291460
  (13 other events, 14.9 us)
Sparse Core Ops, SparseCore 0:
  14.4 107.8 all-gather.1
  388.3 182.8 reduce-scatter.1
  574.4 119.1 all-reduce.7
  699.1 170.5 all-reduce.5
where the time goes:
time: 897 us; the launch traced here: 887 us
  waiting for transfers between devices  542 us (60%)
  blocking collectives  104 us (12%)
  matrix products  93.2 us (10%)
  local copies, waits for them, and re-layouts  80.4 us (9%)
  other arithmetic  32.4 us (4%)
  starting transfers between devices  19.4 us (2%)
  between operations  14.9 us (2%)
    reduce_scatter x1, waiting for transfers between devices, shards(): lax.psum_scatter(grad_pairs.astype(jnp.bfloat16), 'blk', scatter_dimensio...  164 us
    all_gather x1, waiting for transfers between devices, shards(): pairs_all = lax.all_gather(pairs_local, 'blk', axis=1, tiled=True)  102 us
    psum x1, waiting for transfers between devices, shards(): lax.psum((grad_gain_attn, grad_qkv, grad_out, grad_gain_moe), ('rows', 'b...  100 us
    psum x1, waiting for transfers between devices, shards(): lax.psum(grad_gate_up.astype(jnp.bfloat16), 'rows').astype(jnp.float32)  70.8 us
    psum x1, blocking collectives, shards(): lax.psum((grad_gain_attn, grad_qkv, grad_out, grad_gain_moe), ('rows', 'b...  67 us
    all_to_all x1, waiting for transfers between devices, shards(): lax.all_to_all(grad_rows, 'blk', split_axis=0, concat_axis=0, tiled=True)  40.8 us
    all_to_all x1, blocking collectives, shards(): lax.all_to_all(produced, 'blk', split_axis=0, concat_axis=0, tiled=True)  36.6 us
    all_to_all x1, waiting for transfers between devices, shards(): lax.all_to_all(outgoing, 'blk', split_axis=0, concat_axis=0, tiled=True)  34.5 us
  transfers between devices with their start and end apart: 7, of which 7 were waited for; matrix products, arithmetic and copies ran while one was open for 7% of the time, Pallas kernels for 0%

commit v1 on v0

v1 whole, which is shorter than its diff:
```python
import jax
import jax.numpy as jnp
import numpy as np
from jax import lax
from jax.experimental import pallas as pl
from jax.experimental.pallas import tpu as pltpu
from jax.sharding import Mesh
from jax.sharding import PartitionSpec as P

HEADS = 16
KV_HEADS = 8
HEAD = 64
FF_EXP = 512
TOP = 8
MOST = 24
EPS = 1e-06
ROPE_BASE = 10000.0
SCALE = HEAD ** (-0.5)

ROWS = ("zl", "core")
BLK = ("x", "y", "zh")
CHIPS = ("zl", "x", "y", "zh")
AXES = ("zl", "core", "x", "y", "zh")
SWAP = [(0, 1), (1, 0)]
EXPERT_GROUPS = [
    [(parity ^ zh) * 32 + xy * 2 + zh for xy in range(16) for zh in range(2)] for parity in range(2)
]
Z_PAIRS = [(i, 3 - i) for i in range(4)]
F32 = jnp.float32
BF16 = jnp.bfloat16
NT = (((1,), (1,)), ((), ()))
TN = (((0,), (0,)), ((), ()))


def dot(left, right, dims=(((1,), (0,)), ((), ()))):
    return lax.dot_general(left, right, dims, preferred_element_type=F32)


def call(
    kernel,
    grid,
    in_specs,
    out_specs,
    out_shape,
    scratch=(),
    mb=24,
    flops=0,
    moved=0,
    deps=(),
    scalars=0,
    aliases=None,
):
    count = len(in_specs) + scalars

    def body(*refs):
        kernel(*refs[:count], *refs[count + len(deps) :])

    built = pl.pallas_call(
        body,
        grid_spec=pltpu.PrefetchScalarGridSpec(
            num_scalar_prefetch=scalars,
            grid=grid,
            in_specs=[*in_specs, *[pl.BlockSpec(memory_space=pl.ANY)] * len(deps)],
            out_specs=out_specs,
            scratch_shapes=list(scratch),
        ),
        out_shape=out_shape,
        input_output_aliases=aliases or {},
        compiler_params=pltpu.CompilerParams(vmem_limit_bytes=mb * 1024 * 1024),
        cost_estimate=pl.CostEstimate(flops=flops, bytes_accessed=moved, transcendentals=0),
    )
    return lambda *operands: built(*operands, *deps)


def after(x, *deps):
    any_space = pl.BlockSpec(memory_space=pl.ANY)
    return pl.pallas_call(
        lambda *refs: None,
        in_specs=[any_space] * (1 + len(deps)),
        out_specs=any_space,
        out_shape=sds(x.shape, x.dtype),
        input_output_aliases={0: 0},
    )(x, *deps)


def whole(*shape):
    return pl.BlockSpec(shape, lambda *_: (0,) * len(shape))


def sds(shape, dtype):
    return pltpu.HBM(shape, dtype)


def low_half(shape):
    return lax.broadcasted_iota(jnp.int32, shape, len(shape) - 1) < HEAD


def swap_halves(u):
    lane = lax.broadcasted_iota(jnp.int32, u.shape, 1)
    return jnp.where(lane % HEAD < HEAD // 2, pltpu.roll(u, 96, 1), pltpu.roll(u, 32, 1))


def pre_kernel(tok, gain, wq, wk, wv, cos, sin, h_ref, send):
    @pl.when(pl.program_id(0) == 0)
    def _():
        x = tok[...].astype(F32)
        inverse = lax.rsqrt(jnp.mean(x * x, axis=-1, keepdims=True) + EPS)
        h_ref[...] = (x * inverse * gain[...]).astype(BF16)

    h = h_ref[...]
    c = jnp.concatenate([cos[...], cos[...]], 0)
    s = jnp.concatenate([sin[...], sin[...]], 0)

    def rope(u):
        return u * c + swap_halves(u) * s

    q = dot(h, wq[...])
    k = rope(dot(h, wk[...]))
    v = dot(h, wv[...])
    low = low_half(k.shape)
    pairs = (
        jnp.where(low, k, pltpu.roll(v, HEAD, 1)).astype(BF16),
        jnp.where(low, pltpu.roll(k, HEAD, 1), v).astype(BF16),
    )
    for j in range(2):
        qj = (rope(q[:, j * 128 : (j + 1) * 128]).astype(BF16).astype(F32) * SCALE).astype(BF16)
        for t in range(2):
            for half in range(2):
                first = t * 64 + half * 32
                send[t, j, half, 0:32, :] = qj[first : first + 32]
                send[t, j, half, 32:96, :] = pairs[j][t * 64 : t * 64 + 64]


def pre(tok, gain, w_qkv, cos, sin):
    return call(
        pre_kernel,
        (4,),
        [
            whole(128, 1024),
            whole(1, 1024),
            pl.BlockSpec((1024, 256), lambda m: (0, m)),
            pl.BlockSpec((1024, 128), lambda m: (0, 8 + m)),
            pl.BlockSpec((1024, 128), lambda m: (0, 12 + m)),
            whole(64, 128),
            whole(64, 128),
        ],
        [whole(128, 1024), pl.BlockSpec((2, 2, 2, 96, 128), lambda m: (0, m, 0, 0, 0))],
        [sds((128, 1024), BF16), sds((2, 8, 2, 96, 128), BF16)],
        flops=2 * 128 * 1024 * 2048,
        moved=5 << 20,
    )(tok, gain, w_qkv, w_qkv, w_qkv, cos, sin)


def plan_kernel(routes, gates, dz, pos_ref, gate_ref, out):
    named = routes[...].astype(F32).T
    weights = gates[...].T
    experts = lax.broadcasted_iota(jnp.int32, (32, 128), 0).astype(F32)
    chosen = jnp.zeros((32, 128), F32)
    gate = jnp.zeros((32, 128), F32)
    for k in range(TOP):
        match = named[k : k + 1] == experts
        chosen = jnp.where(match, 1.0, chosen)
        gate = jnp.where(match, weights[k : k + 1], gate)
    row = lax.broadcasted_iota(jnp.int32, (128, 128), 0)
    before = jnp.where(row < lax.broadcasted_iota(jnp.int32, (128, 128), 1), 1.0, 0.0)
    rank = dot(chosen.astype(BF16), before.astype(BF16))
    pos = jnp.where(chosen > 0.0, rank, -1.0)
    pos_ref[...] = pos.astype(jnp.int32)
    gate_ref[...] = gate
    high = gate.astype(BF16).astype(F32)
    rest = gate - high
    out[0:128, :] = dz[...]
    for j in range(8):
        part = slice(4 * j, 4 * j + 4)
        tile = jnp.concatenate([pos[part], high[part], rest[part], jnp.zeros((4, 128), F32)], 0)
        out[128:144, j * 128 : (j + 1) * 128] = tile.astype(BF16)


def plan(routes, gates, dz, deps):
    return call(
        plan_kernel,
        (1,),
        [whole(128, 8), whole(128, 8), whole(128, 1024)],
        [whole(32, 128), whole(32, 128), whole(144, 1024)],
        [sds((32, 128), jnp.int32), sds((32, 128), F32), sds((144, 1024), BF16)],
        moved=1 << 20,
        deps=deps,
    )(routes, gates, dz)


def split_queries(q):
    qf = q.astype(F32)
    low = low_half(qf.shape)
    first = jnp.where(low, qf, 0.0)
    second = jnp.where(low, pltpu.roll(qf, HEAD, 1), 0.0)
    return jnp.concatenate([first, second], 0).astype(BF16)


def limits(tile, info):
    place = lax.broadcasted_iota(jnp.int32, (1, 512), 1) % 256
    position = (tile * 8 + place // 32) * 64 + info[1] * 32 + place % 32
    return jnp.minimum(position, info[0] - 1)


def load_pairs(x_ref, kv, kvt):
    kv[...] = x_ref[:, 32:96, :].reshape(2048, 128)
    for c in range(8):
        rows = slice(c * 256, (c + 1) * 256)
        kvt[:, rows] = kv[rows, :].astype(F32).T.astype(BF16)


def attend_kernel(info, x_ref, o_ref, ot_ref, lse_ref, kv, kvt):
    load_pairs(x_ref, kv, kvt)
    for tile in range(4):
        q2 = split_queries(x_ref[tile * 8 : (tile + 1) * 8, 0:32, :].reshape(256, 128))
        limit = limits(tile, info)

        def step(c, carry):
            top, total, acc = carry
            at = pl.ds(pl.multiple_of(c * 512, 512), 512)
            s = dot(kv[at, :], q2, NT)
            place = c * 512 + lax.broadcasted_iota(jnp.int32, (512, 1), 0)
            s = jnp.where(place <= limit, s, -1e30)
            new_top = jnp.maximum(top, jnp.max(s, axis=0, keepdims=True))
            shrink = jnp.exp(top - new_top)
            p = jnp.exp(s - new_top)
            total = total * shrink + jnp.sum(p, axis=0, keepdims=True)
            return new_top, total, acc * shrink + dot(kvt[64:128, at], p.astype(BF16))

        start = (jnp.full((1, 512), -1e30, F32), jnp.zeros((1, 512), F32), jnp.zeros((64, 512), F32))
        top, total, acc = lax.fori_loop(0, tile + 1, step, start)
        out = acc / total
        ot_ref[tile] = out
        lse_ref[tile] = jnp.broadcast_to(top + jnp.log(total), (8, 512))
        both = jnp.concatenate([out[:, :256], out[:, 256:]], 0).T
        o_ref[tile * 8 : (tile + 1) * 8] = both.astype(BF16).reshape(8, 32, 128)


def attend(info, arrived, deps):
    return call(
        attend_kernel,
        (1,),
        [pl.BlockSpec(memory_space=pltpu.SMEM), whole(32, 96, 128)],
        [whole(32, 32, 128), whole(4, 64, 512), whole(4, 8, 512)],
        [sds((32, 32, 128), BF16), sds((4, 64, 512), F32), sds((4, 8, 512), F32)],
        [pltpu.VMEM((2048, 128), BF16), pltpu.VMEM((128, 2048), BF16)],
        flops=4 * 2048 * 1280 * 128,
        moved=2 << 20,
        deps=deps,
    )(info, arrived)


def attend_back_kernel(info, x_ref, do_ref, ot_ref, lse_ref, out_ref, gain_ref, kv, kvt, total):
    load_pairs(x_ref, kv, kvt)
    total[...] = jnp.zeros_like(total)
    for tile in range(4):
        q2 = split_queries(x_ref[tile * 8 : (tile + 1) * 8, 0:32, :].reshape(256, 128))
        grad = do_ref[tile * 8 : (tile + 1) * 8, 0:32, :].reshape(256, 128).astype(F32)
        low = low_half(grad.shape)
        do2 = jnp.concatenate(
            [jnp.where(low, 0.0, pltpu.roll(grad, HEAD, 1)), jnp.where(low, 0.0, grad)], 0
        ).astype(BF16)
        grad_t = grad.T
        grad_t = jnp.concatenate([grad_t[:64], grad_t[64:]], 1)
        inner = jnp.sum(grad_t * ot_ref[tile], axis=0, keepdims=True)
        lse = lse_ref[tile][0:1]
        limit = limits(tile, info)

        def step(c, acc):
            at = pl.ds(pl.multiple_of(c * 256, 256), 256)
            part = kv[at, :]
            s = dot(part, q2, NT)
            place = c * 256 + lax.broadcasted_iota(jnp.int32, (256, 1), 0)
            p = jnp.exp(jnp.where(place <= limit, s, -1e30) - lse)
            ds = (p * (dot(part, do2, NT) - inner)).astype(BF16)
            total[at, :] += dot(ds, q2) + dot(p.astype(BF16), do2)
            return acc + dot(kvt[0:64, at], ds)

        acc = lax.fori_loop(0, 2 * tile + 2, step, jnp.zeros((64, 512), F32))
        dq = jnp.concatenate([acc[:, :256], acc[:, 256:]], 0).T
        out_ref[tile * 8 : (tile + 1) * 8, 0:32, :] = dq.astype(BF16).reshape(8, 32, 128)
    out_ref[:, 32:96, :] = total[...].astype(BF16).reshape(32, 64, 128)
    gains = jnp.sum(do_ref[:, 32:48, :].astype(F32), axis=0)
    gain_ref[...] = gains[:8] + gains[8:]


def attend_back(info, arrived, grad, ot, lse, deps):
    return call(
        attend_back_kernel,
        (1,),
        [
            pl.BlockSpec(memory_space=pltpu.SMEM),
            whole(32, 96, 128),
            whole(32, 48, 128),
            whole(4, 64, 512),
            whole(4, 8, 512),
        ],
        [whole(32, 96, 128), whole(8, 128)],
        [sds((32, 96, 128), BF16), sds((8, 128), F32)],
        [pltpu.VMEM((2048, 128), BF16), pltpu.VMEM((128, 2048), BF16), pltpu.VMEM((2048, 128), F32)],
        flops=10 * 2048 * 1280 * 128,
        moved=3 << 20,
        deps=deps,
    )(info, arrived, grad, ot, lse)


def placement(pos):
    slots = lax.broadcasted_iota(jnp.int32, (8, 48, 128), 1)
    return (pos[...][:, None, :] == slots).reshape(384, 128)


def gated(pos, gate):
    placed = placement(pos)
    weight = jnp.broadcast_to(gate[...][:, None, :], (8, 48, 128)).reshape(384, 128)
    weight = jnp.where(placed, weight, 0.0)
    high = weight.astype(BF16)
    return high, (weight - high.astype(F32)).astype(BF16)


PLACE = pl.BlockSpec((8, 128), lambda e: (e, 0))
SLOTS = pl.BlockSpec((8, 48, 1024), lambda e: (e, 0, 0))


def mid_kernel(recv, w_out, tok, gain, pos, o_ref, y_ref, out, h2):
    @pl.when(pl.program_id(0) == 0)
    def _():
        for s in range(2):
            for half in range(2):
                first = s * 64 + half * 32
                for m in range(8):
                    o_ref[first : first + 32, m * 128 : (m + 1) * 128] = recv[s, m, half]
        y = tok[...].astype(F32) + dot(o_ref[...], w_out[...])
        y_ref[...] = y
        inverse = lax.rsqrt(jnp.mean(y * y, axis=-1, keepdims=True) + EPS)
        h2[...] = (y * inverse * gain[...]).astype(BF16)

    placed = placement(pos).astype(F32).astype(BF16)
    out[...] = dot(placed, h2[...]).astype(BF16).reshape(8, 48, 1024)


def mid(recv, w_out, tok, gain, pos):
    return call(
        mid_kernel,
        (4,),
        [
            whole(2, 8, 2, 32, 128),
            whole(1024, 1024),
            whole(128, 1024),
            whole(1, 1024),
            PLACE,
        ],
        [whole(128, 1024), whole(128, 1024), SLOTS],
        [sds((128, 1024), BF16), sds((128, 1024), F32), sds((32, 48, 1024), BF16)],
        [pltpu.VMEM((128, 1024), BF16)],
        flops=2 * 128 * 1024 * 1024 + 2 * 1536 * 128 * 1024,
        moved=6 << 20,
    )(recv, w_out, tok, gain, pos)


def expert_kernel(x_ref, wgu, wdn, eo, slopes, hid_ref):
    activations = dot(x_ref[...], wgu[...])
    gate, up = activations[:, :FF_EXP], activations[:, FF_EXP:]
    sig = jax.nn.sigmoid(gate)
    act = gate * sig
    hid = (act * up).astype(BF16)
    hid_ref[...] = hid
    slopes[:, :FF_EXP] = (up * sig * (1.0 + gate * (1.0 - sig))).astype(BF16)
    slopes[:, FF_EXP:] = act.astype(BF16)
    eo[...] = dot(hid, wdn[...]).astype(BF16)


ROWS384 = pl.BlockSpec((384, 1024), lambda i: (i, 0))
HIDDEN = pl.BlockSpec((384, 512), lambda i: (i, 0))


def expert(x, wgu, wdn, deps):
    return call(
        expert_kernel,
        (4,),
        [ROWS384, whole(1024, 1024), whole(512, 1024)],
        [ROWS384, ROWS384, HIDDEN],
        [sds((1536, 1024), BF16), sds((1536, 1024), BF16), sds((1536, 512), BF16)],
        flops=2 * 1536 * 1024 * 1536,
        moved=14 << 20,
        deps=deps,
    )(x, wgu, wdn)


def expert_back_kernel(which, info, dz, slopes, wgu, wdn, dx2, da_ref, deo_ref):
    slots = lax.broadcasted_iota(jnp.int32, (48, 128), 0).astype(F32)
    rows16 = lax.broadcasted_iota(jnp.int32, (16, 128), 0)
    blank = jnp.zeros((48, 128), F32)
    mine = which[0] % 4
    for pair in range(4):
        parts, weights = [], []
        for j in range(2):
            tile = info[pair, j].astype(F32)

            def pick(k):
                return jnp.sum(jnp.where(rows16 == mine + 4 * k, tile, 0.0), axis=0, keepdims=True)

            hot = jnp.where(slots == pick(0), 1.0, 0.0)
            weights.append(jnp.sum(hot * (pick(1) + pick(2)), axis=1, keepdims=True))
            parts.append(jnp.concatenate([hot, blank] if j == 0 else [blank, hot], 1))
        rows = dot(jnp.concatenate(parts, 0).astype(BF16), dz[pair].reshape(256, 1024))
        rows = (rows * jnp.concatenate(weights, 0)).astype(BF16)
        for j in range(2):
            first = pl.multiple_of(pair * 96 + (which[1] ^ j) * 48, 48)
            deo_ref[pl.ds(first, 48), :] = rows[j * 48 : (j + 1) * 48]
    dhid = dot(deo_ref[...], wdn[...], NT)
    da_ref[:, :FF_EXP] = (dhid * slopes[:, :FF_EXP].astype(F32)).astype(BF16)
    da_ref[:, FF_EXP:] = (dhid * slopes[:, FF_EXP:].astype(F32)).astype(BF16)
    dx2[...] = dot(da_ref[...], wgu[...], NT).astype(BF16)


def expert_back(which, dz_all, slopes, wgu, wdn):
    dz_all = pltpu.with_memory_space_constraint(dz_all, pltpu.HBM)
    rows = pl.BlockSpec((384, 1024), lambda i, which: (i, 0))
    return call(
        expert_back_kernel,
        (4,),
        [
            pl.BlockSpec((4, 2, 16, 128), lambda i, which: (i, 0, 8, which[0] // 4)),
            pl.BlockSpec((4, 2, 128, 1024), lambda i, which: (i, 0, 0, 0)),
            rows,
            whole(1024, 1024),
            whole(512, 1024),
        ],
        [rows, rows, rows],
        [sds((1536, 1024), BF16)] * 3,
        flops=2 * 1536 * 1024 * 1792,
        moved=24 << 20,
        scalars=1,
    )(which, dz_all, dz_all, slopes, wgu, wdn)


def expert_grad_kernel(core, x_ref, da, hid, deo, own, other):
    step = pl.program_id(0)

    for first, out in ((0, own), (3, other)):

        @pl.when((step >= first) & (step < first + 2))
        def _():
            out[...] = dot(x_ref[...], da[...], TN).astype(BF16)

        @pl.when(step == first + 2)
        def _():
            out[...] = dot(hid[...], deo[...], TN).astype(BF16)


def expert_grad(core, x, da, hid, deo):
    def half(i, core):
        return jnp.where(i < 3, core[0], 1 - core[0])

    return call(
        expert_grad_kernel,
        (6,),
        [
            pl.BlockSpec((1536, 256), lambda i, c: (0, half(i, c) * 2 + jnp.minimum(i % 3, 1))),
            whole(1536, 1024),
            pl.BlockSpec((1536, 256), lambda i, c: (0, half(i, c))),
            whole(1536, 1024),
        ],
        [
            pl.BlockSpec((256, 1024), lambda i, c: (jnp.minimum(i, 2), 0)),
            pl.BlockSpec((256, 1024), lambda i, c: (jnp.maximum(i - 3, 0), 0)),
        ],
        [sds((768, 1024), BF16)] * 2,
        flops=2 * 1536 * 1024 * 1536,
        moved=16 << 20,
        scalars=1,
    )(core, x, da, hid, deo)


def final_expert_kernel(core, own, other, gate_up, down):
    step = pl.program_id(0)
    half = jnp.where(step < 4, step // 2, step - 4)

    def write(out):
        @pl.when(half == core[0])
        def _():
            out[...] = own[...].astype(F32)

        @pl.when(half != core[0])
        def _():
            out[...] = other[...].astype(F32)

    @pl.when(step < 4)
    def _():
        write(gate_up)

    @pl.when(step >= 4)
    def _():
        write(down)


def final_expert(core, own, other):
    part = pl.BlockSpec((256, 1024), lambda i: (jnp.where(i < 4, i % 2, 2), 0))
    return call(
        final_expert_kernel,
        (6,),
        [pl.BlockSpec(memory_space=pltpu.SMEM), part, part],
        [
            pl.BlockSpec((256, 1024), lambda i: (jnp.minimum(i, 3), 0)),
            pl.BlockSpec((256, 1024), lambda i: (jnp.maximum(i - 4, 0), 0)),
        ],
        [sds((1024, 1024), F32), sds((512, 1024), F32)],
        moved=9 << 20,
    )(core, own, other)


def norm_back(incoming, gain, vectors):
    inverse = lax.rsqrt(jnp.mean(vectors * vectors, axis=-1, keepdims=True) + EPS)
    scaled = vectors * inverse
    weighted = incoming * gain
    mean = jnp.mean(weighted * scaled, axis=-1, keepdims=True)
    return inverse * (weighted - scaled * mean), scaled


def mid_back_kernel(core, back, pos, y, gain, dz, w_out, dy_ref, own, other, send, acc):
    @pl.when(pl.program_id(0) == 0)
    def _():
        acc[...] = jnp.zeros_like(acc)

    placed = placement(pos).astype(F32).astype(BF16)
    acc[...] += dot(placed, back[...].reshape(384, 1024), TN)

    @pl.when(pl.program_id(0) == 3)
    def _():
        dh2 = acc[...]
        dv, scaled = norm_back(dh2, gain[...], y[...])
        gains = jnp.sum(dh2 * scaled, axis=0, keepdims=True)
        row = lax.broadcasted_iota(jnp.int32, (8, 128), 0)
        tile = jnp.zeros((8, 128), F32)
        for r in range(8):
            tile = jnp.where(row == r, gains[:, r * 128 : (r + 1) * 128], tile)
        high = tile.astype(BF16).astype(F32)
        extra = jnp.concatenate([high, tile - high], 0).astype(BF16)
        dy = dz[...].astype(F32) + dv
        dy_ref[...] = dy
        dbr = dy.astype(BF16)

        @pl.when(core[0] == 0)
        def _():
            own[...] = dbr[:, :512]
            other[...] = dbr[:, 512:]

        @pl.when(core[0] == 1)
        def _():
            own[...] = dbr[:, 512:]
            other[...] = dbr[:, :512]

        do = dot(dbr, w_out[...], NT).astype(BF16)
        for s in range(2):
            for half in range(2):
                first = s * 64 + half * 32
                for m in range(8):
                    send[s, m, half, 0:32, :] = do[first : first + 32, m * 128 : (m + 1) * 128]
                    send[s, m, half, 32:48, :] = extra


def mid_back(core, back, pos, y, gain, dz, w_out, deps):
    return call(
        mid_back_kernel,
        (4,),
        [
            pl.BlockSpec(memory_space=pltpu.SMEM),
            SLOTS,
            PLACE,
            whole(128, 1024),
            whole(1, 1024),
            whole(128, 1024),
            whole(1024, 1024),
        ],
        [whole(128, 1024), whole(128, 512), whole(128, 512), whole(2, 8, 2, 48, 128)],
        [
            sds((128, 1024), F32),
            sds((128, 512), BF16),
            sds((128, 512), BF16),
            sds((2, 8, 2, 48, 128), BF16),
        ],
        [pltpu.VMEM((128, 1024), F32)],
        flops=2 * 128 * 1024 * 1024 + 2 * 1536 * 128 * 1024,
        moved=6 << 20,
        deps=deps,
    )(core, back, pos, y, gain, dz, w_out)


def combine_kernel(back, pos, gate, y, out, acc):
    @pl.when(pl.program_id(0) == 0)
    def _():
        acc[...] = y[...]

    high, rest = gated(pos, gate)
    rows = back[...].reshape(384, 1024)
    acc[...] += dot(high, rows, TN) + dot(rest, rows, TN)

    @pl.when(pl.program_id(0) == 3)
    def _():
        out[...] = acc[...].astype(BF16)


def combine(back, pos, gate, y):
    return call(
        combine_kernel,
        (4,),
        [SLOTS, PLACE, PLACE, whole(128, 1024)],
        whole(128, 1024),
        sds((128, 1024), BF16),
        [pltpu.VMEM((128, 1024), F32)],
        flops=4 * 1536 * 128 * 1024,
        moved=4 << 20,
    )(back, pos, gate, y)


def unpack_kernel(core, recv, cos, sin, dproj, own, other):
    c, s = cos[...], sin[...]

    def rope_back(u):
        return u * c - swap_halves(u) * s

    for t in range(2):
        rows = slice(t * 64, t * 64 + 64)
        for mm in range(4):
            both = []
            for j in range(2):
                m = 2 * mm + j
                dq = jnp.concatenate([recv[t, m, 0, 0:32, :], recv[t, m, 1, 0:32, :]], 0)
                dproj[rows, m * 128 : (m + 1) * 128] = (rope_back(dq.astype(F32)) * SCALE).astype(
                    BF16
                )
                both.append(
                    recv[t, m, 0, 32:96, :].astype(F32) + recv[t, m, 1, 32:96, :].astype(F32)
                )
            low = low_half((64, 128))
            dk = jnp.where(low, both[0], pltpu.roll(both[1], HEAD, 1))
            dv = jnp.where(low, pltpu.roll(both[0], HEAD, 1), both[1])
            dproj[rows, 1024 + mm * 128 : 1152 + mm * 128] = rope_back(dk).astype(BF16)
            dproj[rows, 1536 + mm * 128 : 1664 + mm * 128] = dv.astype(BF16)

    @pl.when(core[0] == 0)
    def _():
        own[...] = dproj[:, :1024]
        other[...] = dproj[:, 1024:]

    @pl.when(core[0] == 1)
    def _():
        own[...] = dproj[:, 1024:]
        other[...] = dproj[:, :1024]


def unpack(core, recv, cos, sin, deps):
    return call(
        unpack_kernel,
        (1,),
        [
            pl.BlockSpec(memory_space=pltpu.SMEM),
            whole(2, 8, 2, 96, 128),
            whole(64, 128),
            whole(64, 128),
        ],
        [whole(128, 2048), whole(128, 1024), whole(128, 1024)],
        [sds((128, 2048), BF16), sds((128, 1024), BF16), sds((128, 1024), BF16)],
        moved=3 << 20,
        deps=deps,
    )(core, recv, cos, sin)


def last_kernel(dproj, w_qkv, tok, gain, dy, grad_tokens):
    dh = dot(dproj[...], w_qkv[...], NT)
    dv, _ = norm_back(dh, gain[...], tok[...].astype(F32))
    grad_tokens[...] = dy[...] + dv


def last(dproj, w_qkv, tok, gain, dy, deps):
    return call(
        last_kernel,
        (1,),
        [
            whole(128, 2048),
            whole(1024, 2048),
            whole(128, 1024),
            whole(1, 1024),
            whole(128, 1024),
        ],
        whole(128, 1024),
        sds((128, 1024), F32),
        flops=2 * 128 * 1024 * 2048,
        moved=6 << 20,
        deps=deps,
    )(dproj, w_qkv, tok, gain, dy)


def weight_grad_kernel(left, left2, right, right2, out):
    a = jnp.concatenate([left[...], left2[...]], 0)
    b = jnp.concatenate([right[...], right2[...]], 0)
    out[...] = dot(a, b, TN).astype(BF16)


def weight_grad(left, left2, right, right2, deps=()):
    width = right.shape[1]
    thin = pl.BlockSpec((128, 256), lambda i: (0, i))
    return call(
        weight_grad_kernel,
        (4,),
        [thin, thin, whole(128, width), whole(128, width)],
        pl.BlockSpec((256, width), lambda i: (i, 0)),
        sds((1024, width), BF16),
        flops=2 * 256 * 1024 * width,
        moved=3 << 20,
        deps=deps,
    )(left, left2, right, right2)


def add_pieces_kernel(pieces, out):
    total = jnp.sum(pieces[...].astype(F32), axis=0).astype(BF16)
    out[...] = jnp.broadcast_to(total[None], out.shape)


def add_pieces(pieces, deps=()):
    block = pl.BlockSpec((64, 16, 256), lambda i: (0, 0, i))
    return call(
        add_pieces_kernel,
        (pieces.shape[2] // 256,),
        [block],
        block,
        sds(pieces.shape, BF16),
        moved=4 << 20,
        deps=deps,
    )(pieces)


def final_out_kernel(core, own, other, out):
    @pl.when(core[0] == 0)
    def _():
        out[:, :512] = own[...].astype(F32)
        out[:, 512:] = other[...].astype(F32)

    @pl.when(core[0] == 1)
    def _():
        out[:, :512] = other[...].astype(F32)
        out[:, 512:] = own[...].astype(F32)


def final_out(core, own, other):
    half = pl.BlockSpec((256, 512), lambda i: (i, 0))
    return call(
        final_out_kernel,
        (4,),
        [pl.BlockSpec(memory_space=pltpu.SMEM), half, half],
        pl.BlockSpec((256, 1024), lambda i: (i, 0)),
        sds((1024, 1024), F32),
        moved=6 << 20,
    )(core, own, other)


def row_sums(product):
    total = jnp.sum(product, axis=-1, keepdims=True)
    total = jnp.broadcast_to(total, (256, 128))
    return jnp.concatenate([total[:128].T[0:1], total[128:].T[0:1]], 0)


def final_own_kernel(core, own, w_qkv, out, gain_ref):
    value = own[...].astype(F32)
    out[...] = value
    at = pl.ds(pl.program_id(0) * 2, 2)
    gain_ref[at, :] = row_sums(value * w_qkv[...].astype(F32))


def final_own(core, own, w_qkv):
    half = pl.BlockSpec((256, 1024), lambda i, core: (i, core[0]))
    return call(
        final_own_kernel,
        (4,),
        [pl.BlockSpec((256, 1024), lambda i, core: (i, 0)), half],
        [half, whole(8, 128)],
        [sds((1024, 2048), F32), sds((8, 128), F32)],
        moved=8 << 20,
        scalars=1,
    )(core, own, w_qkv)


def final_other_kernel(core, other, w_qkv, part, gain, _, out, gain_ref):
    value = other[...].astype(F32)
    out[...] = value
    at = pl.ds(pl.program_id(0) * 2, 2)
    gain_ref[at, :] = (part[at, :] + row_sums(value * w_qkv[...].astype(F32))) / gain[at, :]


def final_other(core, other, w_qkv, part, gain, out):
    half = pl.BlockSpec((256, 1024), lambda i, core: (i, 1 - core[0]))
    return call(
        final_other_kernel,
        (4,),
        [
            pl.BlockSpec((256, 1024), lambda i, core: (i, 0)),
            half,
            whole(8, 128),
            whole(8, 128),
            pl.BlockSpec(memory_space=pl.ANY),
        ],
        [half, whole(8, 128)],
        [sds((1024, 2048), F32), sds((8, 128), F32)],
        moved=8 << 20,
        scalars=1,
        aliases={5: 0},
    )(core, other, w_qkv, part, gain, out)


def exchange(x):
    return lax.all_to_all(x, BLK, 0, 0, tiled=True)


def add_rounded(a, b):
    return (a.astype(F32) + b.astype(F32)).astype(BF16)


def among_experts(x):
    return lax.all_to_all(x, CHIPS, 0, 0, tiled=True, axis_index_groups=EXPERT_GROUPS)


def among_chips(x):
    return lax.all_to_all(x, CHIPS, 0, 0, tiled=True)


def shards(
    tokens, lengths, routes, gates, gain_attn, w_qkv, w_out, gain_moe, w_gate_up, w_down, cotangent
):
    core = lax.axis_index("core")
    blk = lax.axis_index(BLK)
    tok = tokens.reshape(128, 1024)
    dz = cotangent.reshape(128, 1024)
    wgu = w_gate_up.reshape(1024, 1024)
    wdn = w_down.reshape(512, 1024)
    gain_a = gain_attn.reshape(1, 1024)
    gain_m = gain_moe.reshape(1, 1024)

    lane = np.arange(128)
    frequency = ROPE_BASE ** (-jnp.arange(32, dtype=F32) / 32)
    angles = (blk * 64 + jnp.arange(64, dtype=jnp.int32)).astype(F32)[:, None] * frequency[None, :]
    cos = jnp.tile(jnp.cos(angles), (1, 4))
    sin = jnp.tile(jnp.sin(angles), (1, 4)) * np.where(lane % 64 < 32, -1.0, 1.0).astype(np.float32)

    which = core.astype(jnp.int32).reshape(1)
    info = jnp.stack([jnp.where(blk < 16, lengths[0], lengths[1]), blk % 2]).astype(jnp.int32)

    def to_partner(part):
        return lax.ppermute(part, "core", SWAP)

    h, send = pre(tok, gain_a, w_qkv, cos, sin)
    arrived = exchange(send.reshape(32, 96, 128))
    h_other = to_partner(h)
    pos, gate, planned = plan(routes.reshape(128, 8), gates.reshape(128, 8), dz, [send])
    planned = jnp.stack([planned, lax.ppermute(planned, ("zl", "zh"), Z_PAIRS)])
    dz_all = lax.all_gather(planned, ("x", "y"))
    o_part, ot, lse = attend(info, arrived, [h_other, planned])
    o_recv = exchange(o_part).reshape(2, 8, 2, 32, 128)
    o, y, rows = mid(o_recv, w_out, tok, gain_m, pos)
    o_other = to_partner(o)
    x = among_experts(rows).reshape(1536, 1024)
    eo, slopes, hid = expert(x, wgu, wdn, [o_other])
    eo_back = among_experts(eo.reshape(32, 48, 1024))
    place = jnp.stack([blk, lax.axis_index("zh")]).astype(jnp.int32)
    dx2, da, deo = expert_back(place, dz_all, slopes, wgu, wdn)
    dx2_back = among_experts(after(dx2.reshape(32, 48, 1024), eo_back))
    experts_own, experts_send = expert_grad(which, x, da, hid, deo)
    experts_own = add_rounded(experts_own, to_partner(experts_send))
    mixed = combine(eo_back, pos, gate, y)
    dy, dbr_own, dbr_send, do = mid_back(
        which, dx2_back, pos, y, gain_m, dz, w_out, [experts_own, mixed]
    )
    experts_own = add_rounded(experts_own, lax.ppermute(experts_own, "zl", SWAP))

    do_recv = exchange(do.reshape(32, 48, 128))
    out_partial = weight_grad(o, o_other, dbr_own, to_partner(dbr_send), [experts_own])
    out_pieces = among_chips(out_partial.reshape(64, 16, 512))
    dqkv, gains = attend_back(info, arrived, do_recv, ot, lse, [out_partial])
    dqkv_recv = exchange(after(dqkv, out_pieces)).reshape(2, 8, 2, 96, 128)

    for axis in ROWS:
        gains = gains + lax.ppermute(gains, axis, SWAP)

    out_copies = add_pieces(out_pieces)
    dproj, dproj_own, dproj_send = unpack(which, dqkv_recv, cos, sin, [gains, out_copies])
    out_own = among_chips(out_copies).reshape(1024, 512)
    grad_out = final_out(which, out_own, to_partner(out_own))
    grad_gate_up, grad_down = final_expert(which, experts_own, to_partner(experts_own))

    partial = weight_grad(h, h_other, dproj_own, to_partner(dproj_send))
    grad_tokens = last(dproj, w_qkv, tok, gain_a, dy, [partial])
    pieces = among_chips(after(partial.reshape(64, 16, 1024), out_own))
    own = among_chips(add_pieces(pieces, [grad_out, grad_gate_up, grad_tokens])).reshape(1024, 1024)
    own_part, gain_part = final_own(which, own, w_qkv)
    grad_qkv, grad_gain_attn = final_other(
        which, to_partner(own), w_qkv, gain_part, gain_attn.reshape(8, 128), own_part
    )
    return (
        mixed.reshape(2, 64, 1024),
        grad_tokens.reshape(2, 64, 1024),
        grad_gain_attn.reshape(1024),
        grad_qkv,
        grad_out,
        gains.reshape(1024),
        grad_gate_up[None],
        grad_down[None],
    )


def solution(mesh):
    split = Mesh(mesh.devices.reshape(2, 2, 4, 4, 2), AXES)
    rows = P(ROWS, BLK, None)
    return jax.shard_map(
        shards,
        mesh=split,
        in_specs=(
            rows,
            P(ROWS),
            rows,
            rows,
            P(),
            P(),
            P(),
            P(),
            P(BLK, None, None),
            P(BLK, None, None),
            rows,
        ),
        out_specs=(
            rows,
            rows,
            P(),
            P(),
            P(),
            P(),
            P(BLK, None, None),
            P(BLK, None, None),
        ),
        check_vma=False,
    )
```

time: 897 us -> 454 us (0.51)
  waiting for transfers between devices: 542 us -> 133 us
  starting transfers between devices: 19.4 us -> 115 us
  matrix products: 93.2 us -> 0 us
  Pallas kernels: 0 us -> 91.6 us
  blocking collectives: 104 us -> 47.7 us
  local copies, waits for them, and re-layouts: 80.4 us -> 41.3 us
  other arithmetic: 32.4 us -> 7.61 us
    psum x2 -> x0, waiting for transfers between devices: 171 us -> none  [the longest x1 100 us: shards(): lax.psum((grad_gain_attn, grad_qkv, grad_out, grad_gain_moe), ('rows', 'b...]
    reduce_scatter x1 -> x0, waiting for transfers between devices: 164 us -> none  [shards(): lax.psum_scatter(grad_pairs.astype(jnp.bfloat16), 'blk', scatter_dimensio...]
    all_gather x1, waiting for transfers between devices: 102 us -> 0.01 us  [shards(): dz_all = lax.all_gather(planned, ('x', 'y'))]
    dot_general x30 -> x0, matrix products: 93.2 us -> none  [the longest x1 8.41 us: shards(): jnp.einsum('nesmd,efd->nesmf', grad_produced, w_down, preferred_element_t...]
    pallas_call x0 -> x23, Pallas kernels: none -> 91.6 us  [the longest x20 91.6 us: call(): return lambda *operands: built(*operands, *deps)]
    psum x1 -> x0, blocking collectives: 67 us -> none  [shards(): lax.psum((grad_gain_attn, grad_qkv, grad_out, grad_gain_moe), ('rows', 'b...]
    all_to_all x3 -> x9, starting transfers between devices: 19.3 us -> 76.9 us  [the longest x3 31.8 us: among_chips(): return lax.all_to_all(x, CHIPS, 0, 0, tiled=True)]
    ppermute x0 -> x12, starting transfers between devices: none -> 37.7 us  [the longest x8 27.7 us: to_partner(): return lax.ppermute(part, 'core', SWAP)]
  transfers between devices with their start and end apart: 7 -> 22, of which waited for: 7 -> 15; matrix products, arithmetic and copies ran while one was open for 7% -> 2% of each run, Pallas kernels for 0% -> 18%
where the time goes in v1:
time: 454 us; the launch traced here: 452 us
  waiting for transfers between devices  133 us (29%)
  starting transfers between devices  115 us (25%)
  Pallas kernels  91.6 us (20%)
  blocking collectives  47.7 us (11%)
  local copies, waits for them, and re-layouts  41.3 us (9%)
  between operations  15.9 us (4%)
  other arithmetic  7.61 us (2%)
    pallas_call x20, Pallas kernels, call(): return lambda *operands: built(*operands, *deps)  91.6 us
    all_to_all x3, waiting for transfers between devices, among_experts(): lax.all_to_all(x, CHIPS, 0, 0, tiled=True, axis_index_groups=EXPERT_GROUPS)  77.5 us
    unnamed x117, local copies, waits for them, and re-layouts  40.6 us
    all_to_all x1, blocking collectives, among_chips(): return lax.all_to_all(x, CHIPS, 0, 0, tiled=True)  32.6 us
    all_to_all x3, starting transfers between devices, among_chips(): return lax.all_to_all(x, CHIPS, 0, 0, tiled=True)  31.8 us
    ppermute x8, starting transfers between devices, to_partner(): return lax.ppermute(part, 'core', SWAP)  27.7 us
    all_to_all x3, waiting for transfers between devices, exchange(): return lax.all_to_all(x, BLK, 0, 0, tiled=True)  25.1 us
    all_to_all x3, starting transfers between devices, exchange(): return lax.all_to_all(x, BLK, 0, 0, tiled=True)  23.5 us
  transfers between devices with their start and end apart: 22, of which 15 were waited for; matrix products, arithmetic and copies ran while one was open for 2% of the time, Pallas kernels for 18%

profile of v1, /device:TPU:1, one launch (start us, length us, event | category | flops | bytes accessed | tf_op | source)
XLA Modules:
  0.0 451.9 jit_solution(749495989029001414)
XLA Ops:
  9.9 2.2 copy-done
  13.7 3.7 shard_map.179
  18.4 4.6 %collective-permute-start.1 = (bf16[144,1024]{1,0:T(8,128)(2,1)}, bf16[144,1024]{1,0:T(8,128)(2,1)S(1)}, u32[]{:S(2)}, u32[]{:S(2)}) collective-permute-start(bf16[144,1024]{1,0:T(8,128)(2,1)} %get-tuple-element.44), channel_id=1, source_target_pairs={{0,65},{1,64},{64,1},{65,0},{2,67},{3,66},{66,3},{67,2},{4,69},{5,... | collective-permute-start | bytes 884744 | tf_op jit(solution)/shard_map/ppermute | solution.py:854
  22.9 6.9 %collective-permute-done.1 = bf16[144,1024]{1,0:T(8,128)(2,1)S(1)} collective-permute-done((bf16[144,1024]{1,0:T(8,128)(2,1)}, bf16[144,1024]{1,0:T(8,128)(2,1)S(1)}, u32[]{:S(2)}, u32[]{:S(2)}) %collective-permute-start.1) | collective-permute-done | bytes 294944 | tf_op jit(solution)/shard_map/ppermute | solution.py:854
  31.7 8.0 %all-to-all-start = ((bf16[32,96,128]{2,1,0:T(8,128)(2,1)}), bf16[32,96,128]{2,1,0:T(8,128)(2,1)}, u32[]{:S(2)}, u32[]{:S(2)}) async-start(bf16[32,96,128]{2,1,0:T(8,128)(2,1)} %bitcast.8), calls=%async_computation | async-start | bytes 1572864 | tf_op jit(solution)/shard_map/all_to_all | solution.py:811
  43.7 10.3 %all-to-all-done.refs_1_ = bf16[32,96,128]{2,1,0:T(8,128)(2,1)} async-done(((bf16[32,96,128]{2,1,0:T(8,128)(2,1)}), bf16[32,96,128]{2,1,0:T(8,128)(2,1)}, u32[]{:S(2)}, u32[]{:S(2)}) %all-to-all-start) | async-done | bytes 786464 | tf_op jit(solution)/shard_map/all_to_all | solution.py:811
  54.0 9.0 %shard_map.181 = (bf16[32,32,128]{2,1,0:T(8,128)(2,1)}, f32[4,64,512]{2,1,0:T(8,128)}, f32[4,8,512]{2,1,0:T(8,128)}) custom-call(s32[2]{0:T(128)S(1)} %pad_add_fusion.refs_0_, bf16[32,96,128]{2,1,0:T(8,128)(2,1)} %all-to-all-done.refs_1_, bf16[128,1024]{1,0:T(8,128)(2,1)} %collective-permute-done.refs_2_.refs_1_, bf16[2,144,1024]{2,1,0:T(8,128)(2,1)S(1)} %copy-done.22), custom_call_target="tpu_custom_call" | custom-call | flops 1342177280 | bytes 2097152 | tf_op jit(solution)/shard_map/pallas_call | solution.py:72
  62.9 15.1 %all_to_all.55 = bf16[32,32,128]{2,1,0:T(8,128)(2,1)S(1)} all-to-all(bf16[32,32,128]{2,1,0:T(8,128)(2,1)} %get-tuple-element.45), channel_id=1, replica_groups=mesh['zl'=2,'core'=2,'x'=4,'y'=4,'zh'=2] {'x','y','zh'}, dimensions={0} | all-to-all | bytes 524288 | tf_op jit(solution)/shard_map/all_to_all | solution.py:811
  78.0 3.6 shard_map.182
  81.6 6.2 %all-to-all-start.2 = ((bf16[32,48,1024]{2,1,0:T(8,128)(2,1)}), bf16[32,48,1024]{2,1,0:T(8,128)(2,1)S(1)}, u32[]{:S(2)}, u32[]{:S(2)}) async-start(bf16[32,48,1024]{2,1,0:T(8,128)(2,1)} %get-tuple-element.47), calls=%async_computation.2 | async-start | bytes 6291456 | tf_op jit(solution)/shard_map/all_to_all | solution.py:819
  87.8 11.2 %collective-permute-start.2 = (bf16[128,1024]{1,0:T(8,128)(2,1)}, bf16[128,1024]{1,0:T(8,128)(2,1)S(1)}, u32[]{:S(2)}, u32[]{:S(2)}) collective-permute-start(bf16[128,1024]{1,0:T(8,128)(2,1)} %get-tuple-element.48.refs_0_), channel_id=1, source_target_pairs={{0,32},{32,0},{1,33},{33,1},{2,34},{34,2},{3,35},{35,3},{4,36},{36... | collective-permute-start | bytes 786440 | tf_op jit(solution)/shard_map/ppermute | solution.py:848
  101.0 44.2 %all-to-all-done.2 = bf16[32,48,1024]{2,1,0:T(8,128)(2,1)S(1)} async-done(((bf16[32,48,1024]{2,1,0:T(8,128)(2,1)}), bf16[32,48,1024]{2,1,0:T(8,128)(2,1)S(1)}, u32[]{:S(2)}, u32[]{:S(2)}) %all-to-all-start.2) | async-done | bytes 3145760 | tf_op jit(solution)/shard_map/all_to_all | solution.py:819
  145.2 2.7 copy-done.25
  150.1 7.1 %shard_map.183 = (bf16[1536,1024]{1,0:T(8,128)(2,1)}, bf16[1536,1024]{1,0:T(8,128)(2,1)}, bf16[1536,512]{1,0:T(8,128)(2,1)}) custom-call(bf16[1536,1024]{1,0:T(8,128)(2,1)S(1)} %bitcast.46, bf16[1024,1024]{1,0:T(8,128)(2,1)S(1)} %bitcast.53, bf16[512,1024]{1,0:T(8,128)(2,1)S(1)} %bitcast.55, bf16[128,1024]{1,0:T(8,128)(2,1)S(1)} %copy-done.40), custom_call_target="tpu_custom_call" | custom-call | flops 4831838208 | bytes 14680064 | tf_op jit(solution)/shard_map/pallas_call | solution.py:72
  157.3 7.1 %all-to-all-start.3 = ((bf16[32,48,1024]{2,1,0:T(8,128)(2,1)}), bf16[32,48,1024]{2,1,0:T(8,128)(2,1)S(1)}, u32[]{:S(2)}, u32[]{:S(2)}) async-start(bf16[32,48,1024]{2,1,0:T(8,128)(2,1)} %bitcast.72), calls=%async_computation.3 | async-start | bytes 6291456 | tf_op jit(solution)/shard_map/all_to_all | solution.py:819
  169.2 11.3 %shard_map.185 = (bf16[1536,1024]{1,0:T(8,128)(2,1)}, bf16[1536,1024]{1,0:T(8,128)(2,1)}, bf16[1536,1024]{1,0:T(8,128)(2,1)}) custom-call(s32[2]{0:T(128)S(1)} %pad_add_fusion.1.refs_0_, bf16[16,2,144,1024]{3,2,1,0:T(8,128)(2,1)} %bitcast.69, bf16[16,2,144,1024]{3,2,1,0:T(8,128)(2,1)} %bitcast.70, bf16[1536,1024]{1,0:T(8,128)(2,1)S(1)} %copy-done.18, ...), custom_call_target="tpu_custom_call" | custom-call | flops 5637144576 | bytes 25165824 | tf_op jit(solution)/shard_map/pallas_call | solution.py:72
  184.3 7.9 %shard_map.187 = (bf16[768,1024]{1,0:T(8,128)(2,1)}, bf16[768,1024]{1,0:T(8,128)(2,1)}) custom-call(s32[1]{0:T(128)} %bitcast.21.refs_0_, bf16[1536,1024]{1,0:T(8,128)(2,1)S(1)} %bitcast.47, bf16[1536,1024]{1,0:T(8,128)(2,1)S(1)} %copy-done.50, bf16[1536,512]{1,0:T(8,128)(2,1)S(1)} %copy-done.53, bf16[1536,1024]{1,0:T(8,128)(2,1)S(1)} %copy-done.51), custom_call_target="tpu_custom_call" | custom-call | flops 4831838208 | bytes 16777216 | tf_op jit(solution)/shard_map/pallas_call | solution.py:72
  192.2 4.9 %collective-permute-start.3 = (bf16[768,1024]{1,0:T(8,128)(2,1)}, bf16[768,1024]{1,0:T(8,128)(2,1)}, u32[]{:S(2)}, u32[]{:S(2)}) collective-permute-start(bf16[768,1024]{1,0:T(8,128)(2,1)} %get-tuple-element.58), channel_id=1, source_target_pairs={{0,32},{32,0},{1,33},{33,1},{2,34},{34,2},{3,35},{35,3},{4,36},{36... | collective-permute-start | bytes 4718600 | tf_op jit(solution)/shard_map/ppermute | solution.py:848
  197.0 3.0 all-to-all-done.3.refs_0_.refs_1_
  201.8 8.3 %all-to-all-start.4 = ((bf16[32,48,1024]{2,1,0:T(8,128)(2,1)}), bf16[32,48,1024]{2,1,0:T(8,128)(2,1)}, u32[]{:S(2)}, u32[]{:S(2)}) async-start(bf16[32,48,1024]{2,1,0:T(8,128)(2,1)} %shard_map.186), calls=%async_computation.4 | async-start | bytes 6291456 | tf_op jit(solution)/shard_map/all_to_all | solution.py:819
  210.1 2.7 add_convert_fusion.1.refs_7_
  213.0 2.7 shard_map.184.refs_8_
  215.7 30.3 %all-to-all-done.4.refs_1_ = bf16[32,48,1024]{2,1,0:T(8,128)(2,1)} async-done(((bf16[32,48,1024]{2,1,0:T(8,128)(2,1)}), bf16[32,48,1024]{2,1,0:T(8,128)(2,1)}, u32[]{:S(2)}, u32[]{:S(2)}) %all-to-all-start.4) | async-done | bytes 3145760 | tf_op jit(solution)/shard_map/all_to_all | solution.py:819
  248.5 5.6 %shard_map.188 = (f32[128,1024]{1,0:T(8,128)}, bf16[128,512]{1,0:T(8,128)(2,1)}, bf16[128,512]{1,0:T(8,128)(2,1)}, bf16[2,8,2,48,128]{4,3,2,1,0:T(8,128)(2,1)}) custom-call(s32[1]{0:T(128)} %bitcast.21.refs_0_, bf16[32,48,1024]{2,1,0:T(8,128)(2,1)} %all-to-all-done.4.refs_1_, s32[32,128]{1,0:T(8,128)S(1)} %copy-done.42, f32[128,1024]{1,0:T(8,128)S(1)} %copy-done.23, ...), custom_call_target="tpu_custom_call" | custom-call | flops 671088640 | bytes 6291456 | tf_op jit(solution)/shard_map/pallas_call | solution.py:72
  254.1 7.9 %all-to-all-start.5 = ((bf16[32,48,128]{2,1,0:T(8,128)(2,1)}), bf16[32,48,128]{2,1,0:T(8,128)(2,1)S(1)}, u32[]{:S(2)}, u32[]{:S(2)}) async-start(bf16[32,48,128]{2,1,0:T(8,128)(2,1)} %bitcast.73), calls=%async_computation.5 | async-start | bytes 786432 | tf_op jit(solution)/shard_map/all_to_all | solution.py:811
  262.1 4.3 collective-permute-start.4
  268.5 2.3 shard_map.189.refs_5_
  272.4 9.6 %all-to-all-start.6 = ((bf16[64,16,512]{2,1,0:T(8,128)(2,1)}), bf16[64,16,512]{2,1,0:T(8,128)(2,1)S(1)}, u32[]{:S(2)}, u32[]{:S(2)}) async-start(bf16[64,16,512]{2,1,0:T(8,128)(2,1)} %bitcast.45), calls=%async_computation.6 | async-start | bytes 2097152 | tf_op jit(solution)/shard_map/all_to_all | solution.py:823
  284.1 12.6 %shard_map.190 = (bf16[32,96,128]{2,1,0:T(8,128)(2,1)}, f32[8,128]{1,0:T(8,128)}) custom-call(s32[2]{0:T(128)S(1)} %pad_add_fusion.refs_0_, bf16[32,96,128]{2,1,0:T(8,128)(2,1)} %all-to-all-done.refs_1_, bf16[32,48,128]{2,1,0:T(8,128)(2,1)S(1)} %all-to-all-done.5.refs_2_, f32[4,64,512]{2,1,0:T(8,128)S(1)} %copy-done.52, f32[4,8,512]{2,1,0:T(8,128)S(1)} %copy-done.54, ...), custom_call_target="tpu_custom_call" | custom-call | flops 3355443200 | bytes 3145728 | tf_op jit(solution)/shard_map/pallas_call | solution.py:72
  299.1 7.6 %all-to-all-start.7 = ((bf16[32,96,128]{2,1,0:T(8,128)(2,1)}), bf16[32,96,128]{2,1,0:T(8,128)(2,1)S(1)}, u32[]{:S(2)}, u32[]{:S(2)}) async-start(bf16[32,96,128]{2,1,0:T(8,128)(2,1)} %shard_map.191), calls=%async_computation.7 | async-start | bytes 1572864 | tf_op jit(solution)/shard_map/all_to_all | solution.py:811
  307.9 13.2 %all-to-all-done.7 = bf16[32,96,128]{2,1,0:T(8,128)(2,1)S(1)} async-done(((bf16[32,96,128]{2,1,0:T(8,128)(2,1)}), bf16[32,96,128]{2,1,0:T(8,128)(2,1)S(1)}, u32[]{:S(2)}, u32[]{:S(2)}) %all-to-all-start.7) | async-done | bytes 786464 | tf_op jit(solution)/shard_map/all_to_all | solution.py:811
  321.1 4.8 %all-to-all-start.8 = ((bf16[64,16,512]{2,1,0:T(8,128)(2,1)}), bf16[64,16,512]{2,1,0:T(8,128)(2,1)S(1)}, u32[]{:S(2)}, u32[]{:S(2)}) async-start(bf16[64,16,512]{2,1,0:T(8,128)(2,1)} %shard_map.192.refs_5_), calls=%async_computation.8 | async-start | bytes 2097152 | tf_op jit(solution)/shard_map/all_to_all | solution.py:823
  328.4 4.2 collective-permute-start.7
  339.1 4.0 shard_map.194.refs_5_
  343.1 3.2 copy.38.refs_0_
  347.3 17.5 %all-to-all-start.9 = ((bf16[64,16,1024]{2,1,0:T(8,128)(2,1)}), bf16[64,16,1024]{2,1,0:T(8,128)(2,1)}, u32[]{:S(2)}, u32[]{:S(2)}) async-start(bf16[64,16,1024]{2,1,0:T(8,128)(2,1)} %shard_map.196), calls=%async_computation.9 | async-start | bytes 4194304 | tf_op jit(solution)/shard_map/all_to_all | solution.py:823
  365.7 2.9 collective-permute-done.10.refs_2_
  368.6 3.8 shard_map.198
  374.6 2.4 shard_map.195.refs_3_
  377.1 2.4 shard_map.197.refs_1_
  379.5 13.3 %all-to-all-done.9.refs_0_ = bf16[64,16,1024]{2,1,0:T(8,128)(2,1)} async-done(((bf16[64,16,1024]{2,1,0:T(8,128)(2,1)}), bf16[64,16,1024]{2,1,0:T(8,128)(2,1)}, u32[]{:S(2)}, u32[]{:S(2)}) %all-to-all-start.9) | async-done | bytes 2097184 | tf_op jit(solution)/shard_map/all_to_all | solution.py:823
  392.8 2.2 copy-done.6
  395.0 2.2 copy-done.14
  397.2 3.9 shard_map.199
  401.1 32.6 %all_to_all.56 = bf16[64,16,1024]{2,1,0:T(8,128)(2,1)S(1)} all-to-all(bf16[64,16,1024]{2,1,0:T(8,128)(2,1)} %shard_map.199), channel_id=1, replica_groups=mesh['zl'=2,'core'=2,'x'=4,'y'=4,'zh'=2] {'zl','x','y','zh'}, dimensions={0} | all-to-all | bytes 4194304 | tf_op jit(solution)/shard_map/all_to_all | solution.py:823
  433.7 4.3 collective-permute-start.11
  438.0 2.7 shard_map.200
  442.4 2.7 shard_map.201
  (155 shorter events, 51.0 us)
Async XLA Ops:
  7.2 157.3 %all-gather.3.cloned.1.call-start = ((), (), s32[]{:S(2)}) async-start(), calls=%async_computation.11 | async-start | bytes 10027008 | tf_op jit(solution)/shard_map/all_gather | solution.py:855
  7.6 9.9 %copy-start.33 = (f32[64,128]{1,0:T(8,128)}, f32[64,128]{1,0:T(8,128)S(1)}, u32[]{:S(2)}) copy-start(f32[64,128]{1,0:T(8,128)S(1)} %copy.32.refs_5_.refs_2_) | copy-start | bytes 98308
  9.9 7.6 %copy-start.35 = (f32[64,128]{1,0:T(8,128)}, f32[64,128]{1,0:T(8,128)S(1)}, u32[]{:S(2)}) copy-start(f32[64,128]{1,0:T(8,128)S(1)} %broadcast_multiply_fusion.refs_6_.refs_3_) | copy-start | bytes 98308
  17.4 24.2 %copy-start.56 = (s32[2]{0:T(128)S(1)}, s32[2]{0:T(128)}, u32[]{:S(2)}) copy-start(s32[2]{0:T(128)} %param.13) | copy-start | bytes 28
  18.4 11.5 %collective-permute-start.1 = (bf16[144,1024]{1,0:T(8,128)(2,1)}, bf16[144,1024]{1,0:T(8,128)(2,1)S(1)}, u32[]{:S(2)}, u32[]{:S(2)}) collective-permute-start(bf16[144,1024]{1,0:T(8,128)(2,1)} %get-tuple-element.44), channel_id=1, source_target_pairs={{0,65},{1,64},{64,1},{65,0},{2,67},{3,66},{66,3},{67,2},{4,69},{5,... | collective-permute-start | bytes 884744 | tf_op jit(solution)/shard_map/ppermute | solution.py:854
  31.7 22.3 %copy-start.22 = (bf16[2,144,1024]{2,1,0:T(8,128)(2,1)S(1)}, bf16[2,144,1024]{2,1,0:T(8,128)(2,1)}, u32[]{:S(2)}) copy-start(bf16[2,144,1024]{2,1,0:T(8,128)(2,1)} %pad_maximum_fusion.refs_3_) | copy-start | bytes 1769476
  31.7 22.2 %all-to-all-start = ((bf16[32,96,128]{2,1,0:T(8,128)(2,1)}), bf16[32,96,128]{2,1,0:T(8,128)(2,1)}, u32[]{:S(2)}, u32[]{:S(2)}) async-start(bf16[32,96,128]{2,1,0:T(8,128)(2,1)} %bitcast.8), calls=%async_computation | async-start | bytes 1572864 | tf_op jit(solution)/shard_map/all_to_all | solution.py:811
  39.8 3.9 collective-permute-start
  43.6 34.4 %copy-start.12 = (bf16[1024,1024]{1,0:T(8,128)(2,1)S(1)}, bf16[1024,1024]{1,0:T(8,128)(2,1)}, u32[]{:S(2)}) copy-start(bf16[1024,1024]{1,0:T(8,128)(2,1)} %refs_6_.1) | copy-start | bytes 6291460
  43.6 34.4 %copy-start.20 = (bf16[2,64,1024]{2,1,0:T(8,128)(2,1)S(1)}, bf16[2,64,1024]{2,1,0:T(8,128)(2,1)}, u32[]{:S(2)}) copy-start(bf16[2,64,1024]{2,1,0:T(8,128)(2,1)} %param.12) | copy-start | bytes 786436
  43.6 34.4 %copy-start.42 = (s32[32,128]{1,0:T(8,128)S(1)}, s32[32,128]{1,0:T(8,128)}, u32[]{:S(2)}) copy-start(s32[32,128]{1,0:T(8,128)} %get-tuple-element.46.refs_4_.refs_1_.refs_2_) | copy-start | bytes 49156
  43.6 34.4 %copy-start.46 = (f32[1024]{0:T(1024)S(1)}, f32[1024]{0:T(1024)}, u32[]{:S(2)}) copy-start(f32[1024]{0:T(1024)} %param.19) | copy-start | bytes 12292
  81.6 63.6 %all-to-all-start.2 = ((bf16[32,48,1024]{2,1,0:T(8,128)(2,1)}), bf16[32,48,1024]{2,1,0:T(8,128)(2,1)S(1)}, u32[]{:S(2)}, u32[]{:S(2)}) async-start(bf16[32,48,1024]{2,1,0:T(8,128)(2,1)} %get-tuple-element.47), calls=%async_computation.2 | async-start | bytes 6291456 | tf_op jit(solution)/shard_map/all_to_all | solution.py:819
  87.8 12.5 %collective-permute-start.2 = (bf16[128,1024]{1,0:T(8,128)(2,1)}, bf16[128,1024]{1,0:T(8,128)(2,1)S(1)}, u32[]{:S(2)}, u32[]{:S(2)}) collective-permute-start(bf16[128,1024]{1,0:T(8,128)(2,1)} %get-tuple-element.48.refs_0_), channel_id=1, source_target_pairs={{0,32},{32,0},{1,33},{33,1},{2,34},{34,2},{3,35},{35,3},{4,36},{36... | collective-permute-start | bytes 786440 | tf_op jit(solution)/shard_map/ppermute | solution.py:848
  145.2 12.0 %copy-start.16 = (bf16[32,48,1024]{2,1,0:T(8,128)(2,1)}, bf16[32,48,1024]{2,1,0:T(8,128)(2,1)S(1)}, u32[]{:S(2)}) copy-start(bf16[32,48,1024]{2,1,0:T(8,128)(2,1)S(1)} %all-to-all-done.2) | copy-start | bytes 9437188
  157.3 42.8 %all-to-all-start.3 = ((bf16[32,48,1024]{2,1,0:T(8,128)(2,1)}), bf16[32,48,1024]{2,1,0:T(8,128)(2,1)S(1)}, u32[]{:S(2)}, u32[]{:S(2)}) async-start(bf16[32,48,1024]{2,1,0:T(8,128)(2,1)} %bitcast.72), calls=%async_computation.3 | async-start | bytes 6291456 | tf_op jit(solution)/shard_map/all_to_all | solution.py:819
  169.2 11.3 %copy-start.17 = (bf16[32,48,1024]{2,1,0:T(8,128)(2,1)S(1)}, bf16[32,48,1024]{2,1,0:T(8,128)(2,1)}, u32[]{:S(2)}) copy-start(bf16[32,48,1024]{2,1,0:T(8,128)(2,1)} %copy-done.16) | copy-start | bytes 9437188
  169.2 11.3 %copy-start.53 = (bf16[1536,512]{1,0:T(8,128)(2,1)S(1)}, bf16[1536,512]{1,0:T(8,128)(2,1)}, u32[]{:S(2)}) copy-start(bf16[1536,512]{1,0:T(8,128)(2,1)} %get-tuple-element.55.refs_3_) | copy-start | bytes 4718596
  192.2 17.9 %collective-permute-start.3 = (bf16[768,1024]{1,0:T(8,128)(2,1)}, bf16[768,1024]{1,0:T(8,128)(2,1)}, u32[]{:S(2)}, u32[]{:S(2)}) collective-permute-start(bf16[768,1024]{1,0:T(8,128)(2,1)} %get-tuple-element.58), channel_id=1, source_target_pairs={{0,32},{32,0},{1,33},{33,1},{2,34},{34,2},{3,35},{35,3},{4,36},{36... | collective-permute-start | bytes 4718600 | tf_op jit(solution)/shard_map/ppermute | solution.py:848
  201.8 44.2 %all-to-all-start.4 = ((bf16[32,48,1024]{2,1,0:T(8,128)(2,1)}), bf16[32,48,1024]{2,1,0:T(8,128)(2,1)}, u32[]{:S(2)}, u32[]{:S(2)}) async-start(bf16[32,48,1024]{2,1,0:T(8,128)(2,1)} %shard_map.186), calls=%async_computation.4 | async-start | bytes 6291456 | tf_op jit(solution)/shard_map/all_to_all | solution.py:819
  212.8 53.6 %collective-permute-start.5 = (bf16[768,1024]{1,0:T(8,128)(2,1)S(1)}, bf16[768,1024]{1,0:T(8,128)(2,1)}, u32[]{:S(2)}, u32[]{:S(2)}) collective-permute-start(bf16[768,1024]{1,0:T(8,128)(2,1)S(1)} %add_convert_fusion.1.refs_7_), channel_id=1, source_target_pairs={{0,64},{64,0},{1,65},{65,1},{2,66},{66,2},{3,67},{67,3},{4,68},{68... | collective-permute-start | bytes 4718600 | tf_op jit(solution)/shard_map/ppermute | solution.py:872
  254.1 18.3 %all-to-all-start.5 = ((bf16[32,48,128]{2,1,0:T(8,128)(2,1)}), bf16[32,48,128]{2,1,0:T(8,128)(2,1)S(1)}, u32[]{:S(2)}, u32[]{:S(2)}) async-start(bf16[32,48,128]{2,1,0:T(8,128)(2,1)} %bitcast.73), calls=%async_computation.5 | async-start | bytes 786432 | tf_op jit(solution)/shard_map/all_to_all | solution.py:811
  262.0 6.5 %copy-start.38 = (bf16[128,1024]{1,0:T(8,128)(2,1)S(1)}, bf16[128,1024]{1,0:T(8,128)(2,1)}, u32[]{:S(2)}) copy-start(bf16[128,1024]{1,0:T(8,128)(2,1)} %get-tuple-element.48.refs_0_) | copy-start | bytes 786436
  262.1 6.4 %collective-permute-start.4 = (bf16[128,512]{1,0:T(8,128)(2,1)}, bf16[128,512]{1,0:T(8,128)(2,1)S(1)}, u32[]{:S(2)}, u32[]{:S(2)}) collective-permute-start(bf16[128,512]{1,0:T(8,128)(2,1)} %get-tuple-element.63), channel_id=1, source_target_pairs={{0,32},{32,0},{1,33},{33,1},{2,34},{34,2},{3,35},{35,3},{4,36},{36... | collective-permute-start | bytes 393224 | tf_op jit(solution)/shard_map/ppermute | solution.py:848
  268.5 13.5 %copy-start.52 = (f32[4,64,512]{2,1,0:T(8,128)S(1)}, f32[4,64,512]{2,1,0:T(8,128)}, u32[]{:S(2)}) copy-start(f32[4,64,512]{2,1,0:T(8,128)} %get-tuple-element.60.refs_3_) | copy-start | bytes 1572868
  272.4 25.7 %all-to-all-start.6 = ((bf16[64,16,512]{2,1,0:T(8,128)(2,1)}), bf16[64,16,512]{2,1,0:T(8,128)(2,1)S(1)}, u32[]{:S(2)}, u32[]{:S(2)}) async-start(bf16[64,16,512]{2,1,0:T(8,128)(2,1)} %bitcast.45), calls=%async_computation.6 | async-start | bytes 2097152 | tf_op jit(solution)/shard_map/all_to_all | solution.py:823
  299.1 7.6 %copy-start.11 = (bf16[64,16,512]{2,1,0:T(8,128)(2,1)S(1)}, bf16[64,16,512]{2,1,0:T(8,128)(2,1)}, u32[]{:S(2)}) copy-start(bf16[64,16,512]{2,1,0:T(8,128)(2,1)} %copy-done.10) | copy-start | bytes 3145732
  299.1 22.0 %all-to-all-start.7 = ((bf16[32,96,128]{2,1,0:T(8,128)(2,1)}), bf16[32,96,128]{2,1,0:T(8,128)(2,1)S(1)}, u32[]{:S(2)}, u32[]{:S(2)}) async-start(bf16[32,96,128]{2,1,0:T(8,128)(2,1)} %shard_map.191), calls=%async_computation.7 | async-start | bytes 1572864 | tf_op jit(solution)/shard_map/all_to_all | solution.py:811
  306.7 19.1 %copy-start.55 = (f32[8,128]{1,0:T(8,128)S(1)}, f32[8,128]{1,0:T(8,128)}, u32[]{:S(2)}) copy-start(f32[8,128]{1,0:T(8,128)} %get-tuple-element.65) | copy-start | bytes 12292
  306.7 26.7 %copy-start.34 = (f32[64,128]{1,0:T(8,128)S(1)}, f32[64,128]{1,0:T(8,128)}, u32[]{:S(2)}) copy-start(f32[64,128]{1,0:T(8,128)} %copy-done.33) | copy-start | bytes 98308
  306.7 26.7 %copy-start.36 = (f32[64,128]{1,0:T(8,128)S(1)}, f32[64,128]{1,0:T(8,128)}, u32[]{:S(2)}) copy-start(f32[64,128]{1,0:T(8,128)} %copy-done.35) | copy-start | bytes 98308
  321.1 25.3 %all-to-all-start.8 = ((bf16[64,16,512]{2,1,0:T(8,128)(2,1)}), bf16[64,16,512]{2,1,0:T(8,128)(2,1)S(1)}, u32[]{:S(2)}, u32[]{:S(2)}) async-start(bf16[64,16,512]{2,1,0:T(8,128)(2,1)} %shard_map.192.refs_5_), calls=%async_computation.8 | async-start | bytes 2097152 | tf_op jit(solution)/shard_map/all_to_all | solution.py:823
  325.8 2.5 collective-permute-start.6
  328.4 5.0 %collective-permute-start.7 = (f32[8,128]{1,0:T(8,128)S(1)}, f32[8,128]{1,0:T(8,128)S(1)}, u32[]{:S(2)}, u32[]{:S(2)}) collective-permute-start(f32[8,128]{1,0:T(8,128)S(1)} %add.39), channel_id=1, source_target_pairs={{0,32},{32,0},{1,33},{33,1},{2,34},{34,2},{3,35},{35,3},{4,36},{36... | collective-permute-start | bytes 12296 | tf_op jit(solution)/shard_map/ppermute | solution.py:881
  333.4 9.7 %copy-start.48 = (f32[8,128]{1,0:T(8,128)}, f32[8,128]{1,0:T(8,128)S(1)}, u32[]{:S(2)}) copy-start(f32[8,128]{1,0:T(8,128)S(1)} %add.40.refs_4_) | copy-start | bytes 12292
  336.4 1.7 collective-permute-start.8
  347.3 18.3 %copy-start.8 = (bf16[64,16,512]{2,1,0:T(8,128)(2,1)S(1)}, bf16[64,16,512]{2,1,0:T(8,128)(2,1)}, u32[]{:S(2)}) copy-start(bf16[64,16,512]{2,1,0:T(8,128)(2,1)} %copy-done.7) | copy-start | bytes 3145732
  347.3 25.1 %copy-start.32 = (bf16[128,2048]{1,0:T(8,128)(2,1)S(1)}, bf16[128,2048]{1,0:T(8,128)(2,1)}, u32[]{:S(2)}) copy-start(bf16[128,2048]{1,0:T(8,128)(2,1)} %get-tuple-element.66.refs_0_) | copy-start | bytes 1572868
  347.3 45.5 %all-to-all-start.9 = ((bf16[64,16,1024]{2,1,0:T(8,128)(2,1)}), bf16[64,16,1024]{2,1,0:T(8,128)(2,1)}, u32[]{:S(2)}, u32[]{:S(2)}) async-start(bf16[64,16,1024]{2,1,0:T(8,128)(2,1)} %shard_map.196), calls=%async_computation.9 | async-start | bytes 4194304 | tf_op jit(solution)/shard_map/all_to_all | solution.py:823
  364.8 7.6 %copy-start.5 = (bf16[1024,1024]{1,0:T(8,128)(2,1)S(1)}, bf16[1024,1024]{1,0:T(8,128)(2,1)}, u32[]{:S(2)}) copy-start(bf16[1024,1024]{1,0:T(8,128)(2,1)} %shard_map.194.refs_5_) | copy-start | bytes 6291460
  364.8 7.6 %copy-start.21 = (bf16[2,64,1024]{2,1,0:T(8,128)(2,1)S(1)}, bf16[2,64,1024]{2,1,0:T(8,128)(2,1)}, u32[]{:S(2)}) copy-start(bf16[2,64,1024]{2,1,0:T(8,128)(2,1)} %param.12) | copy-start | bytes 786436
  364.8 7.6 %copy-start.31 = (f32[128,1024]{1,0:T(8,128)S(1)}, f32[128,1024]{1,0:T(8,128)}, u32[]{:S(2)}) copy-start(f32[128,1024]{1,0:T(8,128)} %get-tuple-element.67.refs_4_) | copy-start | bytes 1572868
  364.8 7.6 %copy-start.45 = (f32[1024]{0:T(1024)S(1)}, f32[1024]{0:T(1024)}, u32[]{:S(2)}) copy-start(f32[1024]{0:T(1024)} %param.16) | copy-start | bytes 12292
  364.8 3.7 collective-permute-start.10
  365.6 11.5 %collective-permute-start.9 = (bf16[1024,512]{1,0:T(8,128)(2,1)S(1)}, bf16[1024,512]{1,0:T(8,128)(2,1)S(1)}, u32[]{:S(2)}, u32[]{:S(2)}) collective-permute-start(bf16[1024,512]{1,0:T(8,128)(2,1)S(1)} %bitcast.40), channel_id=1, source_target_pairs={{0,32},{32,0},{1,33},{33,1},{2,34},{34,2},{3,35},{35,3},{4,36},{36... | collective-permute-start | bytes 3145736 | tf_op jit(solution)/shard_map/ppermute | solution.py:848
  377.1 15.7 %copy-start.24 = (f32[128,1024]{1,0:T(8,128)S(1)}, f32[128,1024]{1,0:T(8,128)}, u32[]{:S(2)}) copy-start(f32[128,1024]{1,0:T(8,128)} %shard_map.195.refs_3_) | copy-start | bytes 1572868
  401.1 36.9 %copy-start.2 = (bf16[1024,2048]{1,0:T(8,128)(2,1)S(1)}, bf16[1024,2048]{1,0:T(8,128)(2,1)}, u32[]{:S(2)}) copy-start(bf16[1024,2048]{1,0:T(8,128)(2,1)} %refs_2_.5) | copy-start | bytes 12582916
  433.7 8.1 %collective-permute-start.11 = (bf16[1024,1024]{1,0:T(8,128)(2,1)S(1)}, bf16[1024,1024]{1,0:T(8,128)(2,1)S(1)}, u32[]{:S(2)}, u32[]{:S(2)}) collective-permute-start(bf16[1024,1024]{1,0:T(8,128)(2,1)S(1)} %bitcast.42), channel_id=1, source_target_pairs={{0,32},{32,0},{1,33},{33,1},{2,34},{34,2},{3,35},{35,3},{4,36},{36... | collective-permute-start | bytes 6291464 | tf_op jit(solution)/shard_map/ppermute | solution.py:848
  (31 other events, 61.0 us)
Sparse Core Ops, SparseCore 0:
  31.9 114.5 all-gather.2

commit v2 on v1

--- a/solution.py
+++ b/solution.py
@@ -18,9 +18,11 @@
 SCALE = HEAD ** (-0.5)
 
 ROWS = ("zl", "core")
-BLK = ("x", "y", "zh")
-CHIPS = ("zl", "x", "y", "zh")
-AXES = ("zl", "core", "x", "y", "zh")
+PLANE = ("xh", "xl", "y")
+BLK = ("xh", "xl", "y", "zh")
+CHIPS = ("zl", "xh", "xl", "y", "zh")
+AXES = ("zl", "core", "xh", "xl", "y", "zh")
+SAME_COLUMNS = ("zl", "core", "xh", "zh")
 SWAP = [(0, 1), (1, 0)]
 EXPERT_GROUPS = [
     [(parity ^ zh) * 32 + xy * 2 + zh for xy in range(16) for zh in range(2)] for parity in range(2)
@@ -30,6 +32,15 @@
 BF16 = jnp.bfloat16
 NT = (((1,), (1,)), ((), ()))
 TN = (((0,), (0,)), ((), ()))
+
+
+def rope_tables():
+    lane = np.arange(128) % HEAD
+    frequency = (ROPE_BASE ** (-(lane % 32) / 32.0)).astype(np.float32)
+    angles = np.arange(2048, dtype=np.float32)[:, None] * frequency[None, :]
+    sign = np.where(lane < 32, -1.0, 1.0)
+    cosine = np.cos(angles.astype(np.float64)).astype(np.float32)
+    return cosine, (np.sin(angles.astype(np.float64)) * sign).astype(np.float32)
 
 
 def dot(left, right, dims=(((1,), (0,)), ((), ()))):
@@ -49,8 +60,13 @@
     deps=(),
     scalars=0,
     aliases=None,
+    moving=(),
 ):
     count = len(in_specs) + scalars
+
+    def place(i, x):
+        small = i < scalars or in_specs[i - scalars].memory_space == pltpu.SMEM
+        return x if small or i in moving else hold(x)
 
     def body(*refs):
         kernel(*refs[:count], *refs[count + len(deps) :])
@@ -69,7 +85,7 @@
         compiler_params=pltpu.CompilerParams(vmem_limit_bytes=mb * 1024 * 1024),
         cost_estimate=pl.CostEstimate(flops=flops, bytes_accessed=moved, transcendentals=0),
     )
-    return lambda *operands: built(*operands, *deps)
+    return lambda *operands: built(*[place(i, x) for i, x in enumerate(operands)], *deps)
 
 
 def after(x, *deps):
@@ -80,7 +96,16 @@
         out_specs=any_space,
         out_shape=sds(x.shape, x.dtype),
         input_output_aliases={0: 0},
-    )(x, *deps)
+        compiler_params=pltpu.CompilerParams(vmem_limit_bytes=1024 * 1024),
+    )(hold(x), *deps)
+
+
+def hold(x):
+    return pltpu.with_memory_space_constraint(x, pltpu.HBM)
+
+
+def corner(x):
+    return x[(0,) * (x.ndim - 2)][:8, :128]
 
 
 def whole(*shape):
@@ -100,7 +125,7 @@
     return jnp.where(lane % HEAD < HEAD // 2, pltpu.roll(u, 96, 1), pltpu.roll(u, 32, 1))
 
 
-def pre_kernel(tok, gain, wq, wk, wv, cos, sin, h_ref, send):
+def pre_kernel(blk, tok, gain, wq, wk, wv, cos, sin, h_ref, send):
     @pl.when(pl.program_id(0) == 0)
     def _():
         x = tok[...].astype(F32)
@@ -127,33 +152,36 @@
         for t in range(2):
             for half in range(2):
                 first = t * 64 + half * 32
-                send[t, j, half, 0:32, :] = qj[first : first + 32]
-                send[t, j, half, 32:96, :] = pairs[j][t * 64 : t * 64 + 64]
-
-
-def pre(tok, gain, w_qkv, cos, sin):
+                send[half, j, t, 0:32, :] = qj[first : first + 32]
+                send[half, j, t, 32:96, :] = pairs[j][t * 64 : t * 64 + 64]
+
+
+def pre(blk, tok, gain, w_qkv, cos, sin, deps):
+    places = pl.BlockSpec((64, 128), lambda m, blk: (blk[0], 0))
     return call(
         pre_kernel,
         (4,),
         [
             whole(128, 1024),
             whole(1, 1024),
-            pl.BlockSpec((1024, 256), lambda m: (0, m)),
-            pl.BlockSpec((1024, 128), lambda m: (0, 8 + m)),
-            pl.BlockSpec((1024, 128), lambda m: (0, 12 + m)),
-            whole(64, 128),
-            whole(64, 128),
-        ],
-        [whole(128, 1024), pl.BlockSpec((2, 2, 2, 96, 128), lambda m: (0, m, 0, 0, 0))],
+            pl.BlockSpec((1024, 256), lambda m, blk: (0, m)),
+            pl.BlockSpec((1024, 128), lambda m, blk: (0, 8 + m)),
+            pl.BlockSpec((1024, 128), lambda m, blk: (0, 12 + m)),
+            places,
+            places,
+        ],
+        [whole(128, 1024), pl.BlockSpec((2, 2, 2, 96, 128), lambda m, blk: (0, m, 0, 0, 0))],
         [sds((128, 1024), BF16), sds((2, 8, 2, 96, 128), BF16)],
         flops=2 * 128 * 1024 * 2048,
         moved=5 << 20,
-    )(tok, gain, w_qkv, w_qkv, w_qkv, cos, sin)
+        scalars=1,
+        deps=deps,
+    )(blk, tok, gain, w_qkv, w_qkv, w_qkv, cos, sin)
 
 
 def plan_kernel(routes, gates, dz, pos_ref, gate_ref, out):
-    named = routes[...].astype(F32).T
-    weights = gates[...].T
+    named = jnp.concatenate([routes[0], routes[1]], 1).astype(F32)
+    weights = jnp.concatenate([gates[0], gates[1]], 1)
     experts = lax.broadcasted_iota(jnp.int32, (32, 128), 0).astype(F32)
     chosen = jnp.zeros((32, 128), F32)
     gate = jnp.zeros((32, 128), F32)
@@ -176,15 +204,14 @@
         out[128:144, j * 128 : (j + 1) * 128] = tile.astype(BF16)
 
 
-def plan(routes, gates, dz, deps):
+def plan(routes, gates, dz):
     return call(
         plan_kernel,
         (1,),
-        [whole(128, 8), whole(128, 8), whole(128, 1024)],
+        [whole(2, 8, 64), whole(2, 8, 64), whole(128, 1024)],
         [whole(32, 128), whole(32, 128), whole(144, 1024)],
         [sds((32, 128), jnp.int32), sds((32, 128), F32), sds((144, 1024), BF16)],
         moved=1 << 20,
-        deps=deps,
     )(routes, gates, dz)
 
 
@@ -247,10 +274,13 @@
         flops=4 * 2048 * 1280 * 128,
         moved=2 << 20,
         deps=deps,
+        moving=(1,),
     )(info, arrived)
 
 
-def attend_back_kernel(info, x_ref, do_ref, ot_ref, lse_ref, out_ref, gain_ref, kv, kvt, total):
+def attend_back_kernel(
+    info, x_ref, do_ref, ot_ref, lse_ref, cos, sin, out_ref, gain_ref, kv, kvt, total
+):
     load_pairs(x_ref, kv, kvt)
     total[...] = jnp.zeros_like(total)
     for tile in range(4):
@@ -278,13 +308,23 @@
 
         acc = lax.fori_loop(0, 2 * tile + 2, step, jnp.zeros((64, 512), F32))
         dq = jnp.concatenate([acc[:, :256], acc[:, 256:]], 0).T
-        out_ref[tile * 8 : (tile + 1) * 8, 0:32, :] = dq.astype(BF16).reshape(8, 32, 128)
-    out_ref[:, 32:96, :] = total[...].astype(BF16).reshape(32, 64, 128)
+        at = (slice(tile * 8, tile * 8 + 8), pl.ds(pl.multiple_of(info[1] * 32, 32), 32))
+        c, s = cos[at].reshape(256, 128), sin[at].reshape(256, 128)
+        dq = ((dq * c - swap_halves(dq) * s) * SCALE).astype(BF16)
+        out_ref[tile * 8 : (tile + 1) * 8, 0:32, :] = dq.reshape(8, 32, 128)
+    for tile in range(4):
+        blocks = slice(tile * 8, tile * 8 + 8)
+        part = total[tile * 512 : (tile + 1) * 512, :]
+        turned = part * cos[blocks].reshape(512, 128) - swap_halves(part) * sin[
+            blocks
+        ].reshape(512, 128)
+        part = jnp.where(low_half(part.shape), turned, part)
+        out_ref[blocks, 32:96, :] = part.astype(BF16).reshape(8, 64, 128)
     gains = jnp.sum(do_ref[:, 32:48, :].astype(F32), axis=0)
     gain_ref[...] = gains[:8] + gains[8:]
 
 
-def attend_back(info, arrived, grad, ot, lse, deps):
+def attend_back(info, arrived, grad, ot, lse, cos, sin, deps):
     return call(
         attend_back_kernel,
         (1,),
@@ -294,6 +334,8 @@
             whole(32, 48, 128),
             whole(4, 64, 512),
             whole(4, 8, 512),
+            whole(32, 64, 128),
+            whole(32, 64, 128),
         ],
         [whole(32, 96, 128), whole(8, 128)],
         [sds((32, 96, 128), BF16), sds((8, 128), F32)],
@@ -301,7 +343,8 @@
         flops=10 * 2048 * 1280 * 128,
         moved=3 << 20,
         deps=deps,
-    )(info, arrived, grad, ot, lse)
+        moving=(1, 2,),
+    )(info, arrived, grad, ot, lse, cos.reshape(32, 64, 128), sin.reshape(32, 64, 128))
 
 
 def placement(pos):
@@ -321,15 +364,17 @@
 SLOTS = pl.BlockSpec((8, 48, 1024), lambda e: (e, 0, 0))
 
 
-def mid_kernel(recv, w_out, tok, gain, pos, o_ref, y_ref, out, h2):
+def mid_kernel(recv, w0, w1, w2, w3, tok, gain, pos, o_ref, y_ref, out, h2):
     @pl.when(pl.program_id(0) == 0)
     def _():
         for s in range(2):
             for half in range(2):
                 first = s * 64 + half * 32
                 for m in range(8):
-                    o_ref[first : first + 32, m * 128 : (m + 1) * 128] = recv[s, m, half]
-        y = tok[...].astype(F32) + dot(o_ref[...], w_out[...])
+                    o_ref[first : first + 32, m * 128 : (m + 1) * 128] = recv[half, m, s]
+        o = o_ref[...]
+        branch = jnp.concatenate([dot(o, w[...]) for w in (w0, w1, w2, w3)], 1)
+        y = tok[...].astype(F32) + branch
         y_ref[...] = y
         inverse = lax.rsqrt(jnp.mean(y * y, axis=-1, keepdims=True) + EPS)
         h2[...] = (y * inverse * gain[...]).astype(BF16)
@@ -338,13 +383,13 @@
     out[...] = dot(placed, h2[...]).astype(BF16).reshape(8, 48, 1024)
 
 
-def mid(recv, w_out, tok, gain, pos):
+def mid(recv, w_out, tok, gain, pos, deps):
     return call(
         mid_kernel,
         (4,),
         [
             whole(2, 8, 2, 32, 128),
-            whole(1024, 1024),
+            *[pl.BlockSpec((1024, 256), lambda e, j=j: (0, j)) for j in range(4)],
             whole(128, 1024),
             whole(1, 1024),
             PLACE,
@@ -354,39 +399,14 @@
         [pltpu.VMEM((128, 1024), BF16)],
         flops=2 * 128 * 1024 * 1024 + 2 * 1536 * 128 * 1024,
         moved=6 << 20,
-    )(recv, w_out, tok, gain, pos)
-
-
-def expert_kernel(x_ref, wgu, wdn, eo, slopes, hid_ref):
-    activations = dot(x_ref[...], wgu[...])
-    gate, up = activations[:, :FF_EXP], activations[:, FF_EXP:]
-    sig = jax.nn.sigmoid(gate)
-    act = gate * sig
-    hid = (act * up).astype(BF16)
-    hid_ref[...] = hid
-    slopes[:, :FF_EXP] = (up * sig * (1.0 + gate * (1.0 - sig))).astype(BF16)
-    slopes[:, FF_EXP:] = act.astype(BF16)
-    eo[...] = dot(hid, wdn[...]).astype(BF16)
-
-
-ROWS384 = pl.BlockSpec((384, 1024), lambda i: (i, 0))
-HIDDEN = pl.BlockSpec((384, 512), lambda i: (i, 0))
-
-
-def expert(x, wgu, wdn, deps):
-    return call(
-        expert_kernel,
-        (4,),
-        [ROWS384, whole(1024, 1024), whole(512, 1024)],
-        [ROWS384, ROWS384, HIDDEN],
-        [sds((1536, 1024), BF16), sds((1536, 1024), BF16), sds((1536, 512), BF16)],
-        flops=2 * 1536 * 1024 * 1536,
-        moved=14 << 20,
+        moving=(0,),
         deps=deps,
-    )(x, wgu, wdn)
-
-
-def expert_back_kernel(which, info, dz, slopes, wgu, wdn, dx2, da_ref, deo_ref):
+    )(recv, w_out, w_out, w_out, w_out, tok, gain, pos)
+
+
+def expert_kernel(
+    which, x_ref, info, dz, g0, g1, u0, u1, d0, d1, dx2, eo, da_ref, deo_ref, hid_ref
+):
     slots = lax.broadcasted_iota(jnp.int32, (48, 128), 0).astype(F32)
     rows16 = lax.broadcasted_iota(jnp.int32, (16, 128), 0)
     blank = jnp.zeros((48, 128), F32)
@@ -407,31 +427,61 @@
         for j in range(2):
             first = pl.multiple_of(pair * 96 + (which[1] ^ j) * 48, 48)
             deo_ref[pl.ds(first, 48), :] = rows[j * 48 : (j + 1) * 48]
-    dhid = dot(deo_ref[...], wdn[...], NT)
-    da_ref[:, :FF_EXP] = (dhid * slopes[:, :FF_EXP].astype(F32)).astype(BF16)
-    da_ref[:, FF_EXP:] = (dhid * slopes[:, FF_EXP:].astype(F32)).astype(BF16)
-    dx2[...] = dot(da_ref[...], wgu[...], NT).astype(BF16)
-
-
-def expert_back(which, dz_all, slopes, wgu, wdn):
-    dz_all = pltpu.with_memory_space_constraint(dz_all, pltpu.HBM)
+    x, deo = x_ref[...], deo_ref[...]
+    total = None
+    for part, (wg, wu) in enumerate(((g0, u0), (g1, u1))):
+        at = slice(part * 256, part * 256 + 256)
+        late = slice(part * 256 + FF_EXP, part * 256 + FF_EXP + 256)
+        gate, up = dot(x, wg[...]), dot(x, wu[...])
+        dhid = dot(deo[:, :512], d0[at, :], NT) + dot(deo[:, 512:], d1[at, :], NT)
+        sig = jax.nn.sigmoid(gate)
+        act = gate * sig
+        hid_ref[:, at] = (act * up).astype(BF16)
+        da_gate = (dhid * up * sig * (1.0 + gate * (1.0 - sig))).astype(BF16)
+        da_up = (dhid * act).astype(BF16)
+        da_ref[:, at] = da_gate
+        da_ref[:, late] = da_up
+        product = dot(da_gate, wg[...], NT) + dot(da_up, wu[...], NT)
+        total = product if total is None else total + product
+    dx2[...] = total.astype(BF16)
+    hid = hid_ref[...]
+    eo[:, 0:48, :512] = dot(hid, d0[...]).astype(BF16).reshape(8, 48, 512)
+    eo[:, 0:48, 512:] = dot(hid, d1[...]).astype(BF16).reshape(8, 48, 512)
+
+
+def expert(which, x, dz_all, wgu, wdn, deps):
     rows = pl.BlockSpec((384, 1024), lambda i, which: (i, 0))
     return call(
-        expert_back_kernel,
+        expert_kernel,
         (4,),
         [
+            rows,
             pl.BlockSpec((4, 2, 16, 128), lambda i, which: (i, 0, 8, which[0] // 4)),
             pl.BlockSpec((4, 2, 128, 1024), lambda i, which: (i, 0, 0, 0)),
+            *[pl.BlockSpec((1024, 256), lambda i, which, j=j: (0, j)) for j in range(4)],
+            *[pl.BlockSpec((512, 512), lambda i, which, j=j: (0, j)) for j in range(2)],
+        ],
+        [
             rows,
-            whole(1024, 1024),
-            whole(512, 1024),
-        ],
-        [rows, rows, rows],
-        [sds((1536, 1024), BF16)] * 3,
-        flops=2 * 1536 * 1024 * 1792,
-        moved=24 << 20,
+            pl.BlockSpec((8, 64, 1024), lambda i, which: (i, 0, 0)),
+            rows,
+            rows,
+            pl.BlockSpec((384, 512), lambda i, which: (i, 0)),
+        ],
+        [
+            sds((1536, 1024), BF16),
+            sds((32, 64, 1024), BF16),
+            sds((1536, 1024), BF16),
+            sds((1536, 1024), BF16),
+            sds((1536, 512), BF16),
+        ],
+        mb=32,
+        flops=2 * 1536 * 1024 * 3328,
+        moved=30 << 20,
         scalars=1,
-    )(which, dz_all, dz_all, slopes, wgu, wdn)
+        moving=(1,),
+        deps=deps,
+    )(which, x, dz_all, dz_all, wgu, wgu, wgu, wgu, wdn, wdn)
 
 
 def expert_grad_kernel(core, x_ref, da, hid, deo, own, other):
@@ -469,6 +519,7 @@
         flops=2 * 1536 * 1024 * 1536,
         moved=16 << 20,
         scalars=1,
+        moving=(1,),
     )(core, x, da, hid, deo)
 
 
@@ -506,6 +557,7 @@
         ],
         [sds((1024, 1024), F32), sds((512, 1024), F32)],
         moved=9 << 20,
+        moving=(1, 2,),
     )(core, own, other)
 
 
@@ -517,7 +569,9 @@
     return inverse * (weighted - scaled * mean), scaled
 
 
-def mid_back_kernel(core, back, pos, y, gain, dz, w_out, dy_ref, own, other, send, acc):
+def mid_back_kernel(
+    core, back, pos, y, gain, dz, w0, w1, w2, w3, dy_ref, own, other, send, acc
+):
     @pl.when(pl.program_id(0) == 0)
     def _():
         acc[...] = jnp.zeros_like(acc)
@@ -550,13 +604,13 @@
             own[...] = dbr[:, 512:]
             other[...] = dbr[:, :512]
 
-        do = dot(dbr, w_out[...], NT).astype(BF16)
+        do = jnp.concatenate([dot(dbr, w[...], NT) for w in (w0, w1, w2, w3)], 1).astype(BF16)
         for s in range(2):
             for half in range(2):
                 first = s * 64 + half * 32
                 for m in range(8):
-                    send[s, m, half, 0:32, :] = do[first : first + 32, m * 128 : (m + 1) * 128]
-                    send[s, m, half, 32:48, :] = extra
+                    send[half, m, s, 0:32, :] = do[first : first + 32, m * 128 : (m + 1) * 128]
+                    send[half, m, s, 32:48, :] = extra
 
 
 def mid_back(core, back, pos, y, gain, dz, w_out, deps):
@@ -570,7 +624,7 @@
             whole(128, 1024),
             whole(1, 1024),
             whole(128, 1024),
-            whole(1024, 1024),
+            *[pl.BlockSpec((256, 1024), lambda e, j=j: (j, 0)) for j in range(4)],
         ],
         [whole(128, 1024), whole(128, 512), whole(128, 512), whole(2, 8, 2, 48, 128)],
         [
@@ -583,7 +637,8 @@
         flops=2 * 128 * 1024 * 1024 + 2 * 1536 * 128 * 1024,
         moved=6 << 20,
         deps=deps,
-    )(core, back, pos, y, gain, dz, w_out)
+        moving=(1,),
+    )(core, back, pos, y, gain, dz, w_out, w_out, w_out, w_out)
 
 
 def combine_kernel(back, pos, gate, y, out, acc):
@@ -610,74 +665,38 @@
         [pltpu.VMEM((128, 1024), F32)],
         flops=4 * 1536 * 128 * 1024,
         moved=4 << 20,
+        moving=(0,),
     )(back, pos, gate, y)
 
 
-def unpack_kernel(core, recv, cos, sin, dproj, own, other):
-    c, s = cos[...], sin[...]
-
-    def rope_back(u):
-        return u * c - swap_halves(u) * s
-
+def last_kernel(recv, w_qkv, tok, gain, dy, grad_tokens, dproj):
+    low = low_half((64, 128))
     for t in range(2):
         rows = slice(t * 64, t * 64 + 64)
         for mm in range(4):
             both = []
             for j in range(2):
                 m = 2 * mm + j
-                dq = jnp.concatenate([recv[t, m, 0, 0:32, :], recv[t, m, 1, 0:32, :]], 0)
-                dproj[rows, m * 128 : (m + 1) * 128] = (rope_back(dq.astype(F32)) * SCALE).astype(
-                    BF16
+                dq = jnp.concatenate([recv[0, m, t, 0:32, :], recv[1, m, t, 0:32, :]], 0)
+                dproj[rows, m * 128 : (m + 1) * 128] = dq
+                both.append(
+                    recv[0, m, t, 32:96, :].astype(F32) + recv[1, m, t, 32:96, :].astype(F32)
                 )
-                both.append(
-                    recv[t, m, 0, 32:96, :].astype(F32) + recv[t, m, 1, 32:96, :].astype(F32)
-                )
-            low = low_half((64, 128))
             dk = jnp.where(low, both[0], pltpu.roll(both[1], HEAD, 1))
             dv = jnp.where(low, pltpu.roll(both[0], HEAD, 1), both[1])
-            dproj[rows, 1024 + mm * 128 : 1152 + mm * 128] = rope_back(dk).astype(BF16)
+            dproj[rows, 1024 + mm * 128 : 1152 + mm * 128] = dk.astype(BF16)
             dproj[rows, 1536 + mm * 128 : 1664 + mm * 128] = dv.astype(BF16)
-
-    @pl.when(core[0] == 0)
-    def _():
-        own[...] = dproj[:, :1024]
-        other[...] = dproj[:, 1024:]
-
-    @pl.when(core[0] == 1)
-    def _():
-        own[...] = dproj[:, 1024:]
-        other[...] = dproj[:, :1024]
-
-
-def unpack(core, recv, cos, sin, deps):
-    return call(
-        unpack_kernel,
-        (1,),
-        [
-            pl.BlockSpec(memory_space=pltpu.SMEM),
-            whole(2, 8, 2, 96, 128),
-            whole(64, 128),
-            whole(64, 128),
-        ],
-        [whole(128, 2048), whole(128, 1024), whole(128, 1024)],
-        [sds((128, 2048), BF16), sds((128, 1024), BF16), sds((128, 1024), BF16)],
-        moved=3 << 20,
-        deps=deps,
-    )(core, recv, cos, sin)
-
-
-def last_kernel(dproj, w_qkv, tok, gain, dy, grad_tokens):
     dh = dot(dproj[...], w_qkv[...], NT)
     dv, _ = norm_back(dh, gain[...], tok[...].astype(F32))
     grad_tokens[...] = dy[...] + dv
 
 
-def last(dproj, w_qkv, tok, gain, dy, deps):
+def last(recv, w_qkv, tok, gain, dy, deps):
     return call(
         last_kernel,
         (1,),
         [
-            whole(128, 2048),
+            whole(2, 8, 2, 96, 128),
             whole(1024, 2048),
             whole(128, 1024),
             whole(1, 1024),
@@ -685,126 +704,194 @@
         ],
         whole(128, 1024),
         sds((128, 1024), F32),
+        [pltpu.VMEM((128, 2048), BF16)],
         flops=2 * 128 * 1024 * 2048,
         moved=6 << 20,
         deps=deps,
-    )(dproj, w_qkv, tok, gain, dy)
-
-
-def weight_grad_kernel(left, left2, right, right2, out):
+        moving=(0,),
+    )(recv, w_qkv, tok, gain, dy)
+
+
+def qkv_grad_kernel(place, h_all, d_ref, gains, out, rows, acc):
+    step = pl.program_id(0)
+    for pair in range(4):
+        for zh in range(2):
+            first = (pair * 2 + zh) * 64
+            rows[first : first + 64, :] = h_all[pair, place[1] ^ zh]
+    dq = d_ref[:, 0:32, :]
+    none = jnp.zeros_like(dq)
+    dq = jnp.where(place[0] == 0, jnp.concatenate([dq, none], 1), jnp.concatenate([none, dq], 1))
+    both = jnp.concatenate([dq.reshape(512, 128), d_ref[:, 32:96, :].reshape(512, 128)], 1)
+    product = dot(rows[...], both, TN)
+
+    @pl.when(step == 0)
+    def _():
+        acc[...] = product
+
+    @pl.when((step > 0) & (step < 3))
+    def _():
+        acc[...] += product
+
+    @pl.when(step == 3)
+    def _():
+        out[:, 0:64, :] = (acc[...] + product).astype(BF16).reshape(16, 64, 256)
+        high = gains[...].astype(BF16).astype(F32)
+        tile = jnp.concatenate([high, gains[...] - high], 1)
+        tile = jnp.concatenate([tile, jnp.zeros_like(tile)], 0).astype(BF16)
+        out[:, 64:80, :] = jnp.broadcast_to(tile[None], (16, 16, 256))
+
+
+def qkv_grad(place, h_all, dqkv, gains):
+    return call(
+        qkv_grad_kernel,
+        (4,),
+        [
+            pl.BlockSpec((4, 2, 64, 1024), lambda i, place: (i, 0, 0, 0)),
+            pl.BlockSpec((8, 96, 128), lambda i, place: (i, 0, 0)),
+            whole(8, 128),
+        ],
+        whole(16, 80, 256),
+        sds((16, 80, 256), BF16),
+        [pltpu.VMEM((512, 1024), BF16), pltpu.VMEM((1024, 256), F32)],
+        flops=2 * 2048 * 1024 * 256,
+        moved=6 << 20,
+        scalars=1,
+    )(place, h_all, dqkv, gains)
+
+
+def out_grad_kernel(left, left2, right, right2, _, out):
     a = jnp.concatenate([left[...], left2[...]], 0)
     b = jnp.concatenate([right[...], right2[...]], 0)
-    out[...] = dot(a, b, TN).astype(BF16)
-
-
-def weight_grad(left, left2, right, right2, deps=()):
-    width = right.shape[1]
+    product = dot(a, b, TN).astype(BF16).reshape(8, 2, 16, 512)
+    out[:, :, :512] = product[:, 0]
+    out[:, :, 512:] = product[:, 1]
+
+
+def out_grad(left, left2, right, right2, eo):
     thin = pl.BlockSpec((128, 256), lambda i: (0, i))
     return call(
-        weight_grad_kernel,
+        out_grad_kernel,
         (4,),
-        [thin, thin, whole(128, width), whole(128, width)],
-        pl.BlockSpec((256, width), lambda i: (i, 0)),
-        sds((1024, width), BF16),
-        flops=2 * 256 * 1024 * width,
+        [thin, thin, whole(128, 512), whole(128, 512), pl.BlockSpec(memory_space=pl.ANY)],
+        pl.BlockSpec((8, 16, 1024), lambda i: (i, 3, 0)),
+        sds((32, 64, 1024), BF16),
+        flops=2 * 256 * 1024 * 512,
         moved=3 << 20,
+        aliases={4: 0},
+        moving=(1, 3),
+    )(left, left2, right, right2, eo)
+
+
+def out_sum_kernel(pieces, out):
+    out[...] = jnp.sum(pieces[...].astype(F32), axis=0).astype(BF16)
+
+
+def out_sum(pieces):
+    return call(
+        out_sum_kernel,
+        (1,),
+        [pl.BlockSpec((32, 16, 1024), lambda i: (0, 3, 0))],
+        whole(16, 1024),
+        sds((16, 1024), BF16),
+        moved=1 << 20,
+        moving=(0,),
+    )(pieces)
+
+
+def add_pieces_kernel(which, qkv, out_w, out_w2, out, gains):
+    total = jnp.sum(qkv[:, 0:64, :].astype(F32), axis=0).astype(BF16)
+    out[:, 0:64, :] = jnp.broadcast_to(total[None], (16, 64, 256))
+    other = (out_w[...].astype(F32) + out_w2[...].astype(F32)).astype(BF16)
+    other = jnp.where(which[0] == 0, other[:, :512], other[:, 512:])
+    out[:, 64:80, :] = jnp.broadcast_to(other[None, :, :256], (16, 16, 256))
+    out[:, 80:96, :] = jnp.broadcast_to(other[None, :, 256:], (16, 16, 256))
+    parts = [qkv[row, 64:80, :].astype(F32)[:8] for row in (0, 4, 8, 12)]
+    parts = [part[:, :128] + part[:, 128:] for part in parts]
+    gains[...] = parts[0] + parts[1] + parts[2] + parts[3]
+
+
+def add_pieces(which, qkv, out_w, out_w2, deps):
+    return call(
+        add_pieces_kernel,
+        (4,),
+        [
+            pl.BlockSpec(memory_space=pltpu.SMEM),
+            whole(16, 80, 256),
+            whole(16, 1024),
+            whole(16, 1024),
+        ],
+        [pl.BlockSpec((16, 96, 256), lambda i: (i, 0, 0)), whole(8, 128)],
+        [sds((64, 96, 256), BF16), sds((8, 128), F32)],
+        moved=5 << 20,
+        moving=(1, 3),
         deps=deps,
-    )(left, left2, right, right2)
-
-
-def add_pieces_kernel(pieces, out):
-    total = jnp.sum(pieces[...].astype(F32), axis=0).astype(BF16)
-    out[...] = jnp.broadcast_to(total[None], out.shape)
-
-
-def add_pieces(pieces, deps=()):
-    block = pl.BlockSpec((64, 16, 256), lambda i: (0, 0, i))
-    return call(
-        add_pieces_kernel,
-        (pieces.shape[2] // 256,),
-        [block],
-        block,
-        sds(pieces.shape, BF16),
-        moved=4 << 20,
-        deps=deps,
-    )(pieces)
-
-
-def final_out_kernel(core, own, other, out):
-    @pl.when(core[0] == 0)
-    def _():
-        out[:, :512] = own[...].astype(F32)
-        out[:, 512:] = other[...].astype(F32)
-
-    @pl.when(core[0] == 1)
-    def _():
-        out[:, :512] = other[...].astype(F32)
-        out[:, 512:] = own[...].astype(F32)
-
-
-def final_out(core, own, other):
-    half = pl.BlockSpec((256, 512), lambda i: (i, 0))
-    return call(
-        final_out_kernel,
-        (4,),
-        [pl.BlockSpec(memory_space=pltpu.SMEM), half, half],
-        pl.BlockSpec((256, 1024), lambda i: (i, 0)),
-        sds((1024, 1024), F32),
-        moved=6 << 20,
-    )(core, own, other)
+    )(which, qkv, out_w, out_w2)
 
 
 def row_sums(product):
     total = jnp.sum(product, axis=-1, keepdims=True)
-    total = jnp.broadcast_to(total, (256, 128))
-    return jnp.concatenate([total[:128].T[0:1], total[128:].T[0:1]], 0)
-
-
-def final_own_kernel(core, own, w_qkv, out, gain_ref):
-    value = own[...].astype(F32)
-    out[...] = value
-    at = pl.ds(pl.program_id(0) * 2, 2)
-    gain_ref[at, :] = row_sums(value * w_qkv[...].astype(F32))
-
-
-def final_own(core, own, w_qkv):
-    half = pl.BlockSpec((256, 1024), lambda i, core: (i, core[0]))
-    return call(
-        final_own_kernel,
+    return jnp.broadcast_to(total, (128, 128)).T[0:1]
+
+
+def final_kernel(which, part, w_qkv, gain, *refs):
+    out, out_w, gain_ref = refs[-3:]
+    step = pl.program_id(0)
+    low = low_half((64, 128))
+    for zh in range(2):
+        rows = slice(zh * 64, zh * 64 + 64)
+        for mm in range(4):
+            both = []
+            for j in range(2):
+                m = 2 * mm + j
+                out[rows, m * 128 : (m + 1) * 128] = part[0, 0, m, zh, 0:64, 0:128].astype(F32)
+                both.append(part[0, 0, m, zh, 0:64, 128:256].astype(F32))
+            out[rows, 1024 + mm * 128 : 1152 + mm * 128] = jnp.where(
+                low, both[0], pltpu.roll(both[1], HEAD, 1)
+            )
+            out[rows, 1536 + mm * 128 : 1664 + mm * 128] = jnp.where(
+                low, pltpu.roll(both[0], HEAD, 1), both[1]
+            )
+        for m in range(8):
+            out_w[0, m, zh, 0, :, 0:256] = part[0, 0, m, zh, 64:80, :].astype(F32)
+            out_w[0, m, zh, 0, :, 256:512] = part[0, 0, m, zh, 80:96, :].astype(F32)
+
+    @pl.when(step == 0)
+    def _():
+        gain_ref[...] = gain[...] if len(refs) == 3 else refs[0][...]
+
+    at = pl.ds(step // 2 * 4 + which[0] * 2 + step % 2, 1)
+    sums = row_sums(out[...] * w_qkv[...].astype(F32))
+    gain_ref[at, :] = sums / gain[at, :]
+
+
+def final(which, part, w_qkv, gain, before=()):
+    def rows(i, which):
+        return (i // 2 * 4 + which[0] * 2 + i % 2, 0)
+
+    wide = pl.BlockSpec((128, 2048), rows)
+    any_space = pl.BlockSpec(memory_space=pl.ANY)
+    return call(
+        final_kernel,
         (4,),
-        [pl.BlockSpec((256, 1024), lambda i, core: (i, 0)), half],
-        [half, whole(8, 128)],
-        [sds((1024, 2048), F32), sds((8, 128), F32)],
-        moved=8 << 20,
+        [
+            pl.BlockSpec((1, 1, 8, 2, 96, 256), lambda i, which: (i // 2, i % 2, 0, 0, 0, 0)),
+            wide,
+            whole(8, 128),
+            *([whole(8, 128), any_space, any_space] if before else []),
+        ],
+        [
+            wide,
+            pl.BlockSpec(
+                (1, 8, 2, 1, 16, 512), lambda i, which: (i % 2, 0, 0, i // 2, 0, which[0])
+            ),
+            whole(8, 128),
+        ],
+        [sds((1024, 2048), F32), sds((2, 8, 2, 2, 16, 1024), F32), sds((8, 128), F32)],
+        moved=16 << 20,
         scalars=1,
-    )(core, own, w_qkv)
-
-
-def final_other_kernel(core, other, w_qkv, part, gain, _, out, gain_ref):
-    value = other[...].astype(F32)
-    out[...] = value
-    at = pl.ds(pl.program_id(0) * 2, 2)
-    gain_ref[at, :] = (part[at, :] + row_sums(value * w_qkv[...].astype(F32))) / gain[at, :]
-
-
-def final_other(core, other, w_qkv, part, gain, out):
-    half = pl.BlockSpec((256, 1024), lambda i, core: (i, 1 - core[0]))
-    return call(
-        final_other_kernel,
-        (4,),
-        [
-            pl.BlockSpec((256, 1024), lambda i, core: (i, 0)),
-            half,
-            whole(8, 128),
-            whole(8, 128),
-            pl.BlockSpec(memory_space=pl.ANY),
-        ],
-        [half, whole(8, 128)],
-        [sds((1024, 2048), F32), sds((8, 128), F32)],
-        moved=8 << 20,
-        scalars=1,
-        aliases={5: 0},
-    )(core, other, w_qkv, part, gain, out)
+        aliases={5: 0, 6: 1} if before else None,
+        moving=(1,),
+    )(which, part.reshape(2, 2, 8, 2, 96, 256), w_qkv, gain, *before)
 
 
 def exchange(x):
@@ -828,6 +915,7 @@
 ):
     core = lax.axis_index("core")
     blk = lax.axis_index(BLK)
+    xh, zh = lax.axis_index("xh"), lax.axis_index("zh")
     tok = tokens.reshape(128, 1024)
     dz = cotangent.reshape(128, 1024)
     wgu = w_gate_up.reshape(1024, 1024)
@@ -835,71 +923,75 @@
     gain_a = gain_attn.reshape(1, 1024)
     gain_m = gain_moe.reshape(1, 1024)
 
-    lane = np.arange(128)
-    frequency = ROPE_BASE ** (-jnp.arange(32, dtype=F32) / 32)
-    angles = (blk * 64 + jnp.arange(64, dtype=jnp.int32)).astype(F32)[:, None] * frequency[None, :]
-    cos = jnp.tile(jnp.cos(angles), (1, 4))
-    sin = jnp.tile(jnp.sin(angles), (1, 4)) * np.where(lane % 64 < 32, -1.0, 1.0).astype(np.float32)
-
+    cos, sin = map(jnp.asarray, rope_tables())
+    zl = lax.axis_index("zl").astype(jnp.int32).reshape(1)
     which = core.astype(jnp.int32).reshape(1)
-    info = jnp.stack([jnp.where(blk < 16, lengths[0], lengths[1]), blk % 2]).astype(jnp.int32)
+    info = jnp.stack([lax.dynamic_index_in_dim(lengths, zh, 0, False), xh]).astype(jnp.int32)
 
     def to_partner(part):
         return lax.ppermute(part, "core", SWAP)
 
-    h, send = pre(tok, gain_a, w_qkv, cos, sin)
+    pos, gate, planned = plan(routes.transpose(0, 2, 1), gates.transpose(0, 2, 1), dz)
+    h, send = pre(
+        blk.astype(jnp.int32).reshape(1), tok, gain_a, w_qkv, cos, sin, [hold(planned)]
+    )
+    planned_far = lax.ppermute(planned, ("zl", "zh"), Z_PAIRS)
+    planned = jnp.stack([after(planned, hold(send)), planned_far])
+    dz_all = lax.all_gather(planned, PLANE).reshape(16, 2, 144, 1024)
     arrived = exchange(send.reshape(32, 96, 128))
-    h_other = to_partner(h)
-    pos, gate, planned = plan(routes.reshape(128, 8), gates.reshape(128, 8), dz, [send])
-    planned = jnp.stack([planned, lax.ppermute(planned, ("zl", "zh"), Z_PAIRS)])
-    dz_all = lax.all_gather(planned, ("x", "y"))
-    o_part, ot, lse = attend(info, arrived, [h_other, planned])
+    o_part, ot, lse = attend(info, arrived, [corner(planned)])
+    h_both = h.reshape(2, 64, 1024)
+    h_mine = lax.dynamic_index_in_dim(h_both, zh, 0, keepdims=False)
+    h_far = lax.ppermute(lax.dynamic_index_in_dim(h_both, 1 - zh, 0, keepdims=False), "zh", SWAP)
+    h_near = jnp.stack([after(h_mine, hold(o_part)), h_far])
     o_recv = exchange(o_part).reshape(2, 8, 2, 32, 128)
-    o, y, rows = mid(o_recv, w_out, tok, gain_m, pos)
+    o, y, rows = mid(o_recv, w_out, tok, gain_m, pos, [corner(h_near[1])])
     o_other = to_partner(o)
     x = among_experts(rows).reshape(1536, 1024)
-    eo, slopes, hid = expert(x, wgu, wdn, [o_other])
-    eo_back = among_experts(eo.reshape(32, 48, 1024))
-    place = jnp.stack([blk, lax.axis_index("zh")]).astype(jnp.int32)
-    dx2, da, deo = expert_back(place, dz_all, slopes, wgu, wdn)
-    dx2_back = among_experts(after(dx2.reshape(32, 48, 1024), eo_back))
+    place = jnp.stack([blk, zh]).astype(jnp.int32)
+    dx2, eo, da, deo, hid = expert(place, x, dz_all, wgu, wdn, [corner(o_other)])
+    dx2_back = among_experts(dx2.reshape(32, 48, 1024))
     experts_own, experts_send = expert_grad(which, x, da, hid, deo)
+    dy, dbr_own, dbr_send, do = mid_back(
+        which, dx2_back, pos, y, gain_m, dz, w_out, [hold(experts_send)]
+    )
     experts_own = add_rounded(experts_own, to_partner(experts_send))
+    experts_far = lax.ppermute(experts_own, "zl", SWAP)
+    h_near = after(h_near, hold(experts_send))
+    h_all = lax.all_gather(h_near, PLANE).reshape(16, 2, 64, 1024)
+
+
+    do_recv = exchange(do.reshape(32, 48, 128))
+    eo = out_grad(o, o_other, dbr_own, to_partner(dbr_send), eo)
+    eo_back = among_experts(after(eo, do_recv))
     mixed = combine(eo_back, pos, gate, y)
-    dy, dbr_own, dbr_send, do = mid_back(
-        which, dx2_back, pos, y, gain_m, dz, w_out, [experts_own, mixed]
+    out_part = out_sum(eo_back)
+    out_far = lax.ppermute(out_part, "zl", SWAP)
+    dqkv, gains = attend_back(info, arrived, do_recv, ot, lse, cos, sin, [])
+    experts_own = add_rounded(after(experts_own, hold(dqkv)), experts_far)
+
+    place = jnp.stack([xh, zh]).astype(jnp.int32)
+    dqkv_recv = exchange(after(dqkv, eo_back)).reshape(2, 8, 2, 96, 128)
+    qkv_partial = after(qkv_grad(place, h_all, dqkv, gains), dqkv_recv, corner(experts_own))
+    qkv_pieces = lax.all_to_all(qkv_partial, SAME_COLUMNS, 0, 0, tiled=True)
+    experts_other = to_partner(experts_own)
+    grad_gate_up, grad_down = final_expert(which, experts_own, experts_other)
+    copies, gains = add_pieces(
+        zl, qkv_pieces, out_part, out_far, []
     )
-    experts_own = add_rounded(experts_own, lax.ppermute(experts_own, "zl", SWAP))
-
-    do_recv = exchange(do.reshape(32, 48, 128))
-    out_partial = weight_grad(o, o_other, dbr_own, to_partner(dbr_send), [experts_own])
-    out_pieces = among_chips(out_partial.reshape(64, 16, 512))
-    dqkv, gains = attend_back(info, arrived, do_recv, ot, lse, [out_partial])
-    dqkv_recv = exchange(after(dqkv, out_pieces)).reshape(2, 8, 2, 96, 128)
-
-    for axis in ROWS:
-        gains = gains + lax.ppermute(gains, axis, SWAP)
-
-    out_copies = add_pieces(out_pieces)
-    dproj, dproj_own, dproj_send = unpack(which, dqkv_recv, cos, sin, [gains, out_copies])
-    out_own = among_chips(out_copies).reshape(1024, 512)
-    grad_out = final_out(which, out_own, to_partner(out_own))
-    grad_gate_up, grad_down = final_expert(which, experts_own, to_partner(experts_own))
-
-    partial = weight_grad(h, h_other, dproj_own, to_partner(dproj_send))
-    grad_tokens = last(dproj, w_qkv, tok, gain_a, dy, [partial])
-    pieces = among_chips(after(partial.reshape(64, 16, 1024), out_own))
-    own = among_chips(add_pieces(pieces, [grad_out, grad_gate_up, grad_tokens])).reshape(1024, 1024)
-    own_part, gain_part = final_own(which, own, w_qkv)
-    grad_qkv, grad_gain_attn = final_other(
-        which, to_partner(own), w_qkv, gain_part, gain_attn.reshape(8, 128), own_part
+    grad_tokens = last(dqkv_recv, w_qkv, tok, gain_a, dy, [])
+    own = after(among_chips(copies), hold(mixed), hold(grad_gate_up), hold(grad_tokens))
+    rows = final(which, own, w_qkv, gain_attn.reshape(8, 128))
+    grad_qkv, grad_out, grad_gain_attn = final(
+        1 - which, to_partner(own), w_qkv, gain_attn.reshape(8, 128), (rows[2], rows[0], rows[1])
     )
+
     return (
         mixed.reshape(2, 64, 1024),
         grad_tokens.reshape(2, 64, 1024),
         grad_gain_attn.reshape(1024),
         grad_qkv,
-        grad_out,
+        grad_out.reshape(1024, 1024),
         gains.reshape(1024),
         grad_gate_up[None],
         grad_down[None],
@@ -907,7 +999,7 @@
 
 
 def solution(mesh):
-    split = Mesh(mesh.devices.reshape(2, 2, 4, 4, 2), AXES)
+    split = Mesh(mesh.devices.reshape(2, 2, 2, 2, 4, 2), AXES)
     rows = P(ROWS, BLK, None)
     return jax.shard_map(
         shards,

time: 454 us -> 406 us (0.89)
  blocking collectives: 47.7 us -> 0 us
  waiting for transfers between devices: 133 us -> 163 us
  local copies, waits for them, and re-layouts: 41.3 us -> 12 us
  starting transfers between devices: 115 us -> 96.7 us
  Pallas kernels: 91.6 us -> 109 us
    all_to_all x2 -> x0, blocking collectives: 47.7 us -> none  [the longest x1 32.6 us: among_chips(): return lax.all_to_all(x, CHIPS, 0, 0, tiled=True)]
    unnamed x117 -> x29, local copies, waits for them, and re-layouts: 40.6 us -> 10 us
    all_to_all x3 -> x1, starting transfers between devices: 31.8 us -> 7.98 us  [among_chips(): return lax.all_to_all(x, CHIPS, 0, 0, tiled=True)]
    all_to_all x3, waiting for transfers between devices: 77.5 us -> 96.8 us  [among_experts(): lax.all_to_all(x, CHIPS, 0, 0, tiled=True, axis_index_groups=EXPERT_GROUPS)]
    pallas_call x20 -> x17, Pallas kernels: 91.6 us -> 109 us  [call(): built(*[place(i, x) for i, x in enumerate(operands)], *deps)]
    all_to_all x0 -> x1, starting transfers between devices: none -> 9.34 us  [shards(): qkv_pieces = lax.all_to_all(qkv_partial, SAME_COLUMNS, 0, 0, tiled=True)]
    ppermute x8 -> x5, starting transfers between devices: 27.7 us -> 18.4 us  [to_partner(): return lax.ppermute(part, 'core', SWAP)]
    all_to_all x3 -> x1, waiting for transfers between devices: 14.6 us -> 20.1 us  [among_chips(): return lax.all_to_all(x, CHIPS, 0, 0, tiled=True)]
  transfers between devices with their start and end apart: 22 -> 20, of which waited for: 15 -> 16; matrix products, arithmetic and copies ran while one was open for 2% -> 3% of each run, Pallas kernels for 18% -> 20%
where the time goes in v2:
time: 406 us; the launch traced here: 404 us
  waiting for transfers between devices  163 us (40%)
  Pallas kernels  109 us (27%)
  starting transfers between devices  96.7 us (24%)
  between operations  14.2 us (3%)
  local copies, waits for them, and re-layouts  12 us (3%)
  other arithmetic  8.99 us (2%)
    pallas_call x17, Pallas kernels, call(): built(*[place(i, x) for i, x in enumerate(operands)], *deps)  109 us
    all_to_all x3, waiting for transfers between devices, among_experts(): lax.all_to_all(x, CHIPS, 0, 0, tiled=True, axis_index_groups=EXPERT_GROUPS)  96.8 us
    all_to_all x4, starting transfers between devices, exchange(): return lax.all_to_all(x, BLK, 0, 0, tiled=True)  28.8 us
    all_to_all x4, waiting for transfers between devices, exchange(): return lax.all_to_all(x, BLK, 0, 0, tiled=True)  25 us
    all_to_all x3, starting transfers between devices, among_experts(): lax.all_to_all(x, CHIPS, 0, 0, tiled=True, axis_index_groups=EXPERT_GROUPS)  22.4 us
    all_to_all x1, waiting for transfers between devices, among_chips(): return lax.all_to_all(x, CHIPS, 0, 0, tiled=True)  20.1 us
    ppermute x5, starting transfers between devices, to_partner(): return lax.ppermute(part, 'core', SWAP)  18.4 us
    unnamed x29, local copies, waits for them, and re-layouts  10 us
  transfers between devices with their start and end apart: 20, of which 16 were waited for; matrix products, arithmetic and copies ran while one was open for 3% of the time, Pallas kernels for 20%

profile of v2, /device:TPU:1, one launch (start us, length us, event | category | flops | bytes accessed | tf_op | source)
XLA Modules:
  0.0 404.0 jit_solution(11533197881043355656)
XLA Ops:
  7.2 1.9 shard_map.188
  9.1 4.6 %collective-permute-start.2 = (bf16[144,1024]{1,0:T(8,128)(2,1)}, bf16[144,1024]{1,0:T(8,128)(2,1)S(1)}, u32[]{:S(2)}, u32[]{:S(2)}) collective-permute-start(bf16[144,1024]{1,0:T(8,128)(2,1)} %get-tuple-element.42.refs_8_.refs_0_), channel_id=1, source_target_pairs={{0,65},{1,64},{64,1},{65,0},{2,67},{3,66},{66,3},{67,2},{4,69},{5,... | collective-permute-start | bytes 884744 | tf_op jit(solution)/shard_map/ppermute | solution.py:938
  13.7 5.1 %shard_map.189 = (bf16[128,1024]{1,0:T(8,128)(2,1)}, bf16[2,8,2,96,128]{4,3,2,1,0:T(8,128)(2,1)}) custom-call(s32[1]{0:T(128)} %bitcast.1.refs_0_, bf16[128,1024]{1,0:T(8,128)(2,1)} %bitcast.52, f32[1,1024]{1,0:T(1,128)} %bitcast.64, bf16[1024,2048]{1,0:T(8,128)(2,1)} %refs_2_.5, bf16[1024,2048]{1,0:T(8,128)(2,1)} %refs_2_.5, bf16[1024,2048]{1,0:T(8,128)(2,1)} %refs_2_.5, ...), custom_call_target="tpu_custom_call" | custom-call | flops 536870912 | bytes 5242880 | tf_op jit(solution)/shard_map/pallas_call | solution.py:88
  22.5 7.8 %all-to-all-start = ((bf16[32,96,128]{2,1,0:T(8,128)(2,1)}), bf16[32,96,128]{2,1,0:T(8,128)(2,1)S(1)}, u32[]{:S(2)}, u32[]{:S(2)}) async-start(bf16[32,96,128]{2,1,0:T(8,128)(2,1)} %bitcast.7), calls=%async_computation | async-start | bytes 1572864 | tf_op jit(solution)/shard_map/all_to_all | solution.py:898
  32.3 12.1 %all-to-all-done.refs_1_ = bf16[32,96,128]{2,1,0:T(8,128)(2,1)S(1)} async-done(((bf16[32,96,128]{2,1,0:T(8,128)(2,1)}), bf16[32,96,128]{2,1,0:T(8,128)(2,1)S(1)}, u32[]{:S(2)}, u32[]{:S(2)}) %all-to-all-start) | async-done | bytes 786464 | tf_op jit(solution)/shard_map/all_to_all | solution.py:898
  44.4 8.3 %shard_map.191 = (bf16[32,32,128]{2,1,0:T(8,128)(2,1)}, f32[4,64,512]{2,1,0:T(8,128)}, f32[4,8,512]{2,1,0:T(8,128)}) custom-call(s32[2]{0:T(128)S(1)} %pad_add_fusion.refs_0_, bf16[32,96,128]{2,1,0:T(8,128)(2,1)S(1)} %all-to-all-done.refs_1_, bf16[8,128]{1,0:T(8,128)(2,1)S(1)} %slice.16.refs_2_), custom_call_target="tpu_custom_call" | custom-call | flops 1342177280 | bytes 2097152 | tf_op jit(solution)/shard_map/pallas_call | solution.py:88
  52.8 5.6 %all-to-all-start.1 = ((bf16[32,32,128]{2,1,0:T(8,128)(2,1)}), bf16[32,32,128]{2,1,0:T(8,128)(2,1)S(1)}, u32[]{:S(2)}, u32[]{:S(2)}) async-start(bf16[32,32,128]{2,1,0:T(8,128)(2,1)} %get-tuple-element.44.refs_1_), calls=%async_computation.1 | async-start | bytes 524288 | tf_op jit(solution)/shard_map/all_to_all | solution.py:898
  59.1 2.7 collective-permute-start
  61.8 3.0 collective-permute-done
  64.8 3.2 all-to-all-done.1
  68.0 5.3 %shard_map.192 = (bf16[128,1024]{1,0:T(8,128)(2,1)}, f32[128,1024]{1,0:T(8,128)}, bf16[32,48,1024]{2,1,0:T(8,128)(2,1)}) custom-call(bf16[2,8,2,32,128]{4,3,2,1,0:T(8,128)(2,1)S(1)} %bitcast.46, bf16[1024,1024]{1,0:T(8,128)(2,1)} %refs_9_.1, bf16[1024,1024]{1,0:T(8,128)(2,1)} %refs_9_.1, bf16[1024,1024]{1,0:T(8,128)(2,1)} %refs_9_.1, ...), custom_call_target="tpu_custom_call" | custom-call | flops 671088640 | bytes 6291456 | tf_op jit(solution)/shard_map/pallas_call | solution.py:88
  73.3 7.3 %all-to-all-start.2 = ((bf16[32,48,1024]{2,1,0:T(8,128)(2,1)}), bf16[32,48,1024]{2,1,0:T(8,128)(2,1)S(1)}, u32[]{:S(2)}, u32[]{:S(2)}) async-start(bf16[32,48,1024]{2,1,0:T(8,128)(2,1)} %get-tuple-element.48), calls=%async_computation.2 | async-start | bytes 6291456 | tf_op jit(solution)/shard_map/all_to_all | solution.py:906
  80.6 9.7 %collective-permute-start.1 = (bf16[128,1024]{1,0:T(8,128)(2,1)}, bf16[128,1024]{1,0:T(8,128)(2,1)S(1)}, u32[]{:S(2)}, u32[]{:S(2)}) collective-permute-start(bf16[128,1024]{1,0:T(8,128)(2,1)} %get-tuple-element.47.refs_0_), channel_id=1, source_target_pairs={{0,32},{32,0},{1,33},{33,1},{2,34},{34,2},{3,35},{35,3},{4,36},{36... | collective-permute-start | bytes 786440 | tf_op jit(solution)/shard_map/ppermute | solution.py:932
  92.1 44.1 %all-to-all-done.2 = bf16[32,48,1024]{2,1,0:T(8,128)(2,1)S(1)} async-done(((bf16[32,48,1024]{2,1,0:T(8,128)(2,1)}), bf16[32,48,1024]{2,1,0:T(8,128)(2,1)S(1)}, u32[]{:S(2)}, u32[]{:S(2)}) %all-to-all-start.2) | async-done | bytes 3145760 | tf_op jit(solution)/shard_map/all_to_all | solution.py:906
  136.6 18.9 %shard_map.193 = (bf16[1536,1024]{1,0:T(8,128)(2,1)}, bf16[32,64,1024]{2,1,0:T(8,128)(2,1)}, bf16[1536,1024]{1,0:T(8,128)(2,1)}, bf16[1536,1024]{1,0:T(8,128)(2,1)}, bf16[1536,512]{1,0:T(8,128)(2,1)}) custom-call(s32[2]{0:T(128)S(1)} %pad_add_fusion.1.refs_0_, bf16[1536,1024]{1,0:T(8,128)(2,1)S(1)} %bitcast.43, bf16[16,2,144,1024]{3,2,1,0:T(8,128)(2,1)} %bitcast.72, ...), custom_call_target="tpu_custom_call" | custom-call | flops 10468982784 | bytes 31457280 | tf_op jit(solution)/shard_map/pallas_call | solution.py:88
  155.5 9.3 %all-to-all-start.3 = ((bf16[32,48,1024]{2,1,0:T(8,128)(2,1)}), bf16[32,48,1024]{2,1,0:T(8,128)(2,1)S(1)}, u32[]{:S(2)}, u32[]{:S(2)}) async-start(bf16[32,48,1024]{2,1,0:T(8,128)(2,1)} %bitcast.50), calls=%async_computation.3 | async-start | bytes 6291456 | tf_op jit(solution)/shard_map/all_to_all | solution.py:906
  167.0 10.9 %shard_map.194 = (bf16[768,1024]{1,0:T(8,128)(2,1)}, bf16[768,1024]{1,0:T(8,128)(2,1)}) custom-call(s32[1]{0:T(128)} %bitcast.12.refs_0_, bf16[1536,1024]{1,0:T(8,128)(2,1)S(1)} %bitcast.44, bf16[1536,1024]{1,0:T(8,128)(2,1)} %get-tuple-element.51.refs_2_, bf16[1536,512]{1,0:T(8,128)(2,1)} %get-tuple-element.52.refs_3_, ...), custom_call_target="tpu_custom_call" | custom-call | flops 4831838208 | bytes 16777216 | tf_op jit(solution)/shard_map/pallas_call | solution.py:88
  177.9 28.8 %all-to-all-done.3.refs_1_ = bf16[32,48,1024]{2,1,0:T(8,128)(2,1)S(1)} async-done(((bf16[32,48,1024]{2,1,0:T(8,128)(2,1)}), bf16[32,48,1024]{2,1,0:T(8,128)(2,1)S(1)}, u32[]{:S(2)}, u32[]{:S(2)}) %all-to-all-start.3) | async-done | bytes 3145760 | tf_op jit(solution)/shard_map/all_to_all | solution.py:906
  206.7 5.7 %shard_map.195 = (f32[128,1024]{1,0:T(8,128)}, bf16[128,512]{1,0:T(8,128)(2,1)}, bf16[128,512]{1,0:T(8,128)(2,1)}, bf16[2,8,2,48,128]{4,3,2,1,0:T(8,128)(2,1)}) custom-call(s32[1]{0:T(128)} %bitcast.12.refs_0_, bf16[32,48,1024]{2,1,0:T(8,128)(2,1)S(1)} %all-to-all-done.3.refs_1_, s32[32,128]{1,0:T(8,128)} %get-tuple-element.45.refs_7_.refs_2_.refs_1_, ...), custom_call_target="tpu_custom_call" | custom-call | flops 671088640 | bytes 6291456 | tf_op jit(solution)/shard_map/pallas_call | solution.py:88
  212.4 7.5 %all-to-all-start.4 = ((bf16[32,48,128]{2,1,0:T(8,128)(2,1)}), bf16[32,48,128]{2,1,0:T(8,128)(2,1)S(1)}, u32[]{:S(2)}, u32[]{:S(2)}) async-start(bf16[32,48,128]{2,1,0:T(8,128)(2,1)} %bitcast.60), calls=%async_computation.4 | async-start | bytes 786432 | tf_op jit(solution)/shard_map/all_to_all | solution.py:898
  223.0 3.7 shard_map.196.refs_0_
  226.7 7.0 %all-to-all-done.4.refs_1_.refs_2_ = bf16[32,48,128]{2,1,0:T(8,128)(2,1)S(1)} async-done(((bf16[32,48,128]{2,1,0:T(8,128)(2,1)}), bf16[32,48,128]{2,1,0:T(8,128)(2,1)S(1)}, u32[]{:S(2)}, u32[]{:S(2)}) %all-to-all-start.4) | async-done | bytes 393248 | tf_op jit(solution)/shard_map/all_to_all | solution.py:898
  233.7 5.7 %all-to-all-start.5 = ((bf16[32,64,1024]{2,1,0:T(8,128)(2,1)}), bf16[32,64,1024]{2,1,0:T(8,128)(2,1)}, u32[]{:S(2)}, u32[]{:S(2)}) async-start(bf16[32,64,1024]{2,1,0:T(8,128)(2,1)} %shard_map.197), calls=%async_computation.5 | async-start | bytes 8388608 | tf_op jit(solution)/shard_map/all_to_all | solution.py:906
  239.4 3.5 collective-permute-start.4
  243.0 3.0 collective-permute-done.4
  246.0 2.1 add_convert_fusion.1.refs_0_
  248.9 14.3 %shard_map.199 = (bf16[32,96,128]{2,1,0:T(8,128)(2,1)}, f32[8,128]{1,0:T(8,128)}) custom-call(s32[2]{0:T(128)S(1)} %pad_add_fusion.refs_0_, bf16[32,96,128]{2,1,0:T(8,128)(2,1)S(1)} %copy-done.9, bf16[32,48,128]{2,1,0:T(8,128)(2,1)S(1)} %all-to-all-done.4.refs_1_.refs_2_, f32[4,64,512]{2,1,0:T(8,128)} %get-tuple-element.60.refs_3_, ...), custom_call_target="tpu_custom_call" | custom-call | flops 3355443200 | bytes 3145728 | tf_op jit(solution)/shard_map/pallas_call | solution.py:88
  263.1 2.1 copy.35.refs_0_
  265.2 23.9 %all-to-all-done.5.refs_0_.refs_1_ = bf16[32,64,1024]{2,1,0:T(8,128)(2,1)} async-done(((bf16[32,64,1024]{2,1,0:T(8,128)(2,1)}), bf16[32,64,1024]{2,1,0:T(8,128)(2,1)}, u32[]{:S(2)}, u32[]{:S(2)}) %all-to-all-start.5) | async-done | bytes 4194336 | tf_op jit(solution)/shard_map/all_to_all | solution.py:906
  289.1 8.0 %all-to-all-start.6 = ((bf16[32,96,128]{2,1,0:T(8,128)(2,1)}), bf16[32,96,128]{2,1,0:T(8,128)(2,1)S(1)}, u32[]{:S(2)}, u32[]{:S(2)}) async-start(bf16[32,96,128]{2,1,0:T(8,128)(2,1)} %shard_map.200), calls=%async_computation.6 | async-start | bytes 1572864 | tf_op jit(solution)/shard_map/all_to_all | solution.py:898
  297.1 2.5 add_convert_fusion.refs_1_
  300.8 5.8 %shard_map.204.refs_0_ = bf16[16,80,256]{2,1,0:T(8,128)(2,1)} custom-call(s32[2]{0:T(128)S(1)} %pad_add_fusion.2.refs_0_, bf16[16,2,64,1024]{3,2,1,0:T(8,128)(2,1)} %bitcast.47, bf16[32,96,128]{2,1,0:T(8,128)(2,1)} %get-tuple-element.62.refs_2_.refs_1_, f32[8,128]{1,0:T(8,128)} %get-tuple-element.64.refs_3_), custom_call_target="tpu_custom_call" | custom-call | flops 1073741824 | bytes 6291456 | tf_op jit(solution)/shard_map/pallas_call | solution.py:88
  306.7 2.7 all-to-all-done.6
  309.4 9.3 %all-to-all-start.7 = ((bf16[16,80,256]{2,1,0:T(8,128)(2,1)}), bf16[16,80,256]{2,1,0:T(8,128)(2,1)S(1)}, u32[]{:S(2)}, u32[]{:S(2)}) async-start(bf16[16,80,256]{2,1,0:T(8,128)(2,1)} %shard_map.206), calls=%async_computation.7 | async-start | bytes 1310720 | tf_op jit(solution)/shard_map/all_to_all | solution.py:976
  318.7 2.0 shard_map.207.refs_2_
  322.2 4.5 %collective-permute-done.6.refs_3_ = bf16[16,1024]{1,0:T(8,128)(2,1)S(1)} collective-permute-done((bf16[16,1024]{1,0:T(8,128)(2,1)}, bf16[16,1024]{1,0:T(8,128)(2,1)S(1)}, u32[]{:S(2)}, u32[]{:S(2)}) %collective-permute-start.6) | collective-permute-done | bytes 32800 | tf_op jit(solution)/shard_map/ppermute | solution.py:969
  326.7 4.2 %all-to-all-done.7.refs_1_ = bf16[16,80,256]{2,1,0:T(8,128)(2,1)S(1)} async-done(((bf16[16,80,256]{2,1,0:T(8,128)(2,1)}), bf16[16,80,256]{2,1,0:T(8,128)(2,1)S(1)}, u32[]{:S(2)}, u32[]{:S(2)}) %all-to-all-start.7) | async-done | bytes 655392 | tf_op jit(solution)/shard_map/all_to_all | solution.py:976
  330.9 3.1 shard_map.208
  333.9 8.0 %all-to-all-start.8 = ((bf16[64,96,256]{2,1,0:T(8,128)(2,1)}), bf16[64,96,256]{2,1,0:T(8,128)(2,1)S(1)}, u32[]{:S(2)}, u32[]{:S(2)}) async-start(bf16[64,96,256]{2,1,0:T(8,128)(2,1)} %get-tuple-element.66), calls=%async_computation.8 | async-start | bytes 6291456 | tf_op jit(solution)/shard_map/all_to_all | solution.py:910
  342.7 3.2 collective-permute-done.7.refs_2_
  347.4 3.8 shard_map.209
  351.2 4.8 %shard_map.198.refs_1_ = bf16[128,1024]{1,0:T(8,128)(2,1)} custom-call(bf16[32,64,1024]{2,1,0:T(8,128)(2,1)} %all-to-all-done.5.refs_0_.refs_1_, s32[32,128]{1,0:T(8,128)} %get-tuple-element.45.refs_7_.refs_2_.refs_1_, f32[32,128]{1,0:T(8,128)} %get-tuple-element.59.refs_2_, f32[128,1024]{1,0:T(8,128)} %get-tuple-element.50.refs_3_), custom_call_target="tpu_custom_call" | custom-call | flops 805306368 | bytes 4194304 | tf_op jit(solution)/shard_map/pallas_call | solution.py:88
  356.0 4.9 %shard_map.201.refs_3_ = f32[128,1024]{1,0:T(8,128)} custom-call(bf16[2,8,2,96,128]{4,3,2,1,0:T(8,128)(2,1)S(1)} %bitcast.42, bf16[1024,2048]{1,0:T(8,128)(2,1)} %refs_2_.5, bf16[128,1024]{1,0:T(8,128)(2,1)} %bitcast.54, f32[1,1024]{1,0:T(1,128)} %bitcast.65, f32[128,1024]{1,0:T(8,128)} %get-tuple-element.63.refs_4_), custom_call_target="tpu_custom_call" | custom-call | flops 536870912 | bytes 6291456 | tf_op jit(solution)/shard_map/pallas_call | solution.py:88
  360.8 20.1 %all-to-all-done.8.refs_0_ = bf16[64,96,256]{2,1,0:T(8,128)(2,1)S(1)} async-done(((bf16[64,96,256]{2,1,0:T(8,128)(2,1)}), bf16[64,96,256]{2,1,0:T(8,128)(2,1)S(1)}, u32[]{:S(2)}, u32[]{:S(2)}) %all-to-all-start.8) | async-done | bytes 3145760 | tf_op jit(solution)/shard_map/all_to_all | solution.py:910
  382.6 2.6 collective-permute-start.8
  385.1 1.9 copy-done.1
  387.0 5.0 %shard_map.211 = (f32[1024,2048]{1,0:T(8,128)}, f32[2,8,2,2,16,1024]{5,4,3,2,1,0:T(8,128)}, f32[8,128]{1,0:T(8,128)}) custom-call(s32[1]{0:T(128)} %bitcast.12.refs_0_, bf16[2,2,8,2,96,256]{5,4,3,2,1,0:T(8,128)(2,1)S(1)} %bitcast.40, bf16[1024,2048]{1,0:T(8,128)(2,1)} %refs_2_.5, f32[8,128]{1,0:T(8,128)} %bitcast.66), custom_call_target="tpu_custom_call" | custom-call | bytes 16777216 | tf_op jit(solution)/shard_map/pallas_call | solution.py:88
  392.0 5.2 %shard_map.212 = (f32[1024,2048]{1,0:T(8,128)}, f32[2,8,2,2,16,1024]{5,4,3,2,1,0:T(8,128)}, f32[8,128]{1,0:T(8,128)}) custom-call(s32[1]{0:T(128)S(6)} %sub.7.refs_0_, bf16[2,2,8,2,96,256]{5,4,3,2,1,0:T(8,128)(2,1)S(1)} %bitcast.45, bf16[1024,2048]{1,0:T(8,128)(2,1)} %refs_2_.5, f32[8,128]{1,0:T(8,128)} %bitcast.67, ...), custom_call_target="tpu_custom_call", output_to_operand_aliasing={{0}: (5, {}), {1}: (6, {})} | custom-call | bytes 16777216 | tf_op jit(solution)/shard_map/pallas_call | solution.py:88
  (61 shorter events, 20.9 us)
Async XLA Ops:
  7.2 129.4 %all-gather.5.cloned.1.call-start = ((), (), s32[]{:S(2)}) async-start(), calls=%async_computation.9 | async-start | bytes 10027008 | tf_op jit(solution)/shard_map/all_gather | solution.py:940
  9.1 11.5 %collective-permute-start.2 = (bf16[144,1024]{1,0:T(8,128)(2,1)}, bf16[144,1024]{1,0:T(8,128)(2,1)S(1)}, u32[]{:S(2)}, u32[]{:S(2)}) collective-permute-start(bf16[144,1024]{1,0:T(8,128)(2,1)} %get-tuple-element.42.refs_8_.refs_0_), channel_id=1, source_target_pairs={{0,65},{1,64},{64,1},{65,0},{2,67},{3,66},{66,3},{67,2},{4,69},{5,... | collective-permute-start | bytes 884744 | tf_op jit(solution)/shard_map/ppermute | solution.py:938
  18.9 11.4 %copy-start.13 = (s32[2]{0:T(128)S(1)}, s32[2]{0:T(128)}, u32[]{:S(2)}) copy-start(s32[2]{0:T(128)} %param.14) | copy-start | bytes 28
  22.5 21.9 %all-to-all-start = ((bf16[32,96,128]{2,1,0:T(8,128)(2,1)}), bf16[32,96,128]{2,1,0:T(8,128)(2,1)S(1)}, u32[]{:S(2)}, u32[]{:S(2)}) async-start(bf16[32,96,128]{2,1,0:T(8,128)(2,1)} %bitcast.7), calls=%async_computation | async-start | bytes 1572864 | tf_op jit(solution)/shard_map/all_to_all | solution.py:898
  30.3 28.1 %copy-start.12 = (bf16[128,1024]{1,0:T(8,128)(2,1)S(1)}, bf16[128,1024]{1,0:T(8,128)(2,1)}, u32[]{:S(2)}) copy-start(bf16[128,1024]{1,0:T(8,128)(2,1)} %get-tuple-element.46) | copy-start | bytes 786436
  44.4 8.3 %copy-start.8 = (bf16[32,96,128]{2,1,0:T(8,128)(2,1)}, bf16[32,96,128]{2,1,0:T(8,128)(2,1)S(1)}, u32[]{:S(2)}) copy-start(bf16[32,96,128]{2,1,0:T(8,128)(2,1)S(1)} %all-to-all-done.refs_1_) | copy-start | bytes 2359300
  52.8 15.2 %all-to-all-start.1 = ((bf16[32,32,128]{2,1,0:T(8,128)(2,1)}), bf16[32,32,128]{2,1,0:T(8,128)(2,1)S(1)}, u32[]{:S(2)}, u32[]{:S(2)}) async-start(bf16[32,32,128]{2,1,0:T(8,128)(2,1)} %get-tuple-element.44.refs_1_), calls=%async_computation.1 | async-start | bytes 524288 | tf_op jit(solution)/shard_map/all_to_all | solution.py:898
  59.1 5.8 %collective-permute-start = (bf16[64,1024]{1,0:T(8,128)(2,1)S(1)}, bf16[64,1024]{1,0:T(8,128)(2,1)S(1)}, u32[]{:S(2)}, u32[]{:S(2)}) collective-permute-start(bf16[64,1024]{1,0:T(8,128)(2,1)S(1)} %get-tuple-element.77), channel_id=1, source_target_pairs={{0,1},{1,0},{2,3},{3,2},{4,5},{5,4},{6,7},{7,6},{8,9},{9,8},{10,11... | collective-permute-start | bytes 393224 | tf_op jit(solution)/shard_map/ppermute | solution.py:945
  73.3 62.9 %all-to-all-start.2 = ((bf16[32,48,1024]{2,1,0:T(8,128)(2,1)}), bf16[32,48,1024]{2,1,0:T(8,128)(2,1)S(1)}, u32[]{:S(2)}, u32[]{:S(2)}) async-start(bf16[32,48,1024]{2,1,0:T(8,128)(2,1)} %get-tuple-element.48), calls=%async_computation.2 | async-start | bytes 6291456 | tf_op jit(solution)/shard_map/all_to_all | solution.py:906
  80.6 11.4 %collective-permute-start.1 = (bf16[128,1024]{1,0:T(8,128)(2,1)}, bf16[128,1024]{1,0:T(8,128)(2,1)S(1)}, u32[]{:S(2)}, u32[]{:S(2)}) collective-permute-start(bf16[128,1024]{1,0:T(8,128)(2,1)} %get-tuple-element.47.refs_0_), channel_id=1, source_target_pairs={{0,32},{32,0},{1,33},{33,1},{2,34},{34,2},{3,35},{35,3},{4,36},{36... | collective-permute-start | bytes 786440 | tf_op jit(solution)/shard_map/ppermute | solution.py:932
  136.2 19.3 %copy-start.6 = (bf16[32,48,1024]{2,1,0:T(8,128)(2,1)}, bf16[32,48,1024]{2,1,0:T(8,128)(2,1)S(1)}, u32[]{:S(2)}) copy-start(bf16[32,48,1024]{2,1,0:T(8,128)(2,1)S(1)} %all-to-all-done.2) | copy-start | bytes 9437188
  155.5 51.2 %all-to-all-start.3 = ((bf16[32,48,1024]{2,1,0:T(8,128)(2,1)}), bf16[32,48,1024]{2,1,0:T(8,128)(2,1)S(1)}, u32[]{:S(2)}, u32[]{:S(2)}) async-start(bf16[32,48,1024]{2,1,0:T(8,128)(2,1)} %bitcast.50), calls=%async_computation.3 | async-start | bytes 6291456 | tf_op jit(solution)/shard_map/all_to_all | solution.py:906
  164.8 136.0 %all-gather.7.cloned.1.call-start = ((), (), s32[]{:S(2)}) async-start(), calls=%async_computation.10 | async-start | bytes 4456448 | tf_op jit(solution)/shard_map/all_gather | solution.py:961
  165.1 1.9 copy-start.7
  212.4 21.2 %all-to-all-start.4 = ((bf16[32,48,128]{2,1,0:T(8,128)(2,1)}), bf16[32,48,128]{2,1,0:T(8,128)(2,1)S(1)}, u32[]{:S(2)}, u32[]{:S(2)}) async-start(bf16[32,48,128]{2,1,0:T(8,128)(2,1)} %bitcast.60), calls=%async_computation.4 | async-start | bytes 786432 | tf_op jit(solution)/shard_map/all_to_all | solution.py:898
  219.9 3.0 collective-permute-start.3
  233.7 5.8 %copy-start.11 = (bf16[768,1024]{1,0:T(8,128)(2,1)S(1)}, bf16[768,1024]{1,0:T(8,128)(2,1)}, u32[]{:S(2)}) copy-start(bf16[768,1024]{1,0:T(8,128)(2,1)} %get-tuple-element.54.refs_10_.refs_1_) | copy-start | bytes 4718596
  233.7 55.4 %all-to-all-start.5 = ((bf16[32,64,1024]{2,1,0:T(8,128)(2,1)}), bf16[32,64,1024]{2,1,0:T(8,128)(2,1)}, u32[]{:S(2)}, u32[]{:S(2)}) async-start(bf16[32,64,1024]{2,1,0:T(8,128)(2,1)} %shard_map.197), calls=%async_computation.5 | async-start | bytes 8388608 | tf_op jit(solution)/shard_map/all_to_all | solution.py:906
  239.4 9.4 %copy-start.9 = (bf16[32,96,128]{2,1,0:T(8,128)(2,1)S(1)}, bf16[32,96,128]{2,1,0:T(8,128)(2,1)}, u32[]{:S(2)}) copy-start(bf16[32,96,128]{2,1,0:T(8,128)(2,1)} %copy-done.8) | copy-start | bytes 2359300
  239.4 6.6 %collective-permute-start.4 = (bf16[768,1024]{1,0:T(8,128)(2,1)S(1)}, bf16[768,1024]{1,0:T(8,128)(2,1)S(1)}, u32[]{:S(2)}, u32[]{:S(2)}) collective-permute-start(bf16[768,1024]{1,0:T(8,128)(2,1)S(1)} %copy-done.11), channel_id=1, source_target_pairs={{0,32},{32,0},{1,33},{33,1},{2,34},{34,2},{3,35},{35,3},{4,36},{36... | collective-permute-start | bytes 4718600 | tf_op jit(solution)/shard_map/ppermute | solution.py:932
  248.1 15.0 %copy-start.10 = (bf16[768,1024]{1,0:T(8,128)(2,1)}, bf16[768,1024]{1,0:T(8,128)(2,1)S(1)}, u32[]{:S(2)}) copy-start(bf16[768,1024]{1,0:T(8,128)(2,1)S(1)} %add_convert_fusion.1.refs_0_) | copy-start | bytes 4718596
  248.1 49.0 %collective-permute-start.5 = (bf16[768,1024]{1,0:T(8,128)(2,1)S(1)}, bf16[768,1024]{1,0:T(8,128)(2,1)}, u32[]{:S(2)}, u32[]{:S(2)}) collective-permute-start(bf16[768,1024]{1,0:T(8,128)(2,1)S(1)} %add_convert_fusion.1.refs_0_), channel_id=1, source_target_pairs={{0,64},{64,0},{1,65},{65,1},{2,66},{66,2},{3,67},{67,3},{4,68},{68... | collective-permute-start | bytes 4718600 | tf_op jit(solution)/shard_map/ppermute | solution.py:959
  289.1 20.3 %all-to-all-start.6 = ((bf16[32,96,128]{2,1,0:T(8,128)(2,1)}), bf16[32,96,128]{2,1,0:T(8,128)(2,1)S(1)}, u32[]{:S(2)}, u32[]{:S(2)}) async-start(bf16[32,96,128]{2,1,0:T(8,128)(2,1)} %shard_map.200), calls=%async_computation.6 | async-start | bytes 1572864 | tf_op jit(solution)/shard_map/all_to_all | solution.py:898
  299.7 1.1 copy-start.4
  309.4 11.3 %copy-start.2 = (bf16[32,96,128]{2,1,0:T(8,128)(2,1)}, bf16[32,96,128]{2,1,0:T(8,128)(2,1)S(1)}, u32[]{:S(2)}) copy-start(bf16[32,96,128]{2,1,0:T(8,128)(2,1)S(1)} %all-to-all-done.6) | copy-start | bytes 2359300
  309.4 21.5 %all-to-all-start.7 = ((bf16[16,80,256]{2,1,0:T(8,128)(2,1)}), bf16[16,80,256]{2,1,0:T(8,128)(2,1)S(1)}, u32[]{:S(2)}, u32[]{:S(2)}) async-start(bf16[16,80,256]{2,1,0:T(8,128)(2,1)} %shard_map.206), calls=%async_computation.7 | async-start | bytes 1310720 | tf_op jit(solution)/shard_map/all_to_all | solution.py:976
  320.7 5.9 %collective-permute-start.6 = (bf16[16,1024]{1,0:T(8,128)(2,1)}, bf16[16,1024]{1,0:T(8,128)(2,1)S(1)}, u32[]{:S(2)}, u32[]{:S(2)}) collective-permute-start(bf16[16,1024]{1,0:T(8,128)(2,1)} %shard_map.207.refs_2_), channel_id=1, source_target_pairs={{0,64},{64,0},{1,65},{65,1},{2,66},{66,2},{3,67},{67,3},{4,68},{68... | collective-permute-start | bytes 98312 | tf_op jit(solution)/shard_map/ppermute | solution.py:969
  333.9 47.0 %all-to-all-start.8 = ((bf16[64,96,256]{2,1,0:T(8,128)(2,1)}), bf16[64,96,256]{2,1,0:T(8,128)(2,1)S(1)}, u32[]{:S(2)}, u32[]{:S(2)}) async-start(bf16[64,96,256]{2,1,0:T(8,128)(2,1)} %get-tuple-element.66), calls=%async_computation.8 | async-start | bytes 6291456 | tf_op jit(solution)/shard_map/all_to_all | solution.py:910
  341.9 4.1 %collective-permute-start.7 = (bf16[768,1024]{1,0:T(8,128)(2,1)}, bf16[768,1024]{1,0:T(8,128)(2,1)S(1)}, u32[]{:S(2)}, u32[]{:S(2)}) collective-permute-start(bf16[768,1024]{1,0:T(8,128)(2,1)} %copy-done.4), channel_id=1, source_target_pairs={{0,32},{32,0},{1,33},{33,1},{2,34},{34,2},{3,35},{35,3},{4,36},{36... | collective-permute-start | bytes 4718600 | tf_op jit(solution)/shard_map/ppermute | solution.py:932
  346.0 1.4 copy-start.5
  351.2 4.8 %copy-start.3 = (bf16[32,96,128]{2,1,0:T(8,128)(2,1)S(1)}, bf16[32,96,128]{2,1,0:T(8,128)(2,1)}, u32[]{:S(2)}) copy-start(bf16[32,96,128]{2,1,0:T(8,128)(2,1)} %copy-done.2) | copy-start | bytes 2359300
  380.9 1.6 copy-start
  382.6 9.4 %collective-permute-start.8 = (bf16[64,96,256]{2,1,0:T(8,128)(2,1)}, bf16[64,96,256]{2,1,0:T(8,128)(2,1)S(1)}, u32[]{:S(2)}, u32[]{:S(2)}) collective-permute-start(bf16[64,96,256]{2,1,0:T(8,128)(2,1)} %shard_map.210), channel_id=1, source_target_pairs={{0,32},{32,0},{1,33},{33,1},{2,34},{34,2},{3,35},{35,3},{4,36},{36... | collective-permute-start | bytes 9437192 | tf_op jit(solution)/shard_map/ppermute | solution.py:932
  385.1 1.9 copy-start.1
Sparse Core Ops, SparseCore 0:
  22.6 113.9 all-gather.4
  178.0 63.9 all-gather.6

commit v3 on v2

--- a/solution.py
+++ b/solution.py
@@ -100,6 +100,18 @@
     )(hold(x), *deps)
 
 
+def await_all(x, *deps):
+    any_space = pl.BlockSpec(memory_space=pl.ANY)
+    return pl.pallas_call(
+        lambda *refs: None,
+        in_specs=[any_space] * (1 + len(deps)),
+        out_specs=any_space,
+        out_shape=jax.ShapeDtypeStruct(x.shape, x.dtype),
+        input_output_aliases={0: 0},
+        compiler_params=pltpu.CompilerParams(vmem_limit_bytes=1024 * 1024),
+    )(x, *deps)
+
+
 def hold(x):
     return pltpu.with_memory_space_constraint(x, pltpu.HBM)
 
@@ -179,7 +191,7 @@
     )(blk, tok, gain, w_qkv, w_qkv, w_qkv, cos, sin)
 
 
-def plan_kernel(routes, gates, dz, pos_ref, gate_ref, out):
+def plan_kernel(routes, gates, pos_ref, gate_ref, out):
     named = jnp.concatenate([routes[0], routes[1]], 1).astype(F32)
     weights = jnp.concatenate([gates[0], gates[1]], 1)
     experts = lax.broadcasted_iota(jnp.int32, (32, 128), 0).astype(F32)
@@ -197,22 +209,41 @@
     gate_ref[...] = gate
     high = gate.astype(BF16).astype(F32)
     rest = gate - high
-    out[0:128, :] = dz[...]
     for j in range(8):
         part = slice(4 * j, 4 * j + 4)
         tile = jnp.concatenate([pos[part], high[part], rest[part], jnp.zeros((4, 128), F32)], 0)
-        out[128:144, j * 128 : (j + 1) * 128] = tile.astype(BF16)
-
-
-def plan(routes, gates, dz):
+        out[:, j * 128 : (j + 1) * 128] = tile.astype(BF16)
+
+
+def plan(routes, gates):
     return call(
         plan_kernel,
         (1,),
-        [whole(2, 8, 64), whole(2, 8, 64), whole(128, 1024)],
-        [whole(32, 128), whole(32, 128), whole(144, 1024)],
-        [sds((32, 128), jnp.int32), sds((32, 128), F32), sds((144, 1024), BF16)],
+        [whole(2, 8, 64), whole(2, 8, 64)],
+        [whole(32, 128), whole(32, 128), whole(16, 1024)],
+        [sds((32, 128), jnp.int32), sds((32, 128), F32), sds((16, 1024), BF16)],
+        moved=1 << 17,
+    )(routes, gates)
+
+
+def pack_kernel(dz, info, dz_far, info_far, out):
+    out[0, 0:128, :] = dz[...]
+    out[0, 128:144, :] = info[...]
+    out[1, 0:128, :] = dz_far[...]
+    out[1, 128:144, :] = info_far[...]
+
+
+def pack(dz, info, dz_far, info_far, deps):
+    return call(
+        pack_kernel,
+        (1,),
+        [whole(128, 1024), whole(16, 1024), whole(128, 1024), whole(16, 1024)],
+        whole(2, 144, 1024),
+        sds((2, 144, 1024), BF16),
         moved=1 << 20,
-    )(routes, gates, dz)
+        moving=(2, 3),
+        deps=deps,
+    )(dz, info, dz_far, info_far)
 
 
 def split_queries(q):
@@ -241,22 +272,14 @@
     for tile in range(4):
         q2 = split_queries(x_ref[tile * 8 : (tile + 1) * 8, 0:32, :].reshape(256, 128))
         limit = limits(tile, info)
-
-        def step(c, carry):
-            top, total, acc = carry
-            at = pl.ds(pl.multiple_of(c * 512, 512), 512)
-            s = dot(kv[at, :], q2, NT)
-            place = c * 512 + lax.broadcasted_iota(jnp.int32, (512, 1), 0)
-            s = jnp.where(place <= limit, s, -1e30)
-            new_top = jnp.maximum(top, jnp.max(s, axis=0, keepdims=True))
-            shrink = jnp.exp(top - new_top)
-            p = jnp.exp(s - new_top)
-            total = total * shrink + jnp.sum(p, axis=0, keepdims=True)
-            return new_top, total, acc * shrink + dot(kvt[64:128, at], p.astype(BF16))
-
-        start = (jnp.full((1, 512), -1e30, F32), jnp.zeros((1, 512), F32), jnp.zeros((64, 512), F32))
-        top, total, acc = lax.fori_loop(0, tile + 1, step, start)
-        out = acc / total
+        keys = (tile + 1) * 512
+        s = dot(kv[0:keys, :], q2, NT)
+        place = lax.broadcasted_iota(jnp.int32, (keys, 1), 0)
+        s = jnp.where(place <= limit, s, -1e30)
+        top = jnp.max(s, axis=0, keepdims=True)
+        p = jnp.exp(s - top)
+        total = jnp.sum(p, axis=0, keepdims=True)
+        out = dot(kvt[64:128, 0:keys], p.astype(BF16)) / total
         ot_ref[tile] = out
         lse_ref[tile] = jnp.broadcast_to(top + jnp.log(total), (8, 512))
         both = jnp.concatenate([out[:, :256], out[:, 256:]], 0).T
@@ -348,20 +371,21 @@
 
 
 def placement(pos):
-    slots = lax.broadcasted_iota(jnp.int32, (8, 48, 128), 1)
-    return (pos[...][:, None, :] == slots).reshape(384, 128)
+    shape = (pos.shape[0], 48, 128)
+    slots = lax.broadcasted_iota(jnp.int32, shape, 1)
+    return (pos[...][:, None, :] == slots).reshape(shape[0] * 48, 128)
 
 
 def gated(pos, gate):
     placed = placement(pos)
-    weight = jnp.broadcast_to(gate[...][:, None, :], (8, 48, 128)).reshape(384, 128)
-    weight = jnp.where(placed, weight, 0.0)
+    weight = jnp.broadcast_to(gate[...][:, None, :], (pos.shape[0], 48, 128))
+    weight = jnp.where(placed, weight.reshape(placed.shape), 0.0)
     high = weight.astype(BF16)
     return high, (weight - high.astype(F32)).astype(BF16)
 
 
-PLACE = pl.BlockSpec((8, 128), lambda e: (e, 0))
-SLOTS = pl.BlockSpec((8, 48, 1024), lambda e: (e, 0, 0))
+PLACE = pl.BlockSpec((16, 128), lambda e: (e, 0))
+SLOTS = pl.BlockSpec((16, 48, 1024), lambda e: (e, 0, 0))
 
 
 def mid_kernel(recv, w0, w1, w2, w3, tok, gain, pos, o_ref, y_ref, out, h2):
@@ -380,13 +404,13 @@
         h2[...] = (y * inverse * gain[...]).astype(BF16)
 
     placed = placement(pos).astype(F32).astype(BF16)
-    out[...] = dot(placed, h2[...]).astype(BF16).reshape(8, 48, 1024)
+    out[...] = dot(placed, h2[...]).astype(BF16).reshape(out.shape)
 
 
 def mid(recv, w_out, tok, gain, pos, deps):
     return call(
         mid_kernel,
-        (4,),
+        (2,),
         [
             whole(2, 8, 2, 32, 128),
             *[pl.BlockSpec((1024, 256), lambda e, j=j: (0, j)) for j in range(4)],
@@ -404,14 +428,12 @@
     )(recv, w_out, w_out, w_out, w_out, tok, gain, pos)
 
 
-def expert_kernel(
-    which, x_ref, info, dz, g0, g1, u0, u1, d0, d1, dx2, eo, da_ref, deo_ref, hid_ref
-):
+def expert_kernel(which, x_ref, info, dz, g0, g1, u0, u1, d0, d1, dx2, da_ref, deo_ref, hid_ref):
     slots = lax.broadcasted_iota(jnp.int32, (48, 128), 0).astype(F32)
     rows16 = lax.broadcasted_iota(jnp.int32, (16, 128), 0)
     blank = jnp.zeros((48, 128), F32)
     mine = which[0] % 4
-    for pair in range(4):
+    for pair in range(PLACES):
         parts, weights = [], []
         for j in range(2):
             tile = info[pair, j].astype(F32)
@@ -428,7 +450,6 @@
             first = pl.multiple_of(pair * 96 + (which[1] ^ j) * 48, 48)
             deo_ref[pl.ds(first, 48), :] = rows[j * 48 : (j + 1) * 48]
     x, deo = x_ref[...], deo_ref[...]
-    total = None
     for part, (wg, wu) in enumerate(((g0, u0), (g1, u1))):
         at = slice(part * 256, part * 256 + 256)
         late = slice(part * 256 + FF_EXP, part * 256 + FF_EXP + 256)
@@ -437,51 +458,58 @@
         sig = jax.nn.sigmoid(gate)
         act = gate * sig
         hid_ref[:, at] = (act * up).astype(BF16)
-        da_gate = (dhid * up * sig * (1.0 + gate * (1.0 - sig))).astype(BF16)
-        da_up = (dhid * act).astype(BF16)
-        da_ref[:, at] = da_gate
-        da_ref[:, late] = da_up
-        product = dot(da_gate, wg[...], NT) + dot(da_up, wu[...], NT)
-        total = product if total is None else total + product
+        da_ref[:, at] = (dhid * up * sig * (1.0 + gate * (1.0 - sig))).astype(BF16)
+        da_ref[:, late] = (dhid * act).astype(BF16)
+    total = dot(da_ref[:, 0:256], g0[...], NT) + dot(da_ref[:, 256:512], g1[...], NT)
+    total += dot(da_ref[:, 512:768], u0[...], NT) + dot(da_ref[:, 768:1024], u1[...], NT)
     dx2[...] = total.astype(BF16)
-    hid = hid_ref[...]
-    eo[:, 0:48, :512] = dot(hid, d0[...]).astype(BF16).reshape(8, 48, 512)
-    eo[:, 0:48, 512:] = dot(hid, d1[...]).astype(BF16).reshape(8, 48, 512)
+
+
+PLACES = 4
 
 
 def expert(which, x, dz_all, wgu, wdn, deps):
-    rows = pl.BlockSpec((384, 1024), lambda i, which: (i, 0))
+    count = PLACES * 96
+    rows = pl.BlockSpec((count, 1024), lambda i, which: (i, 0))
     return call(
         expert_kernel,
-        (4,),
+        (16 // PLACES,),
         [
             rows,
-            pl.BlockSpec((4, 2, 16, 128), lambda i, which: (i, 0, 8, which[0] // 4)),
-            pl.BlockSpec((4, 2, 128, 1024), lambda i, which: (i, 0, 0, 0)),
+            pl.BlockSpec((PLACES, 2, 16, 128), lambda i, which: (i, 0, 8, which[0] // 4)),
+            pl.BlockSpec((PLACES, 2, 128, 1024), lambda i, which: (i, 0, 0, 0)),
             *[pl.BlockSpec((1024, 256), lambda i, which, j=j: (0, j)) for j in range(4)],
             *[pl.BlockSpec((512, 512), lambda i, which, j=j: (0, j)) for j in range(2)],
         ],
-        [
-            rows,
-            pl.BlockSpec((8, 64, 1024), lambda i, which: (i, 0, 0)),
-            rows,
-            rows,
-            pl.BlockSpec((384, 512), lambda i, which: (i, 0)),
-        ],
-        [
-            sds((1536, 1024), BF16),
-            sds((32, 64, 1024), BF16),
-            sds((1536, 1024), BF16),
-            sds((1536, 1024), BF16),
-            sds((1536, 512), BF16),
-        ],
+        [rows, rows, rows, pl.BlockSpec((count, 512), lambda i, which: (i, 0))],
+        [*[sds((1536, 1024), BF16)] * 3, sds((1536, 512), BF16)],
         mb=32,
-        flops=2 * 1536 * 1024 * 3328,
-        moved=30 << 20,
+        flops=2 * 1536 * 1024 * 2816,
+        moved=26 << 20,
         scalars=1,
         moving=(1,),
         deps=deps,
     )(which, x, dz_all, dz_all, wgu, wgu, wgu, wgu, wdn, wdn)
+
+
+def expert_out_kernel(hid, d0, d1, eo):
+    eo[:, 0:48, :512] = dot(hid[...], d0[...]).astype(BF16).reshape(8, 48, 512)
+    eo[:, 0:48, 512:] = dot(hid[...], d1[...]).astype(BF16).reshape(8, 48, 512)
+
+
+def expert_out(hid, wdn):
+    return call(
+        expert_out_kernel,
+        (4,),
+        [
+            pl.BlockSpec((384, 512), lambda i: (i, 0)),
+            *[pl.BlockSpec((512, 512), lambda i, j=j: (0, j)) for j in range(2)],
+        ],
+        pl.BlockSpec((8, 64, 1024), lambda i: (i, 0, 0)),
+        sds((32, 64, 1024), BF16),
+        flops=2 * 1536 * 1024 * 512,
+        moved=7 << 20,
+    )(hid, wdn, wdn)
 
 
 def expert_grad_kernel(core, x_ref, da, hid, deo, own, other):
@@ -570,57 +598,49 @@
 
 
 def mid_back_kernel(
-    core, back, pos, y, gain, dz, w0, w1, w2, w3, dy_ref, own, other, send, acc
+    core, back, pos, y, gain, dz, w0, w1, w2, w3, dy_ref, own, other, send
 ):
-    @pl.when(pl.program_id(0) == 0)
+    placed = placement(pos).astype(F32).astype(BF16)
+    dh2 = dot(placed, back[...].reshape(1536, 1024), TN)
+    dv, scaled = norm_back(dh2, gain[...], y[...])
+    gains = jnp.sum(dh2 * scaled, axis=0, keepdims=True)
+    row = lax.broadcasted_iota(jnp.int32, (8, 128), 0)
+    tile = jnp.zeros((8, 128), F32)
+    for r in range(8):
+        tile = jnp.where(row == r, gains[:, r * 128 : (r + 1) * 128], tile)
+    high = tile.astype(BF16).astype(F32)
+    extra = jnp.concatenate([high, tile - high], 0).astype(BF16)
+    dy = dz[...].astype(F32) + dv
+    dy_ref[...] = dy
+    dbr = dy.astype(BF16)
+
+    @pl.when(core[0] == 0)
     def _():
-        acc[...] = jnp.zeros_like(acc)
-
-    placed = placement(pos).astype(F32).astype(BF16)
-    acc[...] += dot(placed, back[...].reshape(384, 1024), TN)
-
-    @pl.when(pl.program_id(0) == 3)
+        own[...] = dbr[:, :512]
+        other[...] = dbr[:, 512:]
+
+    @pl.when(core[0] == 1)
     def _():
-        dh2 = acc[...]
-        dv, scaled = norm_back(dh2, gain[...], y[...])
-        gains = jnp.sum(dh2 * scaled, axis=0, keepdims=True)
-        row = lax.broadcasted_iota(jnp.int32, (8, 128), 0)
-        tile = jnp.zeros((8, 128), F32)
-        for r in range(8):
-            tile = jnp.where(row == r, gains[:, r * 128 : (r + 1) * 128], tile)
-        high = tile.astype(BF16).astype(F32)
-        extra = jnp.concatenate([high, tile - high], 0).astype(BF16)
-        dy = dz[...].astype(F32) + dv
-        dy_ref[...] = dy
-        dbr = dy.astype(BF16)
-
-        @pl.when(core[0] == 0)
-        def _():
-            own[...] = dbr[:, :512]
-            other[...] = dbr[:, 512:]
-
-        @pl.when(core[0] == 1)
-        def _():
-            own[...] = dbr[:, 512:]
-            other[...] = dbr[:, :512]
-
-        do = jnp.concatenate([dot(dbr, w[...], NT) for w in (w0, w1, w2, w3)], 1).astype(BF16)
-        for s in range(2):
-            for half in range(2):
-                first = s * 64 + half * 32
-                for m in range(8):
-                    send[half, m, s, 0:32, :] = do[first : first + 32, m * 128 : (m + 1) * 128]
-                    send[half, m, s, 32:48, :] = extra
+        own[...] = dbr[:, 512:]
+        other[...] = dbr[:, :512]
+
+    do = jnp.concatenate([dot(dbr, w[...], NT) for w in (w0, w1, w2, w3)], 1).astype(BF16)
+    for s in range(2):
+        for half in range(2):
+            first = s * 64 + half * 32
+            for m in range(8):
+                send[half, m, s, 0:32, :] = do[first : first + 32, m * 128 : (m + 1) * 128]
+                send[half, m, s, 32:48, :] = extra
 
 
 def mid_back(core, back, pos, y, gain, dz, w_out, deps):
     return call(
         mid_back_kernel,
-        (4,),
+        (1,),
         [
             pl.BlockSpec(memory_space=pltpu.SMEM),
-            SLOTS,
-            PLACE,
+            whole(32, 48, 1024),
+            whole(32, 128),
             whole(128, 1024),
             whole(1, 1024),
             whole(128, 1024),
@@ -633,7 +653,6 @@
             sds((128, 512), BF16),
             sds((2, 8, 2, 48, 128), BF16),
         ],
-        [pltpu.VMEM((128, 1024), F32)],
         flops=2 * 128 * 1024 * 1024 + 2 * 1536 * 128 * 1024,
         moved=6 << 20,
         deps=deps,
@@ -641,35 +660,31 @@
     )(core, back, pos, y, gain, dz, w_out, w_out, w_out, w_out)
 
 
-def combine_kernel(back, pos, gate, y, out, acc):
-    @pl.when(pl.program_id(0) == 0)
-    def _():
-        acc[...] = y[...]
-
+def combine_kernel(back, pos, gate, y, out):
     high, rest = gated(pos, gate)
-    rows = back[...].reshape(384, 1024)
-    acc[...] += dot(high, rows, TN) + dot(rest, rows, TN)
-
-    @pl.when(pl.program_id(0) == 3)
-    def _():
-        out[...] = acc[...].astype(BF16)
+    rows = back[...].reshape(1536, 1024)
+    out[...] = (y[...] + dot(high, rows, TN) + dot(rest, rows, TN)).astype(BF16)
 
 
 def combine(back, pos, gate, y):
     return call(
         combine_kernel,
-        (4,),
-        [SLOTS, PLACE, PLACE, whole(128, 1024)],
+        (1,),
+        [
+            pl.BlockSpec((32, 48, 1024), lambda _: (0, 0, 0)),
+            whole(32, 128),
+            whole(32, 128),
+            whole(128, 1024),
+        ],
         whole(128, 1024),
         sds((128, 1024), BF16),
-        [pltpu.VMEM((128, 1024), F32)],
         flops=4 * 1536 * 128 * 1024,
         moved=4 << 20,
         moving=(0,),
     )(back, pos, gate, y)
 
 
-def last_kernel(recv, w_qkv, tok, gain, dy, grad_tokens, dproj):
+def last_kernel(recv, w0, w1, w2, w3, tok, gain, dy, grad_tokens, dproj):
     low = low_half((64, 128))
     for t in range(2):
         rows = slice(t * 64, t * 64 + 64)
@@ -686,7 +701,8 @@
             dv = jnp.where(low, pltpu.roll(both[0], HEAD, 1), both[1])
             dproj[rows, 1024 + mm * 128 : 1152 + mm * 128] = dk.astype(BF16)
             dproj[rows, 1536 + mm * 128 : 1664 + mm * 128] = dv.astype(BF16)
-    dh = dot(dproj[...], w_qkv[...], NT)
+    d = dproj[...]
+    dh = jnp.concatenate([dot(d, w[...], NT) for w in (w0, w1, w2, w3)], 1)
     dv, _ = norm_back(dh, gain[...], tok[...].astype(F32))
     grad_tokens[...] = dy[...] + dv
 
@@ -697,7 +713,7 @@
         (1,),
         [
             whole(2, 8, 2, 96, 128),
-            whole(1024, 2048),
+            *[pl.BlockSpec((256, 2048), lambda _, j=j: (j, 0)) for j in range(4)],
             whole(128, 1024),
             whole(1, 1024),
             whole(128, 1024),
@@ -709,7 +725,7 @@
         moved=6 << 20,
         deps=deps,
         moving=(0,),
-    )(recv, w_qkv, tok, gain, dy)
+    )(recv, w_qkv, w_qkv, w_qkv, w_qkv, tok, gain, dy)
 
 
 def qkv_grad_kernel(place, h_all, d_ref, gains, out, rows, acc):
@@ -800,11 +816,11 @@
 
 def add_pieces_kernel(which, qkv, out_w, out_w2, out, gains):
     total = jnp.sum(qkv[:, 0:64, :].astype(F32), axis=0).astype(BF16)
-    out[:, 0:64, :] = jnp.broadcast_to(total[None], (16, 64, 256))
+    out[:, 0:64, :] = jnp.broadcast_to(total[None], (32, 64, 256))
     other = (out_w[...].astype(F32) + out_w2[...].astype(F32)).astype(BF16)
     other = jnp.where(which[0] == 0, other[:, :512], other[:, 512:])
-    out[:, 64:80, :] = jnp.broadcast_to(other[None, :, :256], (16, 16, 256))
-    out[:, 80:96, :] = jnp.broadcast_to(other[None, :, 256:], (16, 16, 256))
+    out[:, 64:80, :] = jnp.broadcast_to(other[None, :, :256], (32, 16, 256))
+    out[:, 80:96, :] = jnp.broadcast_to(other[None, :, 256:], (32, 16, 256))
     parts = [qkv[row, 64:80, :].astype(F32)[:8] for row in (0, 4, 8, 12)]
     parts = [part[:, :128] + part[:, 128:] for part in parts]
     gains[...] = parts[0] + parts[1] + parts[2] + parts[3]
@@ -813,14 +829,14 @@
 def add_pieces(which, qkv, out_w, out_w2, deps):
     return call(
         add_pieces_kernel,
-        (4,),
+        (2,),
         [
             pl.BlockSpec(memory_space=pltpu.SMEM),
             whole(16, 80, 256),
             whole(16, 1024),
             whole(16, 1024),
         ],
-        [pl.BlockSpec((16, 96, 256), lambda i: (i, 0, 0)), whole(8, 128)],
+        [pl.BlockSpec((32, 96, 256), lambda i: (i, 0, 0)), whole(8, 128)],
         [sds((64, 96, 256), BF16), sds((8, 128), F32)],
         moved=5 << 20,
         moving=(1, 3),
@@ -931,12 +947,13 @@
     def to_partner(part):
         return lax.ppermute(part, "core", SWAP)
 
-    pos, gate, planned = plan(routes.transpose(0, 2, 1), gates.transpose(0, 2, 1), dz)
+    dz_far = lax.ppermute(dz, ("zl", "zh"), Z_PAIRS)
+    pos, gate, chosen = plan(routes.transpose(0, 2, 1), gates.transpose(0, 2, 1))
+    chosen_far = lax.ppermute(chosen, ("zl", "zh"), Z_PAIRS)
     h, send = pre(
-        blk.astype(jnp.int32).reshape(1), tok, gain_a, w_qkv, cos, sin, [hold(planned)]
+        blk.astype(jnp.int32).reshape(1), tok, gain_a, w_qkv, cos, sin, [hold(chosen)]
     )
-    planned_far = lax.ppermute(planned, ("zl", "zh"), Z_PAIRS)
-    planned = jnp.stack([after(planned, hold(send)), planned_far])
+    planned = pack(dz, chosen, dz_far, chosen_far, [hold(send)])
     dz_all = lax.all_gather(planned, PLANE).reshape(16, 2, 144, 1024)
     arrived = exchange(send.reshape(32, 96, 128))
     o_part, ot, lse = attend(info, arrived, [corner(planned)])
@@ -949,7 +966,7 @@
     o_other = to_partner(o)
     x = among_experts(rows).reshape(1536, 1024)
     place = jnp.stack([blk, zh]).astype(jnp.int32)
-    dx2, eo, da, deo, hid = expert(place, x, dz_all, wgu, wdn, [corner(o_other)])
+    dx2, da, deo, hid = expert(place, x, dz_all, wgu, wdn, [corner(o_other)])
     dx2_back = among_experts(dx2.reshape(32, 48, 1024))
     experts_own, experts_send = expert_grad(which, x, da, hid, deo)
     dy, dbr_own, dbr_send, do = mid_back(
@@ -957,34 +974,33 @@
     )
     experts_own = add_rounded(experts_own, to_partner(experts_send))
     experts_far = lax.ppermute(experts_own, "zl", SWAP)
-    h_near = after(h_near, hold(experts_send))
+    h_near = after(h_near, hold(da))
     h_all = lax.all_gather(h_near, PLANE).reshape(16, 2, 64, 1024)
 
 
     do_recv = exchange(do.reshape(32, 48, 128))
+    eo = expert_out(hid, wdn)
     eo = out_grad(o, o_other, dbr_own, to_partner(dbr_send), eo)
     eo_back = among_experts(after(eo, do_recv))
     mixed = combine(eo_back, pos, gate, y)
     out_part = out_sum(eo_back)
     out_far = lax.ppermute(out_part, "zl", SWAP)
     dqkv, gains = attend_back(info, arrived, do_recv, ot, lse, cos, sin, [])
-    experts_own = add_rounded(after(experts_own, hold(dqkv)), experts_far)
-
     place = jnp.stack([xh, zh]).astype(jnp.int32)
-    dqkv_recv = exchange(after(dqkv, eo_back)).reshape(2, 8, 2, 96, 128)
-    qkv_partial = after(qkv_grad(place, h_all, dqkv, gains), dqkv_recv, corner(experts_own))
+    qkv_partial = qkv_grad(place, h_all, dqkv, gains)
+    experts_own = add_rounded(after(experts_own, hold(qkv_partial)), experts_far)
+    qkv_partial = after(qkv_partial, eo_back, corner(experts_own))
     qkv_pieces = lax.all_to_all(qkv_partial, SAME_COLUMNS, 0, 0, tiled=True)
     experts_other = to_partner(experts_own)
     grad_gate_up, grad_down = final_expert(which, experts_own, experts_other)
-    copies, gains = add_pieces(
-        zl, qkv_pieces, out_part, out_far, []
-    )
-    grad_tokens = last(dqkv_recv, w_qkv, tok, gain_a, dy, [])
-    own = after(among_chips(copies), hold(mixed), hold(grad_gate_up), hold(grad_tokens))
+    copies, gains = add_pieces(zl, qkv_pieces, out_part, out_far, [])
+    own = await_all(among_chips(copies), hold(mixed), hold(grad_gate_up))
+    dqkv_recv = exchange(after(dqkv, corner(own))).reshape(2, 8, 2, 96, 128)
     rows = final(which, own, w_qkv, gain_attn.reshape(8, 128))
     grad_qkv, grad_out, grad_gain_attn = final(
         1 - which, to_partner(own), w_qkv, gain_attn.reshape(8, 128), (rows[2], rows[0], rows[1])
     )
+    grad_tokens = last(dqkv_recv, w_qkv, tok, gain_a, dy, [hold(grad_qkv)])
 
     return (
         mixed.reshape(2, 64, 1024),

time: 406 us -> 396 us (0.975)
  waiting for transfers between devices: 163 us -> 170 us
  starting transfers between devices: 96.7 us -> 89.9 us
  local copies, waits for them, and re-layouts: 12 us -> 5.37 us
    ppermute x1, waiting for transfers between devices: 0.01 us -> 14.8 us  [shards(): experts_far = lax.ppermute(experts_own, 'zl', SWAP)]
    all_to_all x1, waiting for transfers between devices: 20.1 us -> 30.6 us  [among_chips(): return lax.all_to_all(x, CHIPS, 0, 0, tiled=True)]
    all_to_all x3, waiting for transfers between devices: 96.8 us -> 86.8 us  [among_experts(): lax.all_to_all(x, CHIPS, 0, 0, tiled=True, axis_index_groups=EXPERT_GROUPS)]
    unnamed x29 -> x20, local copies, waits for them, and re-layouts: 10 us -> 3.11 us
    all_to_all x4, starting transfers between devices: 28.8 us -> 23.1 us  [exchange(): return lax.all_to_all(x, BLK, 0, 0, tiled=True)]
    ppermute x5, waiting for transfers between devices: 7.49 us -> 3.05 us  [to_partner(): return lax.ppermute(part, 'core', SWAP)]
    pallas_call x17 -> x19, Pallas kernels: 109 us -> 107 us  [call(): built(*[place(i, x) for i, x in enumerate(operands)], *deps)]
  transfers between devices with their start and end apart: 20 -> 21, of which waited for: 16 -> 15; matrix products, arithmetic and copies ran while one was open for 3% -> 2% of each run, Pallas kernels for 20% -> 21%
where the time goes in v3:
time: 396 us; the launch traced here: 394 us
  waiting for transfers between devices  170 us (43%)
  Pallas kernels  107 us (27%)
  starting transfers between devices  89.9 us (23%)
  between operations  14.3 us (4%)
  other arithmetic  7.15 us (2%)
  local copies, waits for them, and re-layouts  5.37 us (1%)
    pallas_call x19, Pallas kernels, call(): built(*[place(i, x) for i, x in enumerate(operands)], *deps)  107 us
    all_to_all x3, waiting for transfers between devices, among_experts(): lax.all_to_all(x, CHIPS, 0, 0, tiled=True, axis_index_groups=EXPERT_GROUPS)  86.8 us
    all_to_all x1, waiting for transfers between devices, among_chips(): return lax.all_to_all(x, CHIPS, 0, 0, tiled=True)  30.6 us
    all_to_all x3, starting transfers between devices, among_experts(): lax.all_to_all(x, CHIPS, 0, 0, tiled=True, axis_index_groups=EXPERT_GROUPS)  25.8 us
    all_to_all x4, starting transfers between devices, exchange(): return lax.all_to_all(x, BLK, 0, 0, tiled=True)  23.1 us
    all_to_all x4, waiting for transfers between devices, exchange(): return lax.all_to_all(x, BLK, 0, 0, tiled=True)  22.1 us
    ppermute x5, starting transfers between devices, to_partner(): return lax.ppermute(part, 'core', SWAP)  16.4 us
    ppermute x1, waiting for transfers between devices, shards(): experts_far = lax.ppermute(experts_own, 'zl', SWAP)  14.8 us
  transfers between devices with their start and end apart: 21, of which 15 were waited for; matrix products, arithmetic and copies ran while one was open for 2% of the time, Pallas kernels for 21%

profile of v3, /device:TPU:1, one launch (start us, length us, event | category | flops | bytes accessed | tf_op | source)
XLA Modules:
  0.0 393.7 jit_solution(3853888441329624452)
XLA Ops:
  7.2 4.7 %collective-permute-start = (bf16[128,1024]{1,0:T(8,128)(2,1)}, bf16[128,1024]{1,0:T(8,128)(2,1)S(1)}, u32[]{:S(2)}, u32[]{:S(2)}) collective-permute-start(bf16[128,1024]{1,0:T(8,128)(2,1)} %bitcast.59), channel_id=1, source_target_pairs={{0,65},{1,64},{64,1},{65,0},{2,67},{3,66},{66,3},{67,2},{4,69},{5,... | collective-permute-start | bytes 786440 | tf_op jit(solution)/shard_map/ppermute | solution.py:950
  13.4 5.2 %shard_map.189 = (bf16[128,1024]{1,0:T(8,128)(2,1)}, bf16[2,8,2,96,128]{4,3,2,1,0:T(8,128)(2,1)}) custom-call(s32[1]{0:T(128)} %bitcast.1.refs_0_, bf16[128,1024]{1,0:T(8,128)(2,1)} %bitcast.55, f32[1,1024]{1,0:T(1,128)} %bitcast.67, bf16[1024,2048]{1,0:T(8,128)(2,1)} %refs_4_.5, bf16[1024,2048]{1,0:T(8,128)(2,1)} %refs_4_.5, bf16[1024,2048]{1,0:T(8,128)(2,1)} %refs_4_.5, ...), custom_call_target="tpu_custom_call" | custom-call | flops 536870912 | bytes 5242880 | tf_op jit(solution)/shard_map/pallas_call | solution.py:88
  18.8 1.8 shard_map.190
  20.7 7.8 %all-to-all-start = ((bf16[32,96,128]{2,1,0:T(8,128)(2,1)}), bf16[32,96,128]{2,1,0:T(8,128)(2,1)S(1)}, u32[]{:S(2)}, u32[]{:S(2)}) async-start(bf16[32,96,128]{2,1,0:T(8,128)(2,1)} %bitcast.54), calls=%async_computation | async-start | bytes 1572864 | tf_op jit(solution)/shard_map/all_to_all | solution.py:914
  30.8 12.1 %all-to-all-done.refs_1_ = bf16[32,96,128]{2,1,0:T(8,128)(2,1)S(1)} async-done(((bf16[32,96,128]{2,1,0:T(8,128)(2,1)}), bf16[32,96,128]{2,1,0:T(8,128)(2,1)S(1)}, u32[]{:S(2)}, u32[]{:S(2)}) %all-to-all-start) | async-done | bytes 786464 | tf_op jit(solution)/shard_map/all_to_all | solution.py:914
  43.0 6.2 %shard_map.191 = (bf16[32,32,128]{2,1,0:T(8,128)(2,1)}, f32[4,64,512]{2,1,0:T(8,128)}, f32[4,8,512]{2,1,0:T(8,128)}) custom-call(s32[2]{0:T(128)S(1)} %pad_add_fusion.refs_0_, bf16[32,96,128]{2,1,0:T(8,128)(2,1)S(1)} %all-to-all-done.refs_1_, bf16[8,128]{1,0:T(8,128)(2,1)S(1)} %slice.29.refs_2_), custom_call_target="tpu_custom_call" | custom-call | flops 1342177280 | bytes 2097152 | tf_op jit(solution)/shard_map/pallas_call | solution.py:88
  49.1 5.3 %all-to-all-start.1 = ((bf16[32,32,128]{2,1,0:T(8,128)(2,1)}), bf16[32,32,128]{2,1,0:T(8,128)(2,1)S(1)}, u32[]{:S(2)}, u32[]{:S(2)}) async-start(bf16[32,32,128]{2,1,0:T(8,128)(2,1)} %get-tuple-element.43.refs_1_), calls=%async_computation.1 | async-start | bytes 524288 | tf_op jit(solution)/shard_map/all_to_all | solution.py:914
  55.1 2.7 collective-permute-start.2
  57.9 3.0 collective-permute-done.2
  60.9 3.1 all-to-all-done.1
  64.0 4.7 %shard_map.192 = (bf16[128,1024]{1,0:T(8,128)(2,1)}, f32[128,1024]{1,0:T(8,128)}, bf16[32,48,1024]{2,1,0:T(8,128)(2,1)}) custom-call(bf16[2,8,2,32,128]{4,3,2,1,0:T(8,128)(2,1)S(1)} %bitcast.45, bf16[1024,1024]{1,0:T(8,128)(2,1)} %refs_9_.1, bf16[1024,1024]{1,0:T(8,128)(2,1)} %refs_9_.1, bf16[1024,1024]{1,0:T(8,128)(2,1)} %refs_9_.1, ...), custom_call_target="tpu_custom_call" | custom-call | flops 671088640 | bytes 6291456 | tf_op jit(solution)/shard_map/pallas_call | solution.py:88
  68.7 7.6 %all-to-all-start.2 = ((bf16[32,48,1024]{2,1,0:T(8,128)(2,1)}), bf16[32,48,1024]{2,1,0:T(8,128)(2,1)S(1)}, u32[]{:S(2)}, u32[]{:S(2)}) async-start(bf16[32,48,1024]{2,1,0:T(8,128)(2,1)} %get-tuple-element.47), calls=%async_computation.2 | async-start | bytes 6291456 | tf_op jit(solution)/shard_map/all_to_all | solution.py:922
  76.3 9.4 %collective-permute-start.3 = (bf16[128,1024]{1,0:T(8,128)(2,1)}, bf16[128,1024]{1,0:T(8,128)(2,1)S(1)}, u32[]{:S(2)}, u32[]{:S(2)}) collective-permute-start(bf16[128,1024]{1,0:T(8,128)(2,1)} %get-tuple-element.46.refs_0_), channel_id=1, source_target_pairs={{0,32},{32,0},{1,33},{33,1},{2,34},{34,2},{3,35},{35,3},{4,36},{36... | collective-permute-start | bytes 786440 | tf_op jit(solution)/shard_map/ppermute | solution.py:948
  87.5 46.9 %all-to-all-done.2 = bf16[32,48,1024]{2,1,0:T(8,128)(2,1)S(1)} async-done(((bf16[32,48,1024]{2,1,0:T(8,128)(2,1)}), bf16[32,48,1024]{2,1,0:T(8,128)(2,1)S(1)}, u32[]{:S(2)}, u32[]{:S(2)}) %all-to-all-start.2) | async-done | bytes 3145760 | tf_op jit(solution)/shard_map/all_to_all | solution.py:922
  134.6 15.3 %shard_map.193 = (bf16[1536,1024]{1,0:T(8,128)(2,1)}, bf16[1536,1024]{1,0:T(8,128)(2,1)}, bf16[1536,1024]{1,0:T(8,128)(2,1)}, bf16[1536,512]{1,0:T(8,128)(2,1)}) custom-call(s32[2]{0:T(128)S(1)} %pad_add_fusion.1.refs_0_, bf16[1536,1024]{1,0:T(8,128)(2,1)S(1)} %bitcast.43, bf16[16,2,144,1024]{3,2,1,0:T(8,128)(2,1)} %bitcast.75, ...), custom_call_target="tpu_custom_call" | custom-call | flops 8858370048 | bytes 27262976 | tf_op jit(solution)/shard_map/pallas_call | solution.py:88
  150.0 9.8 %all-to-all-start.3 = ((bf16[32,48,1024]{2,1,0:T(8,128)(2,1)}), bf16[32,48,1024]{2,1,0:T(8,128)(2,1)S(1)}, u32[]{:S(2)}, u32[]{:S(2)}) async-start(bf16[32,48,1024]{2,1,0:T(8,128)(2,1)} %bitcast.53), calls=%async_computation.3 | async-start | bytes 6291456 | tf_op jit(solution)/shard_map/all_to_all | solution.py:922
  159.8 1.9 copy-done.3
  161.7 11.0 %shard_map.194 = (bf16[768,1024]{1,0:T(8,128)(2,1)}, bf16[768,1024]{1,0:T(8,128)(2,1)}) custom-call(s32[1]{0:T(128)} %bitcast.13.refs_0_, bf16[1536,1024]{1,0:T(8,128)(2,1)S(1)} %bitcast.44, bf16[1536,1024]{1,0:T(8,128)(2,1)} %get-tuple-element.50.refs_2_.refs_1_, bf16[1536,512]{1,0:T(8,128)(2,1)} %get-tuple-element.51.refs_3_.refs_0_, ...), custom_call_target="tpu_custom_call" | custom-call | flops 4831838208 | bytes 16777216 | tf_op jit(solution)/shard_map/pallas_call | solution.py:88
  172.7 31.6 %all-to-all-done.3.refs_1_ = bf16[32,48,1024]{2,1,0:T(8,128)(2,1)S(1)} async-done(((bf16[32,48,1024]{2,1,0:T(8,128)(2,1)}), bf16[32,48,1024]{2,1,0:T(8,128)(2,1)S(1)}, u32[]{:S(2)}, u32[]{:S(2)}) %all-to-all-start.3) | async-done | bytes 3145760 | tf_op jit(solution)/shard_map/all_to_all | solution.py:922
  204.3 4.2 %shard_map.195 = (f32[128,1024]{1,0:T(8,128)}, bf16[128,512]{1,0:T(8,128)(2,1)}, bf16[128,512]{1,0:T(8,128)(2,1)}, bf16[2,8,2,48,128]{4,3,2,1,0:T(8,128)(2,1)}) custom-call(s32[1]{0:T(128)} %bitcast.13.refs_0_, bf16[32,48,1024]{2,1,0:T(8,128)(2,1)S(1)} %all-to-all-done.3.refs_1_, s32[32,128]{1,0:T(8,128)} %get-tuple-element.44.refs_7_.refs_2_.refs_1_, ...), custom_call_target="tpu_custom_call" | custom-call | flops 671088640 | bytes 6291456 | tf_op jit(solution)/shard_map/pallas_call | solution.py:88
  208.5 4.2 %all-to-all-start.4 = ((bf16[32,48,128]{2,1,0:T(8,128)(2,1)}), bf16[32,48,128]{2,1,0:T(8,128)(2,1)S(1)}, u32[]{:S(2)}, u32[]{:S(2)}) async-start(bf16[32,48,128]{2,1,0:T(8,128)(2,1)} %bitcast.64), calls=%async_computation.4 | async-start | bytes 786432 | tf_op jit(solution)/shard_map/all_to_all | solution.py:914
  212.7 2.1 collective-permute-start.4
  214.8 5.4 %shard_map.196.refs_4_ = bf16[32,64,1024]{2,1,0:T(8,128)(2,1)} custom-call(bf16[1536,512]{1,0:T(8,128)(2,1)} %get-tuple-element.51.refs_3_.refs_0_, bf16[512,1024]{1,0:T(8,128)(2,1)} %bitcast.48, bf16[512,1024]{1,0:T(8,128)(2,1)} %bitcast.49), custom_call_target="tpu_custom_call" | custom-call | flops 1610612736 | bytes 7340032 | tf_op jit(solution)/shard_map/pallas_call | solution.py:88
  220.2 3.7 shard_map.197.refs_0_
  223.9 2.4 all-to-all-done.4.refs_1_.refs_2_
  226.4 8.4 %all-to-all-start.5 = ((bf16[32,64,1024]{2,1,0:T(8,128)(2,1)}), bf16[32,64,1024]{2,1,0:T(8,128)(2,1)}, u32[]{:S(2)}, u32[]{:S(2)}) async-start(bf16[32,64,1024]{2,1,0:T(8,128)(2,1)} %shard_map.198), calls=%async_computation.5 | async-start | bytes 8388608 | tf_op jit(solution)/shard_map/all_to_all | solution.py:922
  236.3 3.0 collective-permute-done.5
  239.4 2.1 add_convert_fusion.1.refs_0_
  242.3 14.3 %shard_map.200 = (bf16[32,96,128]{2,1,0:T(8,128)(2,1)}, f32[8,128]{1,0:T(8,128)}) custom-call(s32[2]{0:T(128)S(1)} %pad_add_fusion.refs_0_, bf16[32,96,128]{2,1,0:T(8,128)(2,1)S(1)} %copy-done.5, bf16[32,48,128]{2,1,0:T(8,128)(2,1)S(1)} %all-to-all-done.4.refs_1_.refs_2_, f32[4,64,512]{2,1,0:T(8,128)} %get-tuple-element.58.refs_3_, ...), custom_call_target="tpu_custom_call" | custom-call | flops 3355443200 | bytes 3145728 | tf_op jit(solution)/shard_map/pallas_call | solution.py:88
  256.6 5.8 %shard_map.203.refs_1_.refs_0_ = bf16[16,80,256]{2,1,0:T(8,128)(2,1)} custom-call(s32[2]{0:T(128)S(1)} %pad_add_fusion.2.refs_0_, bf16[16,2,64,1024]{3,2,1,0:T(8,128)(2,1)} %bitcast.50, bf16[32,96,128]{2,1,0:T(8,128)(2,1)} %get-tuple-element.60.refs_2_.refs_0_, f32[8,128]{1,0:T(8,128)} %get-tuple-element.61.refs_3_), custom_call_target="tpu_custom_call" | custom-call | flops 1073741824 | bytes 6291456 | tf_op jit(solution)/shard_map/pallas_call | solution.py:88
  262.4 14.8 %collective-permute-done.6 = bf16[768,1024]{1,0:T(8,128)(2,1)} collective-permute-done((bf16[768,1024]{1,0:T(8,128)(2,1)S(1)}, bf16[768,1024]{1,0:T(8,128)(2,1)}, u32[]{:S(2)}, u32[]{:S(2)}) %collective-permute-start.6) | collective-permute-done | bytes 1572896 | tf_op jit(solution)/shard_map/ppermute | solution.py:976
  277.3 2.5 add_convert_fusion.refs_1_
  281.0 8.3 %all-to-all-done.5.refs_0_.refs_1_ = bf16[32,64,1024]{2,1,0:T(8,128)(2,1)} async-done(((bf16[32,64,1024]{2,1,0:T(8,128)(2,1)}), bf16[32,64,1024]{2,1,0:T(8,128)(2,1)}, u32[]{:S(2)}, u32[]{:S(2)}) %all-to-all-start.5) | async-done | bytes 4194336 | tf_op jit(solution)/shard_map/all_to_all | solution.py:922
  289.3 8.4 %all-to-all-start.6 = ((bf16[16,80,256]{2,1,0:T(8,128)(2,1)}), bf16[16,80,256]{2,1,0:T(8,128)(2,1)S(1)}, u32[]{:S(2)}, u32[]{:S(2)}) async-start(bf16[16,80,256]{2,1,0:T(8,128)(2,1)} %shard_map.205), calls=%async_computation.6 | async-start | bytes 1310720 | tf_op jit(solution)/shard_map/all_to_all | solution.py:993
  297.7 2.0 shard_map.206.refs_2_
  301.1 4.5 %collective-permute-done.7.refs_3_ = bf16[16,1024]{1,0:T(8,128)(2,1)S(1)} collective-permute-done((bf16[16,1024]{1,0:T(8,128)(2,1)}, bf16[16,1024]{1,0:T(8,128)(2,1)S(1)}, u32[]{:S(2)}, u32[]{:S(2)}) %collective-permute-start.7) | collective-permute-done | bytes 32800 | tf_op jit(solution)/shard_map/ppermute | solution.py:987
  305.6 4.2 %all-to-all-done.6.refs_1_ = bf16[16,80,256]{2,1,0:T(8,128)(2,1)S(1)} async-done(((bf16[16,80,256]{2,1,0:T(8,128)(2,1)}), bf16[16,80,256]{2,1,0:T(8,128)(2,1)S(1)}, u32[]{:S(2)}, u32[]{:S(2)}) %all-to-all-start.6) | async-done | bytes 655392 | tf_op jit(solution)/shard_map/all_to_all | solution.py:993
  309.8 2.7 shard_map.207
  312.4 6.6 %all-to-all-start.7 = ((bf16[64,96,256]{2,1,0:T(8,128)(2,1)}), bf16[64,96,256]{2,1,0:T(8,128)(2,1)S(1)}, u32[]{:S(2)}, u32[]{:S(2)}) async-start(bf16[64,96,256]{2,1,0:T(8,128)(2,1)} %get-tuple-element.63), calls=%async_computation.7 | async-start | bytes 6291456 | tf_op jit(solution)/shard_map/all_to_all | solution.py:926
  319.8 3.8 shard_map.199.refs_1_
  323.6 3.9 shard_map.208
  327.5 30.6 %all-to-all-done.7.refs_0_ = bf16[64,96,256]{2,1,0:T(8,128)(2,1)S(1)} async-done(((bf16[64,96,256]{2,1,0:T(8,128)(2,1)}), bf16[64,96,256]{2,1,0:T(8,128)(2,1)S(1)}, u32[]{:S(2)}, u32[]{:S(2)}) %all-to-all-start.7) | async-done | bytes 3145760 | tf_op jit(solution)/shard_map/all_to_all | solution.py:926
  358.1 2.6 collective-permute-start.9
  360.6 5.8 %all-to-all-start.8 = ((bf16[32,96,128]{2,1,0:T(8,128)(2,1)}), bf16[32,96,128]{2,1,0:T(8,128)(2,1)}, u32[]{:S(2)}, u32[]{:S(2)}) async-start(bf16[32,96,128]{2,1,0:T(8,128)(2,1)} %shard_map.210), calls=%async_computation.8 | async-start | bytes 1572864 | tf_op jit(solution)/shard_map/all_to_all | solution.py:914
  366.4 5.0 %shard_map.211 = (f32[1024,2048]{1,0:T(8,128)}, f32[2,8,2,2,16,1024]{5,4,3,2,1,0:T(8,128)}, f32[8,128]{1,0:T(8,128)}) custom-call(s32[1]{0:T(128)} %bitcast.13.refs_0_, bf16[2,2,8,2,96,256]{5,4,3,2,1,0:T(8,128)(2,1)S(1)} %bitcast.42, bf16[1024,2048]{1,0:T(8,128)(2,1)} %refs_4_.5, f32[8,128]{1,0:T(8,128)} %bitcast.68), custom_call_target="tpu_custom_call" | custom-call | bytes 16777216 | tf_op jit(solution)/shard_map/pallas_call | solution.py:88
  371.4 6.0 %shard_map.212 = (f32[1024,2048]{1,0:T(8,128)}, f32[2,8,2,2,16,1024]{5,4,3,2,1,0:T(8,128)}, f32[8,128]{1,0:T(8,128)}) custom-call(s32[1]{0:T(128)S(6)} %sub.7.refs_0_, bf16[2,2,8,2,96,256]{5,4,3,2,1,0:T(8,128)(2,1)} %bitcast.29.refs_1_, bf16[1024,2048]{1,0:T(8,128)(2,1)} %refs_4_.5, ...), custom_call_target="tpu_custom_call", output_to_operand_aliasing={{0}: (5, {}), {1}: (6, {})} | custom-call | bytes 16777216 | tf_op jit(solution)/shard_map/pallas_call | solution.py:88
  377.4 4.4 %all-to-all-done.8 = bf16[32,96,128]{2,1,0:T(8,128)(2,1)} async-done(((bf16[32,96,128]{2,1,0:T(8,128)(2,1)}), bf16[32,96,128]{2,1,0:T(8,128)(2,1)}, u32[]{:S(2)}, u32[]{:S(2)}) %all-to-all-start.8) | async-done | bytes 786464 | tf_op jit(solution)/shard_map/all_to_all | solution.py:914
  381.8 5.1 %shard_map.213 = f32[128,1024]{1,0:T(8,128)} custom-call(bf16[2,8,2,96,128]{4,3,2,1,0:T(8,128)(2,1)} %bitcast.28.refs_0_, bf16[1024,2048]{1,0:T(8,128)(2,1)} %refs_4_.5, bf16[1024,2048]{1,0:T(8,128)(2,1)} %refs_4_.5, bf16[1024,2048]{1,0:T(8,128)(2,1)} %refs_4_.5, bf16[1024,2048]{1,0:T(8,128)(2,1)} %refs_4_.5, bf16[128,1024]{1,0:T(8,128)(2,1)} %bitcast.57, ...), custom_call_target="tpu_custom_call" | custom-call | flops 536870912 | bytes 6291456 | tf_op jit(solution)/shard_map/pallas_call | solution.py:88
  (57 shorter events, 12.6 us)
Async XLA Ops:
  7.2 127.4 %all-gather.5.cloned.1.call-start = ((), (), s32[]{:S(2)}) async-start(), calls=%async_computation.9 | async-start | bytes 10027008 | tf_op jit(solution)/shard_map/all_gather | solution.py:957
  7.2 11.6 %collective-permute-start = (bf16[128,1024]{1,0:T(8,128)(2,1)}, bf16[128,1024]{1,0:T(8,128)(2,1)S(1)}, u32[]{:S(2)}, u32[]{:S(2)}) collective-permute-start(bf16[128,1024]{1,0:T(8,128)(2,1)} %bitcast.59), channel_id=1, source_target_pairs={{0,65},{1,64},{64,1},{65,0},{2,67},{3,66},{66,3},{67,2},{4,69},{5,... | collective-permute-start | bytes 786440 | tf_op jit(solution)/shard_map/ppermute | solution.py:950
  13.4 5.4 %collective-permute-start.1 = (bf16[16,1024]{1,0:T(8,128)(2,1)}, bf16[16,1024]{1,0:T(8,128)(2,1)S(1)}, u32[]{:S(2)}, u32[]{:S(2)}) collective-permute-start(bf16[16,1024]{1,0:T(8,128)(2,1)} %get-tuple-element.41.refs_8_.refs_1_), channel_id=1, source_target_pairs={{0,65},{1,64},{64,1},{65,0},{2,67},{3,66},{66,3},{67,2},{4,69},{5,... | collective-permute-start | bytes 98312 | tf_op jit(solution)/shard_map/ppermute | solution.py:952
  18.6 9.9 %copy-start.9 = (s32[2]{0:T(128)S(1)}, s32[2]{0:T(128)}, u32[]{:S(2)}) copy-start(s32[2]{0:T(128)} %param.14) | copy-start | bytes 28
  20.7 22.3 %all-to-all-start = ((bf16[32,96,128]{2,1,0:T(8,128)(2,1)}), bf16[32,96,128]{2,1,0:T(8,128)(2,1)S(1)}, u32[]{:S(2)}, u32[]{:S(2)}) async-start(bf16[32,96,128]{2,1,0:T(8,128)(2,1)} %bitcast.54), calls=%async_computation | async-start | bytes 1572864 | tf_op jit(solution)/shard_map/all_to_all | solution.py:914
  28.5 26.0 %copy-start.8 = (bf16[128,1024]{1,0:T(8,128)(2,1)S(1)}, bf16[128,1024]{1,0:T(8,128)(2,1)}, u32[]{:S(2)}) copy-start(bf16[128,1024]{1,0:T(8,128)(2,1)} %get-tuple-element.45) | copy-start | bytes 786436
  43.0 6.2 %copy-start.4 = (bf16[32,96,128]{2,1,0:T(8,128)(2,1)}, bf16[32,96,128]{2,1,0:T(8,128)(2,1)S(1)}, u32[]{:S(2)}) copy-start(bf16[32,96,128]{2,1,0:T(8,128)(2,1)S(1)} %all-to-all-done.refs_1_) | copy-start | bytes 2359300
  49.1 14.8 %all-to-all-start.1 = ((bf16[32,32,128]{2,1,0:T(8,128)(2,1)}), bf16[32,32,128]{2,1,0:T(8,128)(2,1)S(1)}, u32[]{:S(2)}, u32[]{:S(2)}) async-start(bf16[32,32,128]{2,1,0:T(8,128)(2,1)} %get-tuple-element.43.refs_1_), calls=%async_computation.1 | async-start | bytes 524288 | tf_op jit(solution)/shard_map/all_to_all | solution.py:914
  55.1 5.8 %collective-permute-start.2 = (bf16[64,1024]{1,0:T(8,128)(2,1)S(1)}, bf16[64,1024]{1,0:T(8,128)(2,1)S(1)}, u32[]{:S(2)}, u32[]{:S(2)}) collective-permute-start(bf16[64,1024]{1,0:T(8,128)(2,1)S(1)} %get-tuple-element.75), channel_id=1, source_target_pairs={{0,1},{1,0},{2,3},{3,2},{4,5},{5,4},{6,7},{7,6},{8,9},{9,8},{10,11... | collective-permute-start | bytes 393224 | tf_op jit(solution)/shard_map/ppermute | solution.py:962
  68.7 65.8 %all-to-all-start.2 = ((bf16[32,48,1024]{2,1,0:T(8,128)(2,1)}), bf16[32,48,1024]{2,1,0:T(8,128)(2,1)S(1)}, u32[]{:S(2)}, u32[]{:S(2)}) async-start(bf16[32,48,1024]{2,1,0:T(8,128)(2,1)} %get-tuple-element.47), calls=%async_computation.2 | async-start | bytes 6291456 | tf_op jit(solution)/shard_map/all_to_all | solution.py:922
  76.3 180.3 %all-gather.7.cloned.1.call-start = ((), (), s32[]{:S(2)}) async-start(), calls=%async_computation.10 | async-start | bytes 4456448 | tf_op jit(solution)/shard_map/all_gather | solution.py:978
  76.3 11.1 %collective-permute-start.3 = (bf16[128,1024]{1,0:T(8,128)(2,1)}, bf16[128,1024]{1,0:T(8,128)(2,1)S(1)}, u32[]{:S(2)}, u32[]{:S(2)}) collective-permute-start(bf16[128,1024]{1,0:T(8,128)(2,1)} %get-tuple-element.46.refs_0_), channel_id=1, source_target_pairs={{0,32},{32,0},{1,33},{33,1},{2,34},{34,2},{3,35},{35,3},{4,36},{36... | collective-permute-start | bytes 786440 | tf_op jit(solution)/shard_map/ppermute | solution.py:948
  134.4 15.5 %copy-start.2 = (bf16[32,48,1024]{2,1,0:T(8,128)(2,1)}, bf16[32,48,1024]{2,1,0:T(8,128)(2,1)S(1)}, u32[]{:S(2)}) copy-start(bf16[32,48,1024]{2,1,0:T(8,128)(2,1)S(1)} %all-to-all-done.2) | copy-start | bytes 9437188
  150.0 54.3 %all-to-all-start.3 = ((bf16[32,48,1024]{2,1,0:T(8,128)(2,1)}), bf16[32,48,1024]{2,1,0:T(8,128)(2,1)S(1)}, u32[]{:S(2)}, u32[]{:S(2)}) async-start(bf16[32,48,1024]{2,1,0:T(8,128)(2,1)} %bitcast.53), calls=%async_computation.3 | async-start | bytes 6291456 | tf_op jit(solution)/shard_map/all_to_all | solution.py:922
  159.8 1.9 copy-start.3
  208.5 17.8 %all-to-all-start.4 = ((bf16[32,48,128]{2,1,0:T(8,128)(2,1)}), bf16[32,48,128]{2,1,0:T(8,128)(2,1)S(1)}, u32[]{:S(2)}, u32[]{:S(2)}) async-start(bf16[32,48,128]{2,1,0:T(8,128)(2,1)} %bitcast.64), calls=%async_computation.4 | async-start | bytes 786432 | tf_op jit(solution)/shard_map/all_to_all | solution.py:914
  212.7 7.5 %collective-permute-start.4 = (bf16[128,512]{1,0:T(8,128)(2,1)}, bf16[128,512]{1,0:T(8,128)(2,1)S(1)}, u32[]{:S(2)}, u32[]{:S(2)}) collective-permute-start(bf16[128,512]{1,0:T(8,128)(2,1)} %get-tuple-element.55), channel_id=1, source_target_pairs={{0,32},{32,0},{1,33},{33,1},{2,34},{34,2},{3,35},{35,3},{4,36},{36... | collective-permute-start | bytes 393224 | tf_op jit(solution)/shard_map/ppermute | solution.py:948
  226.4 8.4 %copy-start.7 = (bf16[768,1024]{1,0:T(8,128)(2,1)S(1)}, bf16[768,1024]{1,0:T(8,128)(2,1)}, u32[]{:S(2)}) copy-start(bf16[768,1024]{1,0:T(8,128)(2,1)} %get-tuple-element.53.refs_10_) | copy-start | bytes 4718596
  226.4 62.9 %all-to-all-start.5 = ((bf16[32,64,1024]{2,1,0:T(8,128)(2,1)}), bf16[32,64,1024]{2,1,0:T(8,128)(2,1)}, u32[]{:S(2)}, u32[]{:S(2)}) async-start(bf16[32,64,1024]{2,1,0:T(8,128)(2,1)} %shard_map.198), calls=%async_computation.5 | async-start | bytes 8388608 | tf_op jit(solution)/shard_map/all_to_all | solution.py:922
  234.8 7.5 %copy-start.5 = (bf16[32,96,128]{2,1,0:T(8,128)(2,1)S(1)}, bf16[32,96,128]{2,1,0:T(8,128)(2,1)}, u32[]{:S(2)}) copy-start(bf16[32,96,128]{2,1,0:T(8,128)(2,1)} %copy-done.4) | copy-start | bytes 2359300
  234.8 4.6 %collective-permute-start.5 = (bf16[768,1024]{1,0:T(8,128)(2,1)S(1)}, bf16[768,1024]{1,0:T(8,128)(2,1)S(1)}, u32[]{:S(2)}, u32[]{:S(2)}) collective-permute-start(bf16[768,1024]{1,0:T(8,128)(2,1)S(1)} %copy-done.7), channel_id=1, source_target_pairs={{0,32},{32,0},{1,33},{33,1},{2,34},{34,2},{3,35},{35,3},{4,36},{36... | collective-permute-start | bytes 4718600 | tf_op jit(solution)/shard_map/ppermute | solution.py:948
  241.5 15.1 %copy-start.6 = (bf16[768,1024]{1,0:T(8,128)(2,1)}, bf16[768,1024]{1,0:T(8,128)(2,1)S(1)}, u32[]{:S(2)}) copy-start(bf16[768,1024]{1,0:T(8,128)(2,1)S(1)} %add_convert_fusion.1.refs_0_) | copy-start | bytes 4718596
  241.5 35.8 %collective-permute-start.6 = (bf16[768,1024]{1,0:T(8,128)(2,1)S(1)}, bf16[768,1024]{1,0:T(8,128)(2,1)}, u32[]{:S(2)}, u32[]{:S(2)}) collective-permute-start(bf16[768,1024]{1,0:T(8,128)(2,1)S(1)} %add_convert_fusion.1.refs_0_), channel_id=1, source_target_pairs={{0,64},{64,0},{1,65},{65,1},{2,66},{66,2},{3,67},{67,3},{4,68},{68... | collective-permute-start | bytes 4718600 | tf_op jit(solution)/shard_map/ppermute | solution.py:976
  279.8 1.1 copy-start
  289.3 20.5 %all-to-all-start.6 = ((bf16[16,80,256]{2,1,0:T(8,128)(2,1)}), bf16[16,80,256]{2,1,0:T(8,128)(2,1)S(1)}, u32[]{:S(2)}, u32[]{:S(2)}) async-start(bf16[16,80,256]{2,1,0:T(8,128)(2,1)} %shard_map.205), calls=%async_computation.6 | async-start | bytes 1310720 | tf_op jit(solution)/shard_map/all_to_all | solution.py:993
  299.7 5.9 %collective-permute-start.7 = (bf16[16,1024]{1,0:T(8,128)(2,1)}, bf16[16,1024]{1,0:T(8,128)(2,1)S(1)}, u32[]{:S(2)}, u32[]{:S(2)}) collective-permute-start(bf16[16,1024]{1,0:T(8,128)(2,1)} %shard_map.206.refs_2_), channel_id=1, source_target_pairs={{0,64},{64,0},{1,65},{65,1},{2,66},{66,2},{3,67},{67,3},{4,68},{68... | collective-permute-start | bytes 98312 | tf_op jit(solution)/shard_map/ppermute | solution.py:987
  312.4 45.6 %all-to-all-start.7 = ((bf16[64,96,256]{2,1,0:T(8,128)(2,1)}), bf16[64,96,256]{2,1,0:T(8,128)(2,1)S(1)}, u32[]{:S(2)}, u32[]{:S(2)}) async-start(bf16[64,96,256]{2,1,0:T(8,128)(2,1)} %get-tuple-element.63), calls=%async_computation.7 | async-start | bytes 6291456 | tf_op jit(solution)/shard_map/all_to_all | solution.py:926
  319.0 4.6 %copy-start.1 = (bf16[768,1024]{1,0:T(8,128)(2,1)S(1)}, bf16[768,1024]{1,0:T(8,128)(2,1)}, u32[]{:S(2)}) copy-start(bf16[768,1024]{1,0:T(8,128)(2,1)} %copy-done) | copy-start | bytes 4718596
  319.0 4.6 %collective-permute-start.8 = (bf16[768,1024]{1,0:T(8,128)(2,1)}, bf16[768,1024]{1,0:T(8,128)(2,1)S(1)}, u32[]{:S(2)}, u32[]{:S(2)}) collective-permute-start(bf16[768,1024]{1,0:T(8,128)(2,1)} %copy-done), channel_id=1, source_target_pairs={{0,32},{32,0},{1,33},{33,1},{2,34},{34,2},{3,35},{35,3},{4,36},{36... | collective-permute-start | bytes 4718600 | tf_op jit(solution)/shard_map/ppermute | solution.py:948
  358.1 13.3 %collective-permute-start.9 = (bf16[64,96,256]{2,1,0:T(8,128)(2,1)S(1)}, bf16[64,96,256]{2,1,0:T(8,128)(2,1)}, u32[]{:S(2)}, u32[]{:S(2)}) collective-permute-start(bf16[64,96,256]{2,1,0:T(8,128)(2,1)S(1)} %shard_map.209), channel_id=1, source_target_pairs={{0,32},{32,0},{1,33},{33,1},{2,34},{34,2},{3,35},{35,3},{4,36},{36... | collective-permute-start | bytes 9437192 | tf_op jit(solution)/shard_map/ppermute | solution.py:948
  360.6 21.2 %all-to-all-start.8 = ((bf16[32,96,128]{2,1,0:T(8,128)(2,1)}), bf16[32,96,128]{2,1,0:T(8,128)(2,1)}, u32[]{:S(2)}, u32[]{:S(2)}) async-start(bf16[32,96,128]{2,1,0:T(8,128)(2,1)} %shard_map.210), calls=%async_computation.8 | async-start | bytes 1572864 | tf_op jit(solution)/shard_map/all_to_all | solution.py:914
Sparse Core Ops, SparseCore 0:
  20.8 113.7 all-gather.4
  150.1 83.3 all-gather.6

commit v4 on v3

--- a/solution.py
+++ b/solution.py
@@ -492,24 +492,41 @@
     )(which, x, dz_all, dz_all, wgu, wgu, wgu, wgu, wdn, wdn)
 
 
-def expert_out_kernel(hid, d0, d1, eo):
-    eo[:, 0:48, :512] = dot(hid[...], d0[...]).astype(BF16).reshape(8, 48, 512)
-    eo[:, 0:48, 512:] = dot(hid[...], d1[...]).astype(BF16).reshape(8, 48, 512)
-
-
-def expert_out(hid, wdn):
+def expert_out_kernel(which, info, hid, d0, d1, out):
+    slots = lax.broadcasted_iota(jnp.int32, (48, 128), 0).astype(F32)
+    rows16 = lax.broadcasted_iota(jnp.int32, (16, 128), 0)
+    mine = which[0] % 4
+    eo = jnp.concatenate([dot(hid[...], d0[...]), dot(hid[...], d1[...])], 1).astype(BF16)
+    for place in range(4):
+        for zh in range(2):
+            tile = info[place, which[1] ^ zh].astype(F32)
+
+            def pick(k):
+                return jnp.sum(jnp.where(rows16 == mine + 4 * k, tile, 0.0), axis=0, keepdims=True)
+
+            hot = jnp.where(slots == pick(0), 1.0, 0.0)
+            gate = jnp.concatenate([hot * pick(1), hot * pick(2)], 0).astype(BF16)
+            first = place * 96 + zh * 48
+            rows = eo[first : first + 48]
+            product = dot(gate, jnp.concatenate([rows, rows], 0), TN)
+            out[place, which[1] ^ zh] = product.astype(BF16)
+
+
+def expert_out(which, dz_all, hid, wdn):
     return call(
         expert_out_kernel,
         (4,),
         [
-            pl.BlockSpec((384, 512), lambda i: (i, 0)),
-            *[pl.BlockSpec((512, 512), lambda i, j=j: (0, j)) for j in range(2)],
-        ],
-        pl.BlockSpec((8, 64, 1024), lambda i: (i, 0, 0)),
-        sds((32, 64, 1024), BF16),
-        flops=2 * 1536 * 1024 * 512,
-        moved=7 << 20,
-    )(hid, wdn, wdn)
+            pl.BlockSpec((4, 2, 16, 128), lambda i, which: (i, 0, 8, which[0] // 4)),
+            pl.BlockSpec((384, 512), lambda i, which: (i, 0)),
+            *[pl.BlockSpec((512, 512), lambda i, which, j=j: (0, j)) for j in range(2)],
+        ],
+        pl.BlockSpec((4, 2, 128, 1024), lambda i, which: (i, 0, 0, 0)),
+        sds((16, 2, 128, 1024), BF16),
+        flops=2 * 1536 * 1024 * 512 + 4 * 1536 * 128 * 1024,
+        moved=12 << 20,
+        scalars=1,
+    )(which, dz_all, hid, wdn, wdn)
 
 
 def expert_grad_kernel(core, x_ref, da, hid, deo, own, other):
@@ -660,31 +677,10 @@
     )(core, back, pos, y, gain, dz, w_out, w_out, w_out, w_out)
 
 
-def combine_kernel(back, pos, gate, y, out):
-    high, rest = gated(pos, gate)
-    rows = back[...].reshape(1536, 1024)
-    out[...] = (y[...] + dot(high, rows, TN) + dot(rest, rows, TN)).astype(BF16)
-
-
-def combine(back, pos, gate, y):
-    return call(
-        combine_kernel,
-        (1,),
-        [
-            pl.BlockSpec((32, 48, 1024), lambda _: (0, 0, 0)),
-            whole(32, 128),
-            whole(32, 128),
-            whole(128, 1024),
-        ],
-        whole(128, 1024),
-        sds((128, 1024), BF16),
-        flops=4 * 1536 * 128 * 1024,
-        moved=4 << 20,
-        moving=(0,),
-    )(back, pos, gate, y)
-
-
-def last_kernel(recv, w0, w1, w2, w3, tok, gain, dy, grad_tokens, dproj):
+def last_kernel(
+    recv, w0, w1, w2, w3, tok, gain, dy, y, near, far, grad_tokens, mixed, dproj
+):
+    mixed[...] = (y[...] + near[0].astype(F32) + far[...].astype(F32)).astype(BF16)
     low = low_half((64, 128))
     for t in range(2):
         rows = slice(t * 64, t * 64 + 64)
@@ -707,7 +703,7 @@
     grad_tokens[...] = dy[...] + dv
 
 
-def last(recv, w_qkv, tok, gain, dy, deps):
+def last(recv, w_qkv, tok, gain, dy, y, sums, far, deps):
     return call(
         last_kernel,
         (1,),
@@ -717,15 +713,18 @@
             whole(128, 1024),
             whole(1, 1024),
             whole(128, 1024),
-        ],
-        whole(128, 1024),
-        sds((128, 1024), F32),
+            whole(128, 1024),
+            pl.BlockSpec((1, 128, 1024), lambda _: (0, 0, 0)),
+            whole(128, 1024),
+        ],
+        [whole(128, 1024), whole(128, 1024)],
+        [sds((128, 1024), F32), sds((128, 1024), BF16)],
         [pltpu.VMEM((128, 2048), BF16)],
         flops=2 * 128 * 1024 * 2048,
         moved=6 << 20,
         deps=deps,
-        moving=(0,),
-    )(recv, w_qkv, w_qkv, w_qkv, w_qkv, tok, gain, dy)
+        moving=(0, 9, 10),
+    )(recv, w_qkv, w_qkv, w_qkv, w_qkv, tok, gain, dy, y, sums, far)
 
 
 def qkv_grad_kernel(place, h_all, d_ref, gains, out, rows, acc):
@@ -775,50 +774,30 @@
     )(place, h_all, dqkv, gains)
 
 
-def out_grad_kernel(left, left2, right, right2, _, out):
+def out_grad_kernel(left, left2, right, right2, out):
     a = jnp.concatenate([left[...], left2[...]], 0)
     b = jnp.concatenate([right[...], right2[...]], 0)
-    product = dot(a, b, TN).astype(BF16).reshape(8, 2, 16, 512)
-    out[:, :, :512] = product[:, 0]
-    out[:, :, 512:] = product[:, 1]
-
-
-def out_grad(left, left2, right, right2, eo):
+    out[...] = dot(a, b, TN).astype(BF16)
+
+
+def out_grad(left, left2, right, right2):
     thin = pl.BlockSpec((128, 256), lambda i: (0, i))
     return call(
         out_grad_kernel,
         (4,),
-        [thin, thin, whole(128, 512), whole(128, 512), pl.BlockSpec(memory_space=pl.ANY)],
-        pl.BlockSpec((8, 16, 1024), lambda i: (i, 3, 0)),
-        sds((32, 64, 1024), BF16),
+        [thin, thin, whole(128, 512), whole(128, 512)],
+        pl.BlockSpec((256, 512), lambda i: (i, 0)),
+        sds((1024, 512), BF16),
         flops=2 * 256 * 1024 * 512,
         moved=3 << 20,
-        aliases={4: 0},
         moving=(1, 3),
-    )(left, left2, right, right2, eo)
-
-
-def out_sum_kernel(pieces, out):
-    out[...] = jnp.sum(pieces[...].astype(F32), axis=0).astype(BF16)
-
-
-def out_sum(pieces):
-    return call(
-        out_sum_kernel,
-        (1,),
-        [pl.BlockSpec((32, 16, 1024), lambda i: (0, 3, 0))],
-        whole(16, 1024),
-        sds((16, 1024), BF16),
-        moved=1 << 20,
-        moving=(0,),
-    )(pieces)
-
-
-def add_pieces_kernel(which, qkv, out_w, out_w2, out, gains):
+    )(left, left2, right, right2)
+
+
+def add_pieces_kernel(qkv, out_w, out, gains):
     total = jnp.sum(qkv[:, 0:64, :].astype(F32), axis=0).astype(BF16)
     out[:, 0:64, :] = jnp.broadcast_to(total[None], (32, 64, 256))
-    other = (out_w[...].astype(F32) + out_w2[...].astype(F32)).astype(BF16)
-    other = jnp.where(which[0] == 0, other[:, :512], other[:, 512:])
+    other = jnp.sum(out_w[...].astype(F32), axis=0).astype(BF16)
     out[:, 64:80, :] = jnp.broadcast_to(other[None, :, :256], (32, 16, 256))
     out[:, 80:96, :] = jnp.broadcast_to(other[None, :, 256:], (32, 16, 256))
     parts = [qkv[row, 64:80, :].astype(F32)[:8] for row in (0, 4, 8, 12)]
@@ -826,22 +805,17 @@
     gains[...] = parts[0] + parts[1] + parts[2] + parts[3]
 
 
-def add_pieces(which, qkv, out_w, out_w2, deps):
+def add_pieces(qkv, out_w, deps):
     return call(
         add_pieces_kernel,
         (2,),
-        [
-            pl.BlockSpec(memory_space=pltpu.SMEM),
-            whole(16, 80, 256),
-            whole(16, 1024),
-            whole(16, 1024),
-        ],
+        [whole(16, 80, 256), whole(64, 16, 512)],
         [pl.BlockSpec((32, 96, 256), lambda i: (i, 0, 0)), whole(8, 128)],
         [sds((64, 96, 256), BF16), sds((8, 128), F32)],
         moved=5 << 20,
-        moving=(1, 3),
+        moving=(0, 1),
         deps=deps,
-    )(which, qkv, out_w, out_w2)
+    )(qkv, out_w)
 
 
 def row_sums(product):
@@ -868,8 +842,8 @@
                 low, pltpu.roll(both[0], HEAD, 1), both[1]
             )
         for m in range(8):
-            out_w[0, m, zh, 0, :, 0:256] = part[0, 0, m, zh, 64:80, :].astype(F32)
-            out_w[0, m, zh, 0, :, 256:512] = part[0, 0, m, zh, 80:96, :].astype(F32)
+            out_w[0, m, zh, :, 0:256] = part[0, 0, m, zh, 64:80, :].astype(F32)
+            out_w[0, m, zh, :, 256:512] = part[0, 0, m, zh, 80:96, :].astype(F32)
 
     @pl.when(step == 0)
     def _():
@@ -897,12 +871,10 @@
         ],
         [
             wide,
-            pl.BlockSpec(
-                (1, 8, 2, 1, 16, 512), lambda i, which: (i % 2, 0, 0, i // 2, 0, which[0])
-            ),
+            pl.BlockSpec((1, 8, 2, 16, 512), lambda i, which: (i, 0, 0, 0, which[0])),
             whole(8, 128),
         ],
-        [sds((1024, 2048), F32), sds((2, 8, 2, 2, 16, 1024), F32), sds((8, 128), F32)],
+        [sds((1024, 2048), F32), sds((4, 8, 2, 16, 1024), F32), sds((8, 128), F32)],
         moved=16 << 20,
         scalars=1,
         aliases={5: 0, 6: 1} if before else None,
@@ -965,43 +937,51 @@
     o, y, rows = mid(o_recv, w_out, tok, gain_m, pos, [corner(h_near[1])])
     o_other = to_partner(o)
     x = among_experts(rows).reshape(1536, 1024)
+
     place = jnp.stack([blk, zh]).astype(jnp.int32)
     dx2, da, deo, hid = expert(place, x, dz_all, wgu, wdn, [corner(o_other)])
-    dx2_back = among_experts(dx2.reshape(32, 48, 1024))
-    experts_own, experts_send = expert_grad(which, x, da, hid, deo)
-    dy, dbr_own, dbr_send, do = mid_back(
-        which, dx2_back, pos, y, gain_m, dz, w_out, [hold(experts_send)]
-    )
-    experts_own = add_rounded(experts_own, to_partner(experts_send))
-    experts_far = lax.ppermute(experts_own, "zl", SWAP)
     h_near = after(h_near, hold(da))
     h_all = lax.all_gather(h_near, PLANE).reshape(16, 2, 64, 1024)
 
+    dx2_back = among_experts(dx2.reshape(32, 48, 1024))
+    outputs = expert_out(place, dz_all, hid, wdn)
+    experts_own, experts_send = expert_grad(which, x, da, hid, deo)
+    experts_own = add_rounded(experts_own, to_partner(experts_send))
+    dy, dbr_own, dbr_send, do = mid_back(
+        which, dx2_back, pos, y, gain_m, dz, w_out, [corner(experts_own), hold(outputs)]
+    )
+
+    sums = after(outputs.reshape(4096, 1024), hold(dbr_own))
+    sums = lax.psum_scatter(sums, PLANE, tiled=True).reshape(2, 128, 1024)
+    far = lax.ppermute(sums[1], ("zl", "zh"), Z_PAIRS)
+
 
     do_recv = exchange(do.reshape(32, 48, 128))
-    eo = expert_out(hid, wdn)
-    eo = out_grad(o, o_other, dbr_own, to_partner(dbr_send), eo)
-    eo_back = among_experts(after(eo, do_recv))
-    mixed = combine(eo_back, pos, gate, y)
-    out_part = out_sum(eo_back)
-    out_far = lax.ppermute(out_part, "zl", SWAP)
-    dqkv, gains = attend_back(info, arrived, do_recv, ot, lse, cos, sin, [])
+    out_partial = out_grad(o, o_other, dbr_own, to_partner(dbr_send))
+    out_sent = after(out_partial.reshape(64, 16, 512), do_recv)
+    experts_own = after(experts_own, hold(out_sent))
+    experts_far = lax.ppermute(experts_own, "zl", SWAP)
+    out_pieces = among_chips(out_sent)
+    dqkv, gains = attend_back(info, arrived, do_recv, ot, lse, cos, sin, [hold(out_sent)])
+
     place = jnp.stack([xh, zh]).astype(jnp.int32)
     qkv_partial = qkv_grad(place, h_all, dqkv, gains)
     experts_own = add_rounded(after(experts_own, hold(qkv_partial)), experts_far)
-    qkv_partial = after(qkv_partial, eo_back, corner(experts_own))
-    qkv_pieces = lax.all_to_all(qkv_partial, SAME_COLUMNS, 0, 0, tiled=True)
+    qkv_pieces = lax.all_to_all(
+        after(qkv_partial, out_pieces), SAME_COLUMNS, 0, 0, tiled=True
+    )
     experts_other = to_partner(experts_own)
     grad_gate_up, grad_down = final_expert(which, experts_own, experts_other)
-    copies, gains = add_pieces(zl, qkv_pieces, out_part, out_far, [])
-    own = await_all(among_chips(copies), hold(mixed), hold(grad_gate_up))
+    copies, gains = add_pieces(qkv_pieces, out_pieces, [corner(experts_own)])
+    own = await_all(among_chips(copies), hold(grad_gate_up))
     dqkv_recv = exchange(after(dqkv, corner(own))).reshape(2, 8, 2, 96, 128)
     rows = final(which, own, w_qkv, gain_attn.reshape(8, 128))
     grad_qkv, grad_out, grad_gain_attn = final(
         1 - which, to_partner(own), w_qkv, gain_attn.reshape(8, 128), (rows[2], rows[0], rows[1])
     )
-    grad_tokens = last(dqkv_recv, w_qkv, tok, gain_a, dy, [hold(grad_qkv)])
-
+    grad_tokens, mixed = last(
+        dqkv_recv, w_qkv, tok, gain_a, dy, y, sums, far, [hold(grad_qkv)]
+    )
     return (
         mixed.reshape(2, 64, 1024),
         grad_tokens.reshape(2, 64, 1024),

time: 396 us -> 394 us (level)
  local copies, waits for them, and re-layouts: 5.37 us -> 11.6 us
  waiting for transfers between devices: 170 us -> 166 us
    all_to_all x1 -> x2, waiting for transfers between devices: 30.6 us -> 52 us  [among_chips(): return lax.all_to_all(x, CHIPS, 0, 0, tiled=True)]
    all_to_all x3 -> x2, waiting for transfers between devices: 86.8 us -> 67.4 us  [among_experts(): lax.all_to_all(x, CHIPS, 0, 0, tiled=True, axis_index_groups=EXPERT_GROUPS)]
    ppermute x1, waiting for transfers between devices: 14.8 us -> 0.01 us  [shards(): experts_far = lax.ppermute(experts_own, 'zl', SWAP)]
    all_to_all x1, waiting for transfers between devices: 4.22 us -> 14.2 us  [shards(): lax.all_to_all(after(qkv_partial, out_pieces), SAME_COLUMNS, 0, 0, tiled=...]
    all_to_all x3 -> x2, starting transfers between devices: 25.8 us -> 17.3 us  [among_experts(): lax.all_to_all(x, CHIPS, 0, 0, tiled=True, axis_index_groups=EXPERT_GROUPS)]
    all_to_all x1 -> x2, starting transfers between devices: 6.58 us -> 13.4 us  [among_chips(): return lax.all_to_all(x, CHIPS, 0, 0, tiled=True)]
    unnamed x20 -> x25, local copies, waits for them, and re-layouts: 3.11 us -> 7.67 us
    pallas_call x19 -> x17, Pallas kernels: 107 us -> 104 us  [call(): built(*[place(i, x) for i, x in enumerate(operands)], *deps)]
  transfers between devices with their start and end apart: 21 -> 22, of which waited for: 15 -> 15; matrix products, arithmetic and copies ran while one was open for 2% -> 3% of each run, Pallas kernels for 21% -> 21%
where the time goes in v4:
time: 394 us; the launch traced here: 392 us
  waiting for transfers between devices  166 us (42%)
  Pallas kernels  104 us (26%)
  starting transfers between devices  90.3 us (23%)
  between operations  14 us (4%)
  local copies, waits for them, and re-layouts  11.6 us (3%)
  other arithmetic  5.83 us (1%)
    pallas_call x17, Pallas kernels, call(): built(*[place(i, x) for i, x in enumerate(operands)], *deps)  104 us
    all_to_all x2, waiting for transfers between devices, among_experts(): lax.all_to_all(x, CHIPS, 0, 0, tiled=True, axis_index_groups=EXPERT_GROUPS)  67.4 us
    all_to_all x2, waiting for transfers between devices, among_chips(): return lax.all_to_all(x, CHIPS, 0, 0, tiled=True)  52 us
    all_to_all x4, waiting for transfers between devices, exchange(): return lax.all_to_all(x, BLK, 0, 0, tiled=True)  22.3 us
    all_to_all x4, starting transfers between devices, exchange(): return lax.all_to_all(x, BLK, 0, 0, tiled=True)  22.1 us
    all_to_all x2, starting transfers between devices, among_experts(): lax.all_to_all(x, CHIPS, 0, 0, tiled=True, axis_index_groups=EXPERT_GROUPS)  17.3 us
    ppermute x5, starting transfers between devices, to_partner(): return lax.ppermute(part, 'core', SWAP)  17.1 us
    all_to_all x1, waiting for transfers between devices, shards(): lax.all_to_all(after(qkv_partial, out_pieces), SAME_COLUMNS, 0, 0, tiled=...  14.2 us
  transfers between devices with their start and end apart: 22, of which 15 were waited for; matrix products, arithmetic and copies ran while one was open for 3% of the time, Pallas kernels for 21%

profile of v4, /device:TPU:1, one launch (start us, length us, event | category | flops | bytes accessed | tf_op | source)
XLA Modules:
  0.0 392.3 jit_solution(17508574593936584929)
XLA Ops:
  7.2 4.7 %collective-permute-start = (bf16[128,1024]{1,0:T(8,128)(2,1)}, bf16[128,1024]{1,0:T(8,128)(2,1)S(1)}, u32[]{:S(2)}, u32[]{:S(2)}) collective-permute-start(bf16[128,1024]{1,0:T(8,128)(2,1)} %bitcast.66), channel_id=1, source_target_pairs={{0,65},{1,64},{64,1},{65,0},{2,67},{3,66},{66,3},{67,2},{4,69},{5,... | collective-permute-start | bytes 786440 | tf_op jit(solution)/shard_map/ppermute | solution.py:922
  11.9 1.5 shard_map.188
  13.4 5.2 %shard_map.189 = (bf16[128,1024]{1,0:T(8,128)(2,1)}, bf16[2,8,2,96,128]{4,3,2,1,0:T(8,128)(2,1)}) custom-call(s32[1]{0:T(128)} %bitcast.1.refs_0_, bf16[128,1024]{1,0:T(8,128)(2,1)} %bitcast.62, f32[1,1024]{1,0:T(1,128)} %bitcast.71, bf16[1024,2048]{1,0:T(8,128)(2,1)} %refs_4_.5, bf16[1024,2048]{1,0:T(8,128)(2,1)} %refs_4_.5, bf16[1024,2048]{1,0:T(8,128)(2,1)} %refs_4_.5, ...), custom_call_target="tpu_custom_call" | custom-call | flops 536870912 | bytes 5242880 | tf_op jit(solution)/shard_map/pallas_call | solution.py:88
  18.8 1.8 shard_map.190
  20.7 7.8 %all-to-all-start = ((bf16[32,96,128]{2,1,0:T(8,128)(2,1)}), bf16[32,96,128]{2,1,0:T(8,128)(2,1)S(1)}, u32[]{:S(2)}, u32[]{:S(2)}) async-start(bf16[32,96,128]{2,1,0:T(8,128)(2,1)} %bitcast.61), calls=%async_computation | async-start | bytes 1572864 | tf_op jit(solution)/shard_map/all_to_all | solution.py:886
  30.8 12.1 %all-to-all-done.refs_1_ = bf16[32,96,128]{2,1,0:T(8,128)(2,1)S(1)} async-done(((bf16[32,96,128]{2,1,0:T(8,128)(2,1)}), bf16[32,96,128]{2,1,0:T(8,128)(2,1)S(1)}, u32[]{:S(2)}, u32[]{:S(2)}) %all-to-all-start) | async-done | bytes 786464 | tf_op jit(solution)/shard_map/all_to_all | solution.py:886
  43.0 6.2 %shard_map.191 = (bf16[32,32,128]{2,1,0:T(8,128)(2,1)}, f32[4,64,512]{2,1,0:T(8,128)}, f32[4,8,512]{2,1,0:T(8,128)}) custom-call(s32[2]{0:T(128)S(1)} %pad_add_fusion.refs_0_, bf16[32,96,128]{2,1,0:T(8,128)(2,1)S(1)} %all-to-all-done.refs_1_, bf16[8,128]{1,0:T(8,128)(2,1)S(1)} %slice.38.refs_2_), custom_call_target="tpu_custom_call" | custom-call | flops 1342177280 | bytes 2097152 | tf_op jit(solution)/shard_map/pallas_call | solution.py:88
  49.1 5.3 %all-to-all-start.1 = ((bf16[32,32,128]{2,1,0:T(8,128)(2,1)}), bf16[32,32,128]{2,1,0:T(8,128)(2,1)S(1)}, u32[]{:S(2)}, u32[]{:S(2)}) async-start(bf16[32,32,128]{2,1,0:T(8,128)(2,1)} %get-tuple-element.44.refs_1_), calls=%async_computation.1 | async-start | bytes 524288 | tf_op jit(solution)/shard_map/all_to_all | solution.py:886
  55.1 2.7 collective-permute-start.2
  57.9 3.0 collective-permute-done.2
  60.9 3.1 all-to-all-done.1
  64.0 4.7 %shard_map.192 = (bf16[128,1024]{1,0:T(8,128)(2,1)}, f32[128,1024]{1,0:T(8,128)}, bf16[32,48,1024]{2,1,0:T(8,128)(2,1)}) custom-call(bf16[2,8,2,32,128]{4,3,2,1,0:T(8,128)(2,1)S(1)} %bitcast.48, bf16[1024,1024]{1,0:T(8,128)(2,1)} %refs_9_.1, bf16[1024,1024]{1,0:T(8,128)(2,1)} %refs_9_.1, bf16[1024,1024]{1,0:T(8,128)(2,1)} %refs_9_.1, ...), custom_call_target="tpu_custom_call" | custom-call | flops 671088640 | bytes 6291456 | tf_op jit(solution)/shard_map/pallas_call | solution.py:88
  68.7 7.6 %all-to-all-start.2 = ((bf16[32,48,1024]{2,1,0:T(8,128)(2,1)}), bf16[32,48,1024]{2,1,0:T(8,128)(2,1)S(1)}, u32[]{:S(2)}, u32[]{:S(2)}) async-start(bf16[32,48,1024]{2,1,0:T(8,128)(2,1)} %get-tuple-element.47), calls=%async_computation.2 | async-start | bytes 6291456 | tf_op jit(solution)/shard_map/all_to_all | solution.py:894
  76.3 9.4 %collective-permute-start.3 = (bf16[128,1024]{1,0:T(8,128)(2,1)}, bf16[128,1024]{1,0:T(8,128)(2,1)S(1)}, u32[]{:S(2)}, u32[]{:S(2)}) collective-permute-start(bf16[128,1024]{1,0:T(8,128)(2,1)} %get-tuple-element.48.refs_0_), channel_id=1, source_target_pairs={{0,32},{32,0},{1,33},{33,1},{2,34},{34,2},{3,35},{35,3},{4,36},{36... | collective-permute-start | bytes 786440 | tf_op jit(solution)/shard_map/ppermute | solution.py:920
  85.8 1.6 pad_maximum_fusion.refs_0_
  87.5 47.0 %all-to-all-done.2 = bf16[32,48,1024]{2,1,0:T(8,128)(2,1)S(1)} async-done(((bf16[32,48,1024]{2,1,0:T(8,128)(2,1)}), bf16[32,48,1024]{2,1,0:T(8,128)(2,1)S(1)}, u32[]{:S(2)}, u32[]{:S(2)}) %all-to-all-start.2) | async-done | bytes 3145760 | tf_op jit(solution)/shard_map/all_to_all | solution.py:894
  134.6 15.3 %shard_map.193 = (bf16[1536,1024]{1,0:T(8,128)(2,1)}, bf16[1536,1024]{1,0:T(8,128)(2,1)}, bf16[1536,1024]{1,0:T(8,128)(2,1)}, bf16[1536,512]{1,0:T(8,128)(2,1)}) custom-call(s32[2]{0:T(128)S(1)} %pad_add_fusion.1.refs_0_, bf16[1536,1024]{1,0:T(8,128)(2,1)S(1)} %bitcast.45, bf16[16,2,144,1024]{3,2,1,0:T(8,128)(2,1)} %bitcast.50, ...), custom_call_target="tpu_custom_call" | custom-call | flops 8858370048 | bytes 27262976 | tf_op jit(solution)/shard_map/pallas_call | solution.py:88
  150.0 9.6 %all-to-all-start.3 = ((bf16[32,48,1024]{2,1,0:T(8,128)(2,1)}), bf16[32,48,1024]{2,1,0:T(8,128)(2,1)S(1)}, u32[]{:S(2)}, u32[]{:S(2)}) async-start(bf16[32,48,1024]{2,1,0:T(8,128)(2,1)} %bitcast.60), calls=%async_computation.3 | async-start | bytes 6291456 | tf_op jit(solution)/shard_map/all_to_all | solution.py:894
  159.9 1.9 copy-done.3
  161.8 11.0 %shard_map.194 = (bf16[768,1024]{1,0:T(8,128)(2,1)}, bf16[768,1024]{1,0:T(8,128)(2,1)}) custom-call(s32[1]{0:T(128)} %bitcast.7.refs_0_, bf16[1536,1024]{1,0:T(8,128)(2,1)S(1)} %bitcast.46, bf16[1536,1024]{1,0:T(8,128)(2,1)} %get-tuple-element.51.refs_2_.refs_1_, bf16[1536,512]{1,0:T(8,128)(2,1)} %get-tuple-element.52.refs_3_.refs_2_, ...), custom_call_target="tpu_custom_call" | custom-call | flops 4831838208 | bytes 16777216 | tf_op jit(solution)/shard_map/pallas_call | solution.py:88
  173.9 8.2 %shard_map.195.refs_11_ = bf16[16,2,128,1024]{3,2,1,0:T(8,128)(2,1)} custom-call(s32[2]{0:T(128)S(1)} %pad_add_fusion.1.refs_0_, bf16[16,2,144,1024]{3,2,1,0:T(8,128)(2,1)} %bitcast.52, bf16[1536,512]{1,0:T(8,128)(2,1)} %get-tuple-element.52.refs_3_.refs_2_, bf16[512,1024]{1,0:T(8,128)(2,1)} %bitcast.55, bf16[512,1024]{1,0:T(8,128)(2,1)} %bitcast.56), custom_call_target="tpu_custom_call" | custom-call | flops 2415919104 | bytes 12582912 | tf_op jit(solution)/shard_map/pallas_call | solution.py:88
  183.9 20.5 %all-to-all-done.3.refs_1_ = bf16[32,48,1024]{2,1,0:T(8,128)(2,1)S(1)} async-done(((bf16[32,48,1024]{2,1,0:T(8,128)(2,1)}), bf16[32,48,1024]{2,1,0:T(8,128)(2,1)S(1)}, u32[]{:S(2)}, u32[]{:S(2)}) %all-to-all-start.3) | async-done | bytes 3145760 | tf_op jit(solution)/shard_map/all_to_all | solution.py:894
  204.4 4.2 %shard_map.196 = (f32[128,1024]{1,0:T(8,128)}, bf16[128,512]{1,0:T(8,128)(2,1)}, bf16[128,512]{1,0:T(8,128)(2,1)}, bf16[2,8,2,48,128]{4,3,2,1,0:T(8,128)(2,1)}) custom-call(s32[1]{0:T(128)} %bitcast.7.refs_0_, bf16[32,48,1024]{2,1,0:T(8,128)(2,1)S(1)} %all-to-all-done.3.refs_1_, s32[32,128]{1,0:T(8,128)} %get-tuple-element.45.refs_7_.refs_2_, ...), custom_call_target="tpu_custom_call" | custom-call | flops 671088640 | bytes 6291456 | tf_op jit(solution)/shard_map/pallas_call | solution.py:88
  208.6 4.3 %all-to-all-start.4 = ((bf16[32,48,128]{2,1,0:T(8,128)(2,1)}), bf16[32,48,128]{2,1,0:T(8,128)(2,1)S(1)}, u32[]{:S(2)}, u32[]{:S(2)}) async-start(bf16[32,48,128]{2,1,0:T(8,128)(2,1)} %bitcast.20), calls=%async_computation.4 | async-start | bytes 786432 | tf_op jit(solution)/shard_map/all_to_all | solution.py:886
  212.9 2.1 collective-permute-start.5
  216.0 3.7 shard_map.197
  219.7 6.9 %all-to-all-done.4.refs_1_.refs_2_ = bf16[32,48,128]{2,1,0:T(8,128)(2,1)S(1)} async-done(((bf16[32,48,128]{2,1,0:T(8,128)(2,1)}), bf16[32,48,128]{2,1,0:T(8,128)(2,1)S(1)}, u32[]{:S(2)}, u32[]{:S(2)}) %all-to-all-start.4) | async-done | bytes 393248 | tf_op jit(solution)/shard_map/all_to_all | solution.py:886
  228.0 6.6 %all-to-all-start.5 = ((bf16[64,16,512]{2,1,0:T(8,128)(2,1)}), bf16[64,16,512]{2,1,0:T(8,128)(2,1)S(1)}, u32[]{:S(2)}, u32[]{:S(2)}) async-start(bf16[64,16,512]{2,1,0:T(8,128)(2,1)} %shard_map.198.refs_7_.refs_1_), calls=%async_computation.5 | async-start | bytes 2097152 | tf_op jit(solution)/shard_map/all_to_all | solution.py:898
  234.6 14.3 %shard_map.199 = (bf16[32,96,128]{2,1,0:T(8,128)(2,1)}, f32[8,128]{1,0:T(8,128)}) custom-call(s32[2]{0:T(128)S(1)} %pad_add_fusion.refs_0_, bf16[32,96,128]{2,1,0:T(8,128)(2,1)S(1)} %copy-done.6, bf16[32,48,128]{2,1,0:T(8,128)(2,1)S(1)} %all-to-all-done.4.refs_1_.refs_2_, f32[4,64,512]{2,1,0:T(8,128)} %get-tuple-element.57.refs_3_, ...), custom_call_target="tpu_custom_call" | custom-call | flops 3355443200 | bytes 3145728 | tf_op jit(solution)/shard_map/pallas_call | solution.py:88
  248.9 5.9 %shard_map.202.refs_1_ = bf16[16,80,256]{2,1,0:T(8,128)(2,1)} custom-call(s32[2]{0:T(128)S(1)} %pad_add_fusion.2.refs_0_, bf16[16,2,64,1024]{3,2,1,0:T(8,128)(2,1)} %bitcast.57, bf16[32,96,128]{2,1,0:T(8,128)(2,1)} %get-tuple-element.61.refs_2_.refs_0_, f32[8,128]{1,0:T(8,128)} %get-tuple-element.62.refs_3_), custom_call_target="tpu_custom_call" | custom-call | flops 1073741824 | bytes 6291456 | tf_op jit(solution)/shard_map/pallas_call | solution.py:88
  254.7 2.0 copy.35.refs_0_
  256.7 14.8 %all-to-all-done.5.refs_1_ = bf16[64,16,512]{2,1,0:T(8,128)(2,1)S(1)} async-done(((bf16[64,16,512]{2,1,0:T(8,128)(2,1)}), bf16[64,16,512]{2,1,0:T(8,128)(2,1)S(1)}, u32[]{:S(2)}, u32[]{:S(2)}) %all-to-all-start.5) | async-done | bytes 1048608 | tf_op jit(solution)/shard_map/all_to_all | solution.py:898
  271.6 8.5 %all-to-all-start.6 = ((bf16[16,80,256]{2,1,0:T(8,128)(2,1)}), bf16[16,80,256]{2,1,0:T(8,128)(2,1)S(1)}, u32[]{:S(2)}, u32[]{:S(2)}) async-start(bf16[16,80,256]{2,1,0:T(8,128)(2,1)} %shard_map.203), calls=%async_computation.6 | async-start | bytes 1310720 | tf_op jit(solution)/shard_map/all_to_all | solution.py:970
  280.1 2.7 add_convert_fusion.refs_1_
  284.0 14.2 %all-to-all-done.6.refs_0_ = bf16[16,80,256]{2,1,0:T(8,128)(2,1)S(1)} async-done(((bf16[16,80,256]{2,1,0:T(8,128)(2,1)}), bf16[16,80,256]{2,1,0:T(8,128)(2,1)S(1)}, u32[]{:S(2)}, u32[]{:S(2)}) %all-to-all-start.6) | async-done | bytes 655392 | tf_op jit(solution)/shard_map/all_to_all | solution.py:970
  298.2 2.0 shard_map.206
  300.2 6.8 %all-to-all-start.7 = ((bf16[64,96,256]{2,1,0:T(8,128)(2,1)}), bf16[64,96,256]{2,1,0:T(8,128)(2,1)S(1)}, u32[]{:S(2)}, u32[]{:S(2)}) async-start(bf16[64,96,256]{2,1,0:T(8,128)(2,1)} %get-tuple-element.63), calls=%async_computation.7 | async-start | bytes 6291456 | tf_op jit(solution)/shard_map/all_to_all | solution.py:898
  308.0 3.2 collective-permute-done.7.refs_2_
  312.7 3.8 shard_map.207
  316.5 37.1 %all-to-all-done.7.refs_0_ = bf16[64,96,256]{2,1,0:T(8,128)(2,1)S(1)} async-done(((bf16[64,96,256]{2,1,0:T(8,128)(2,1)}), bf16[64,96,256]{2,1,0:T(8,128)(2,1)S(1)}, u32[]{:S(2)}, u32[]{:S(2)}) %all-to-all-start.7) | async-done | bytes 3145760 | tf_op jit(solution)/shard_map/all_to_all | solution.py:898
  353.6 3.6 collective-permute-start.9
  357.2 4.6 %all-to-all-start.8 = ((bf16[32,96,128]{2,1,0:T(8,128)(2,1)}), bf16[32,96,128]{2,1,0:T(8,128)(2,1)}, u32[]{:S(2)}, u32[]{:S(2)}) async-start(bf16[32,96,128]{2,1,0:T(8,128)(2,1)} %shard_map.209), calls=%async_computation.8 | async-start | bytes 1572864 | tf_op jit(solution)/shard_map/all_to_all | solution.py:886
  361.9 1.7 slice.45
  363.5 2.8 collective-permute-start.8
  366.3 5.1 %shard_map.211 = (f32[1024,2048]{1,0:T(8,128)}, f32[4,8,2,16,1024]{4,3,2,1,0:T(8,128)}, f32[8,128]{1,0:T(8,128)}) custom-call(s32[1]{0:T(128)} %bitcast.7.refs_0_, bf16[2,2,8,2,96,256]{5,4,3,2,1,0:T(8,128)(2,1)S(1)} %bitcast.44, bf16[1024,2048]{1,0:T(8,128)(2,1)} %refs_4_.5, f32[8,128]{1,0:T(8,128)} %bitcast.72), custom_call_target="tpu_custom_call" | custom-call | bytes 16777216 | tf_op jit(solution)/shard_map/pallas_call | solution.py:88
  371.5 6.0 %shard_map.212 = (f32[1024,2048]{1,0:T(8,128)}, f32[4,8,2,16,1024]{4,3,2,1,0:T(8,128)}, f32[8,128]{1,0:T(8,128)}) custom-call(s32[1]{0:T(128)S(6)} %sub.7.refs_0_, bf16[2,2,8,2,96,256]{5,4,3,2,1,0:T(8,128)(2,1)} %bitcast.30.refs_1_, bf16[1024,2048]{1,0:T(8,128)(2,1)} %refs_4_.5, f32[8,128]{1,0:T(8,128)} %bitcast.73, ...), custom_call_target="tpu_custom_call", output_to_operand_aliasing={{0}: (5, {}), {1}: (6, {})} | custom-call | bytes 16777216 | tf_op jit(solution)/shard_map/pallas_call | solution.py:88
  377.8 2.7 collective-permute-done.8.refs_10_
  380.4 5.3 %shard_map.213 = (f32[128,1024]{1,0:T(8,128)}, bf16[128,1024]{1,0:T(8,128)(2,1)}) custom-call(bf16[2,8,2,96,128]{4,3,2,1,0:T(8,128)(2,1)} %bitcast.27.refs_0_, bf16[1024,2048]{1,0:T(8,128)(2,1)} %refs_4_.5, bf16[1024,2048]{1,0:T(8,128)(2,1)} %refs_4_.5, bf16[1024,2048]{1,0:T(8,128)(2,1)} %refs_4_.5, bf16[1024,2048]{1,0:T(8,128)(2,1)} %refs_4_.5, ...), custom_call_target="tpu_custom_call" | custom-call | flops 536870912 | bytes 6291456 | tf_op jit(solution)/shard_map/pallas_call | solution.py:88
  (67 shorter events, 13.1 us)
Async XLA Ops:
  7.2 127.4 %all-gather.5.cloned.1.call-start = ((), (), s32[]{:S(2)}) async-start(), calls=%async_computation.11 | async-start | bytes 10027008 | tf_op jit(solution)/shard_map/all_gather | solution.py:929
  7.2 11.6 %collective-permute-start = (bf16[128,1024]{1,0:T(8,128)(2,1)}, bf16[128,1024]{1,0:T(8,128)(2,1)S(1)}, u32[]{:S(2)}, u32[]{:S(2)}) collective-permute-start(bf16[128,1024]{1,0:T(8,128)(2,1)} %bitcast.66), channel_id=1, source_target_pairs={{0,65},{1,64},{64,1},{65,0},{2,67},{3,66},{66,3},{67,2},{4,69},{5,... | collective-permute-start | bytes 786440 | tf_op jit(solution)/shard_map/ppermute | solution.py:922
  13.4 5.4 %collective-permute-start.1 = (bf16[16,1024]{1,0:T(8,128)(2,1)}, bf16[16,1024]{1,0:T(8,128)(2,1)S(1)}, u32[]{:S(2)}, u32[]{:S(2)}) collective-permute-start(bf16[16,1024]{1,0:T(8,128)(2,1)} %get-tuple-element.42.refs_8_.refs_1_), channel_id=1, source_target_pairs={{0,65},{1,64},{64,1},{65,0},{2,67},{3,66},{66,3},{67,2},{4,69},{5,... | collective-permute-start | bytes 98312 | tf_op jit(solution)/shard_map/ppermute | solution.py:924
  18.6 9.9 %copy-start.11 = (s32[2]{0:T(128)S(1)}, s32[2]{0:T(128)}, u32[]{:S(2)}) copy-start(s32[2]{0:T(128)} %param.14) | copy-start | bytes 28
  20.7 22.3 %all-to-all-start = ((bf16[32,96,128]{2,1,0:T(8,128)(2,1)}), bf16[32,96,128]{2,1,0:T(8,128)(2,1)S(1)}, u32[]{:S(2)}, u32[]{:S(2)}) async-start(bf16[32,96,128]{2,1,0:T(8,128)(2,1)} %bitcast.61), calls=%async_computation | async-start | bytes 1572864 | tf_op jit(solution)/shard_map/all_to_all | solution.py:886
  28.5 26.0 %copy-start.9 = (bf16[128,1024]{1,0:T(8,128)(2,1)S(1)}, bf16[128,1024]{1,0:T(8,128)(2,1)}, u32[]{:S(2)}) copy-start(bf16[128,1024]{1,0:T(8,128)(2,1)} %get-tuple-element.46) | copy-start | bytes 786436
  43.0 6.2 %copy-start.5 = (bf16[32,96,128]{2,1,0:T(8,128)(2,1)}, bf16[32,96,128]{2,1,0:T(8,128)(2,1)S(1)}, u32[]{:S(2)}) copy-start(bf16[32,96,128]{2,1,0:T(8,128)(2,1)S(1)} %all-to-all-done.refs_1_) | copy-start | bytes 2359300
  49.1 14.8 %all-to-all-start.1 = ((bf16[32,32,128]{2,1,0:T(8,128)(2,1)}), bf16[32,32,128]{2,1,0:T(8,128)(2,1)S(1)}, u32[]{:S(2)}, u32[]{:S(2)}) async-start(bf16[32,32,128]{2,1,0:T(8,128)(2,1)} %get-tuple-element.44.refs_1_), calls=%async_computation.1 | async-start | bytes 524288 | tf_op jit(solution)/shard_map/all_to_all | solution.py:886
  55.1 5.8 %collective-permute-start.2 = (bf16[64,1024]{1,0:T(8,128)(2,1)S(1)}, bf16[64,1024]{1,0:T(8,128)(2,1)S(1)}, u32[]{:S(2)}, u32[]{:S(2)}) collective-permute-start(bf16[64,1024]{1,0:T(8,128)(2,1)S(1)} %get-tuple-element.77), channel_id=1, source_target_pairs={{0,1},{1,0},{2,3},{3,2},{4,5},{5,4},{6,7},{7,6},{8,9},{9,8},{10,11... | collective-permute-start | bytes 393224 | tf_op jit(solution)/shard_map/ppermute | solution.py:934
  68.7 65.8 %all-to-all-start.2 = ((bf16[32,48,1024]{2,1,0:T(8,128)(2,1)}), bf16[32,48,1024]{2,1,0:T(8,128)(2,1)S(1)}, u32[]{:S(2)}, u32[]{:S(2)}) async-start(bf16[32,48,1024]{2,1,0:T(8,128)(2,1)} %get-tuple-element.47), calls=%async_computation.2 | async-start | bytes 6291456 | tf_op jit(solution)/shard_map/all_to_all | solution.py:894
  76.3 172.6 %all-gather.7.cloned.1.call-start = ((), (), s32[]{:S(2)}) async-start(), calls=%async_computation.12 | async-start | bytes 4456448 | tf_op jit(solution)/shard_map/all_gather | solution.py:944
  76.3 11.1 %collective-permute-start.3 = (bf16[128,1024]{1,0:T(8,128)(2,1)}, bf16[128,1024]{1,0:T(8,128)(2,1)S(1)}, u32[]{:S(2)}, u32[]{:S(2)}) collective-permute-start(bf16[128,1024]{1,0:T(8,128)(2,1)} %get-tuple-element.48.refs_0_), channel_id=1, source_target_pairs={{0,32},{32,0},{1,33},{33,1},{2,34},{34,2},{3,35},{35,3},{4,36},{36... | collective-permute-start | bytes 786440 | tf_op jit(solution)/shard_map/ppermute | solution.py:920
  134.4 15.5 %copy-start.2 = (bf16[32,48,1024]{2,1,0:T(8,128)(2,1)}, bf16[32,48,1024]{2,1,0:T(8,128)(2,1)S(1)}, u32[]{:S(2)}) copy-start(bf16[32,48,1024]{2,1,0:T(8,128)(2,1)S(1)} %all-to-all-done.2) | copy-start | bytes 9437188
  150.0 54.4 %all-to-all-start.3 = ((bf16[32,48,1024]{2,1,0:T(8,128)(2,1)}), bf16[32,48,1024]{2,1,0:T(8,128)(2,1)S(1)}, u32[]{:S(2)}, u32[]{:S(2)}) async-start(bf16[32,48,1024]{2,1,0:T(8,128)(2,1)} %bitcast.60), calls=%async_computation.3 | async-start | bytes 6291456 | tf_op jit(solution)/shard_map/all_to_all | solution.py:894
  159.6 202.2 %reduce-scatter.2.cloned.1.call-start = ((), (), s32[]{:S(2)}) async-start(), calls=%async_computation.10 | async-start | bytes 8912896 | tf_op jit(solution)/shard_map/reduce_scatter | solution.py:955
  159.9 1.9 copy-start.3
  172.8 9.3 %copy-start.8 = (bf16[768,1024]{1,0:T(8,128)(2,1)S(1)}, bf16[768,1024]{1,0:T(8,128)(2,1)}, u32[]{:S(2)}) copy-start(bf16[768,1024]{1,0:T(8,128)(2,1)} %get-tuple-element.54) | copy-start | bytes 4718596
  172.8 9.3 %collective-permute-start.4 = (bf16[768,1024]{1,0:T(8,128)(2,1)}, bf16[768,1024]{1,0:T(8,128)(2,1)S(1)}, u32[]{:S(2)}, u32[]{:S(2)}) collective-permute-start(bf16[768,1024]{1,0:T(8,128)(2,1)} %get-tuple-element.55), channel_id=1, source_target_pairs={{0,32},{32,0},{1,33},{33,1},{2,34},{34,2},{3,35},{35,3},{4,36},{36... | collective-permute-start | bytes 4718600 | tf_op jit(solution)/shard_map/ppermute | solution.py:920
  182.8 1.1 copy-start.7
  208.6 4.4 %copy-start.10 = (bf16[128,512]{1,0:T(8,128)(2,1)S(1)}, bf16[128,512]{1,0:T(8,128)(2,1)}, u32[]{:S(2)}) copy-start(bf16[128,512]{1,0:T(8,128)(2,1)} %get-tuple-element.60) | copy-start | bytes 393220
  208.6 18.0 %all-to-all-start.4 = ((bf16[32,48,128]{2,1,0:T(8,128)(2,1)}), bf16[32,48,128]{2,1,0:T(8,128)(2,1)S(1)}, u32[]{:S(2)}, u32[]{:S(2)}) async-start(bf16[32,48,128]{2,1,0:T(8,128)(2,1)} %bitcast.20), calls=%async_computation.4 | async-start | bytes 786432 | tf_op jit(solution)/shard_map/all_to_all | solution.py:886
  212.9 3.0 collective-permute-start.5
  226.6 8.0 %copy-start.6 = (bf16[32,96,128]{2,1,0:T(8,128)(2,1)S(1)}, bf16[32,96,128]{2,1,0:T(8,128)(2,1)}, u32[]{:S(2)}) copy-start(bf16[32,96,128]{2,1,0:T(8,128)(2,1)} %copy-done.5) | copy-start | bytes 2359300
  226.6 53.5 %collective-permute-start.6 = (bf16[768,1024]{1,0:T(8,128)(2,1)}, bf16[768,1024]{1,0:T(8,128)(2,1)}, u32[]{:S(2)}, u32[]{:S(2)}) collective-permute-start(bf16[768,1024]{1,0:T(8,128)(2,1)} %shard_map.204.refs_0_), channel_id=1, source_target_pairs={{0,64},{64,0},{1,65},{65,1},{2,66},{66,2},{3,67},{67,3},{4,68},{68... | collective-permute-start | bytes 4718600 | tf_op jit(solution)/shard_map/ppermute | solution.py:963
  228.0 43.6 %all-to-all-start.5 = ((bf16[64,16,512]{2,1,0:T(8,128)(2,1)}), bf16[64,16,512]{2,1,0:T(8,128)(2,1)S(1)}, u32[]{:S(2)}, u32[]{:S(2)}) async-start(bf16[64,16,512]{2,1,0:T(8,128)(2,1)} %shard_map.198.refs_7_.refs_1_), calls=%async_computation.5 | async-start | bytes 2097152 | tf_op jit(solution)/shard_map/all_to_all | solution.py:898
  271.6 26.6 %all-to-all-start.6 = ((bf16[16,80,256]{2,1,0:T(8,128)(2,1)}), bf16[16,80,256]{2,1,0:T(8,128)(2,1)S(1)}, u32[]{:S(2)}, u32[]{:S(2)}) async-start(bf16[16,80,256]{2,1,0:T(8,128)(2,1)} %shard_map.203), calls=%async_computation.6 | async-start | bytes 1310720 | tf_op jit(solution)/shard_map/all_to_all | solution.py:970
  282.8 1.1 copy-start
  300.2 53.4 %all-to-all-start.7 = ((bf16[64,96,256]{2,1,0:T(8,128)(2,1)}), bf16[64,96,256]{2,1,0:T(8,128)(2,1)S(1)}, u32[]{:S(2)}, u32[]{:S(2)}) async-start(bf16[64,96,256]{2,1,0:T(8,128)(2,1)} %get-tuple-element.63), calls=%async_computation.7 | async-start | bytes 6291456 | tf_op jit(solution)/shard_map/all_to_all | solution.py:898
  307.0 4.2 %collective-permute-start.7 = (bf16[768,1024]{1,0:T(8,128)(2,1)}, bf16[768,1024]{1,0:T(8,128)(2,1)S(1)}, u32[]{:S(2)}, u32[]{:S(2)}) collective-permute-start(bf16[768,1024]{1,0:T(8,128)(2,1)} %copy-done), channel_id=1, source_target_pairs={{0,32},{32,0},{1,33},{33,1},{2,34},{34,2},{3,35},{35,3},{4,36},{36... | collective-permute-start | bytes 4718600 | tf_op jit(solution)/shard_map/ppermute | solution.py:920
  311.2 1.4 copy-start.1
  353.6 17.8 %collective-permute-start.9 = (bf16[64,96,256]{2,1,0:T(8,128)(2,1)S(1)}, bf16[64,96,256]{2,1,0:T(8,128)(2,1)}, u32[]{:S(2)}, u32[]{:S(2)}) collective-permute-start(bf16[64,96,256]{2,1,0:T(8,128)(2,1)S(1)} %shard_map.208), channel_id=1, source_target_pairs={{0,32},{32,0},{1,33},{33,1},{2,34},{34,2},{3,35},{35,3},{4,36},{36... | collective-permute-start | bytes 9437192 | tf_op jit(solution)/shard_map/ppermute | solution.py:920
  357.2 20.6 %all-to-all-start.8 = ((bf16[32,96,128]{2,1,0:T(8,128)(2,1)}), bf16[32,96,128]{2,1,0:T(8,128)(2,1)}, u32[]{:S(2)}, u32[]{:S(2)}) async-start(bf16[32,96,128]{2,1,0:T(8,128)(2,1)} %shard_map.209), calls=%async_computation.8 | async-start | bytes 1572864 | tf_op jit(solution)/shard_map/all_to_all | solution.py:886
  363.5 16.9 %collective-permute-start.8 = (bf16[128,1024]{1,0:T(8,128)(2,1)}, bf16[128,1024]{1,0:T(8,128)(2,1)S(1)}, u32[]{:S(2)}, u32[]{:S(2)}) collective-permute-start(bf16[128,1024]{1,0:T(8,128)(2,1)} %slice.45), channel_id=1, source_target_pairs={{0,65},{1,64},{64,1},{65,0},{2,67},{3,66},{66,3},{67,2},{4,69},{5,... | collective-permute-start | bytes 786440 | tf_op jit(solution)/shard_map/ppermute | solution.py:956
  371.5 9.0 %copy-start.4 = (bf16[256,1024]{1,0:T(8,128)(2,1)S(1)}, bf16[256,1024]{1,0:T(8,128)(2,1)}, u32[]{:S(2)}) copy-start(bf16[256,1024]{1,0:T(8,128)(2,1)} %reduce-scatter.2.cloned.1.call-done) | copy-start | bytes 1572868
Sparse Core Ops, SparseCore 0:
  20.8 113.7 all-gather.4
  150.1 83.3 all-gather.6
  237.5 113.7 reduce-scatter.1

commit v5 on v4

--- a/solution.py
+++ b/solution.py
@@ -946,9 +946,12 @@
     dx2_back = among_experts(dx2.reshape(32, 48, 1024))
     outputs = expert_out(place, dz_all, hid, wdn)
     experts_own, experts_send = expert_grad(which, x, da, hid, deo)
-    experts_own = add_rounded(experts_own, to_partner(experts_send))
+    experts_far = to_partner(experts_send)
+    early = add_rounded(experts_own[:256], experts_far[:256])
+    late = add_rounded(experts_own[256:], experts_far[256:])
+    early = add_rounded(early, lax.ppermute(early, "zl", SWAP))
     dy, dbr_own, dbr_send, do = mid_back(
-        which, dx2_back, pos, y, gain_m, dz, w_out, [corner(experts_own), hold(outputs)]
+        which, dx2_back, pos, y, gain_m, dz, w_out, [corner(early), hold(outputs)]
     )
 
     sums = after(outputs.reshape(4096, 1024), hold(dbr_own))
@@ -959,20 +962,21 @@
     do_recv = exchange(do.reshape(32, 48, 128))
     out_partial = out_grad(o, o_other, dbr_own, to_partner(dbr_send))
     out_sent = after(out_partial.reshape(64, 16, 512), do_recv)
-    experts_own = after(experts_own, hold(out_sent))
-    experts_far = lax.ppermute(experts_own, "zl", SWAP)
+    late = after(late, hold(out_sent))
+    late_far = lax.ppermute(late, "zl", SWAP)
     out_pieces = among_chips(out_sent)
     dqkv, gains = attend_back(info, arrived, do_recv, ot, lse, cos, sin, [hold(out_sent)])
 
     place = jnp.stack([xh, zh]).astype(jnp.int32)
     qkv_partial = qkv_grad(place, h_all, dqkv, gains)
-    experts_own = add_rounded(after(experts_own, hold(qkv_partial)), experts_far)
+    late = add_rounded(after(late, hold(qkv_partial)), late_far)
+    experts_own = jnp.concatenate([early, late], 0)
     qkv_pieces = lax.all_to_all(
         after(qkv_partial, out_pieces), SAME_COLUMNS, 0, 0, tiled=True
     )
     experts_other = to_partner(experts_own)
     grad_gate_up, grad_down = final_expert(which, experts_own, experts_other)
-    copies, gains = add_pieces(qkv_pieces, out_pieces, [corner(experts_own)])
+    copies, gains = add_pieces(qkv_pieces, out_pieces, [corner(late)])
     own = await_all(among_chips(copies), hold(grad_gate_up))
     dqkv_recv = exchange(after(dqkv, corner(own))).reshape(2, 8, 2, 96, 128)
     rows = final(which, own, w_qkv, gain_attn.reshape(8, 128))

time: 394 us -> 382 us (0.970)
  waiting for transfers between devices: 166 us -> 143 us
  starting transfers between devices: 90.3 us -> 97.6 us
  other arithmetic: 5.83 us -> 9.78 us
    all_to_all x2, waiting for transfers between devices: 52 us -> 29.7 us  [among_chips(): return lax.all_to_all(x, CHIPS, 0, 0, tiled=True)]
    all_to_all x2, waiting for transfers between devices: 67.4 us -> 57.4 us  [among_experts(): lax.all_to_all(x, CHIPS, 0, 0, tiled=True, axis_index_groups=EXPERT_GROUPS)]
    ppermute x1 -> x2, waiting for transfers between devices: 0.01 us -> 5.07 us  [the longest x1 5.06 us: shards(): early = add_rounded(early, lax.ppermute(early, 'zl', SWAP))]
  transfers between devices with their start and end apart: 22 -> 23, of which waited for: 15 -> 15; matrix products, arithmetic and copies ran while one was open for 3% -> 4% of each run, Pallas kernels for 21% -> 22%
where the time goes in v5:
time: 382 us; the launch traced here: 380 us
  waiting for transfers between devices  143 us (37%)
  Pallas kernels  104 us (27%)
  starting transfers between devices  97.6 us (26%)
  between operations  14 us (4%)
  local copies, waits for them, and re-layouts  10.8 us (3%)
  other arithmetic  9.78 us (3%)
    pallas_call x17, Pallas kernels, call(): built(*[place(i, x) for i, x in enumerate(operands)], *deps)  104 us
    all_to_all x2, waiting for transfers between devices, among_experts(): lax.all_to_all(x, CHIPS, 0, 0, tiled=True, axis_index_groups=EXPERT_GROUPS)  57.4 us
    all_to_all x2, waiting for transfers between devices, among_chips(): return lax.all_to_all(x, CHIPS, 0, 0, tiled=True)  29.7 us
    all_to_all x4, starting transfers between devices, exchange(): return lax.all_to_all(x, BLK, 0, 0, tiled=True)  23.6 us
    all_to_all x4, waiting for transfers between devices, exchange(): return lax.all_to_all(x, BLK, 0, 0, tiled=True)  22.1 us
    ppermute x5, starting transfers between devices, to_partner(): return lax.ppermute(part, 'core', SWAP)  19.1 us
    all_to_all x2, starting transfers between devices, among_experts(): lax.all_to_all(x, CHIPS, 0, 0, tiled=True, axis_index_groups=EXPERT_GROUPS)  17.3 us
    all_to_all x1, waiting for transfers between devices, shards(): lax.all_to_all(after(qkv_partial, out_pieces), SAME_COLUMNS, 0, 0, tiled=...  15.6 us
  transfers between devices with their start and end apart: 23, of which 15 were waited for; matrix products, arithmetic and copies ran while one was open for 4% of the time, Pallas kernels for 22%

profile of v5, /device:TPU:1, one launch (start us, length us, event | category | flops | bytes accessed | tf_op | source)
XLA Modules:
  0.0 379.8 jit_solution(14170293601852490469)
XLA Ops:
  7.2 4.7 %collective-permute-start = (bf16[128,1024]{1,0:T(8,128)(2,1)}, bf16[128,1024]{1,0:T(8,128)(2,1)S(1)}, u32[]{:S(2)}, u32[]{:S(2)}) collective-permute-start(bf16[128,1024]{1,0:T(8,128)(2,1)} %bitcast.67), channel_id=1, source_target_pairs={{0,65},{1,64},{64,1},{65,0},{2,67},{3,66},{66,3},{67,2},{4,69},{5,... | collective-permute-start | bytes 786440 | tf_op jit(solution)/shard_map/ppermute | solution.py:922
  13.4 5.2 %shard_map.189 = (bf16[128,1024]{1,0:T(8,128)(2,1)}, bf16[2,8,2,96,128]{4,3,2,1,0:T(8,128)(2,1)}) custom-call(s32[1]{0:T(128)} %bitcast.1.refs_0_, bf16[128,1024]{1,0:T(8,128)(2,1)} %bitcast.63, f32[1,1024]{1,0:T(1,128)} %bitcast.72, bf16[1024,2048]{1,0:T(8,128)(2,1)} %refs_4_.5, bf16[1024,2048]{1,0:T(8,128)(2,1)} %refs_4_.5, bf16[1024,2048]{1,0:T(8,128)(2,1)} %refs_4_.5, ...), custom_call_target="tpu_custom_call" | custom-call | flops 536870912 | bytes 5242880 | tf_op jit(solution)/shard_map/pallas_call | solution.py:88
  18.8 1.8 shard_map.190
  20.7 7.8 %all-to-all-start = ((bf16[32,96,128]{2,1,0:T(8,128)(2,1)}), bf16[32,96,128]{2,1,0:T(8,128)(2,1)S(1)}, u32[]{:S(2)}, u32[]{:S(2)}) async-start(bf16[32,96,128]{2,1,0:T(8,128)(2,1)} %bitcast.62), calls=%async_computation | async-start | bytes 1572864 | tf_op jit(solution)/shard_map/all_to_all | solution.py:886
  30.8 12.1 %all-to-all-done.refs_1_ = bf16[32,96,128]{2,1,0:T(8,128)(2,1)S(1)} async-done(((bf16[32,96,128]{2,1,0:T(8,128)(2,1)}), bf16[32,96,128]{2,1,0:T(8,128)(2,1)S(1)}, u32[]{:S(2)}, u32[]{:S(2)}) %all-to-all-start) | async-done | bytes 786464 | tf_op jit(solution)/shard_map/all_to_all | solution.py:886
  43.0 6.2 %shard_map.191 = (bf16[32,32,128]{2,1,0:T(8,128)(2,1)}, f32[4,64,512]{2,1,0:T(8,128)}, f32[4,8,512]{2,1,0:T(8,128)}) custom-call(s32[2]{0:T(128)S(1)} %pad_add_fusion.refs_0_, bf16[32,96,128]{2,1,0:T(8,128)(2,1)S(1)} %all-to-all-done.refs_1_, bf16[8,128]{1,0:T(8,128)(2,1)S(1)} %slice.54.refs_2_), custom_call_target="tpu_custom_call" | custom-call | flops 1342177280 | bytes 2097152 | tf_op jit(solution)/shard_map/pallas_call | solution.py:88
  49.1 5.3 %all-to-all-start.1 = ((bf16[32,32,128]{2,1,0:T(8,128)(2,1)}), bf16[32,32,128]{2,1,0:T(8,128)(2,1)S(1)}, u32[]{:S(2)}, u32[]{:S(2)}) async-start(bf16[32,32,128]{2,1,0:T(8,128)(2,1)} %get-tuple-element.44.refs_1_), calls=%async_computation.1 | async-start | bytes 524288 | tf_op jit(solution)/shard_map/all_to_all | solution.py:886
  55.1 2.7 collective-permute-start.2
  57.9 3.0 collective-permute-done.2
  60.9 3.1 all-to-all-done.1
  64.0 4.7 %shard_map.192 = (bf16[128,1024]{1,0:T(8,128)(2,1)}, f32[128,1024]{1,0:T(8,128)}, bf16[32,48,1024]{2,1,0:T(8,128)(2,1)}) custom-call(bf16[2,8,2,32,128]{4,3,2,1,0:T(8,128)(2,1)S(1)} %bitcast.48, bf16[1024,1024]{1,0:T(8,128)(2,1)} %refs_9_.1, bf16[1024,1024]{1,0:T(8,128)(2,1)} %refs_9_.1, bf16[1024,1024]{1,0:T(8,128)(2,1)} %refs_9_.1, ...), custom_call_target="tpu_custom_call" | custom-call | flops 671088640 | bytes 6291456 | tf_op jit(solution)/shard_map/pallas_call | solution.py:88
  68.7 7.6 %all-to-all-start.2 = ((bf16[32,48,1024]{2,1,0:T(8,128)(2,1)}), bf16[32,48,1024]{2,1,0:T(8,128)(2,1)S(1)}, u32[]{:S(2)}, u32[]{:S(2)}) async-start(bf16[32,48,1024]{2,1,0:T(8,128)(2,1)} %get-tuple-element.47), calls=%async_computation.2 | async-start | bytes 6291456 | tf_op jit(solution)/shard_map/all_to_all | solution.py:894
  76.3 9.4 %collective-permute-start.3 = (bf16[128,1024]{1,0:T(8,128)(2,1)}, bf16[128,1024]{1,0:T(8,128)(2,1)S(1)}, u32[]{:S(2)}, u32[]{:S(2)}) collective-permute-start(bf16[128,1024]{1,0:T(8,128)(2,1)} %get-tuple-element.48.refs_0_), channel_id=1, source_target_pairs={{0,32},{32,0},{1,33},{33,1},{2,34},{34,2},{3,35},{35,3},{4,36},{36... | collective-permute-start | bytes 786440 | tf_op jit(solution)/shard_map/ppermute | solution.py:920
  87.5 47.0 %all-to-all-done.2 = bf16[32,48,1024]{2,1,0:T(8,128)(2,1)S(1)} async-done(((bf16[32,48,1024]{2,1,0:T(8,128)(2,1)}), bf16[32,48,1024]{2,1,0:T(8,128)(2,1)S(1)}, u32[]{:S(2)}, u32[]{:S(2)}) %all-to-all-start.2) | async-done | bytes 3145760 | tf_op jit(solution)/shard_map/all_to_all | solution.py:894
  134.6 15.3 %shard_map.193 = (bf16[1536,1024]{1,0:T(8,128)(2,1)}, bf16[1536,1024]{1,0:T(8,128)(2,1)}, bf16[1536,1024]{1,0:T(8,128)(2,1)}, bf16[1536,512]{1,0:T(8,128)(2,1)}) custom-call(s32[2]{0:T(128)S(1)} %pad_add_fusion.1.refs_0_, bf16[1536,1024]{1,0:T(8,128)(2,1)S(1)} %bitcast.45, bf16[16,2,144,1024]{3,2,1,0:T(8,128)(2,1)} %bitcast.51, ...), custom_call_target="tpu_custom_call" | custom-call | flops 8858370048 | bytes 27262976 | tf_op jit(solution)/shard_map/pallas_call | solution.py:88
  150.0 9.6 %all-to-all-start.3 = ((bf16[32,48,1024]{2,1,0:T(8,128)(2,1)}), bf16[32,48,1024]{2,1,0:T(8,128)(2,1)S(1)}, u32[]{:S(2)}, u32[]{:S(2)}) async-start(bf16[32,48,1024]{2,1,0:T(8,128)(2,1)} %bitcast.61), calls=%async_computation.3 | async-start | bytes 6291456 | tf_op jit(solution)/shard_map/all_to_all | solution.py:894
  159.9 1.9 copy-done.1
  161.8 11.0 %shard_map.194 = (bf16[768,1024]{1,0:T(8,128)(2,1)}, bf16[768,1024]{1,0:T(8,128)(2,1)}) custom-call(s32[1]{0:T(128)} %bitcast.7.refs_0_, bf16[1536,1024]{1,0:T(8,128)(2,1)S(1)} %bitcast.46, bf16[1536,1024]{1,0:T(8,128)(2,1)} %get-tuple-element.51.refs_2_.refs_1_, bf16[1536,512]{1,0:T(8,128)(2,1)} %get-tuple-element.52.refs_3_.refs_2_, ...), custom_call_target="tpu_custom_call" | custom-call | flops 4831838208 | bytes 16777216 | tf_op jit(solution)/shard_map/pallas_call | solution.py:88
  173.9 3.2 collective-permute-done.4
  179.7 8.2 %shard_map.195.refs_11_ = bf16[16,2,128,1024]{3,2,1,0:T(8,128)(2,1)} custom-call(s32[2]{0:T(128)S(1)} %pad_add_fusion.1.refs_0_, bf16[16,2,144,1024]{3,2,1,0:T(8,128)(2,1)} %bitcast.53, bf16[1536,512]{1,0:T(8,128)(2,1)} %get-tuple-element.52.refs_3_.refs_2_, bf16[512,1024]{1,0:T(8,128)(2,1)} %bitcast.56, bf16[512,1024]{1,0:T(8,128)(2,1)} %bitcast.57), custom_call_target="tpu_custom_call" | custom-call | flops 2415919104 | bytes 12582912 | tf_op jit(solution)/shard_map/pallas_call | solution.py:88
  187.8 5.1 %collective-permute-done.5 = bf16[256,1024]{1,0:T(8,128)(2,1)S(1)} collective-permute-done((bf16[256,1024]{1,0:T(8,128)(2,1)S(1)}, bf16[256,1024]{1,0:T(8,128)(2,1)S(1)}, u32[]{:S(2)}, u32[]{:S(2)}) %collective-permute-start.5) | collective-permute-done | bytes 524320 | tf_op jit(solution)/shard_map/ppermute | solution.py:952
  193.9 10.5 %all-to-all-done.3.refs_1_ = bf16[32,48,1024]{2,1,0:T(8,128)(2,1)S(1)} async-done(((bf16[32,48,1024]{2,1,0:T(8,128)(2,1)}), bf16[32,48,1024]{2,1,0:T(8,128)(2,1)S(1)}, u32[]{:S(2)}, u32[]{:S(2)}) %all-to-all-start.3) | async-done | bytes 3145760 | tf_op jit(solution)/shard_map/all_to_all | solution.py:894
  204.4 4.2 %shard_map.196 = (f32[128,1024]{1,0:T(8,128)}, bf16[128,512]{1,0:T(8,128)(2,1)}, bf16[128,512]{1,0:T(8,128)(2,1)}, bf16[2,8,2,48,128]{4,3,2,1,0:T(8,128)(2,1)}) custom-call(s32[1]{0:T(128)} %bitcast.7.refs_0_, bf16[32,48,1024]{2,1,0:T(8,128)(2,1)S(1)} %all-to-all-done.3.refs_1_, s32[32,128]{1,0:T(8,128)} %get-tuple-element.45.refs_7_.refs_2_, ...), custom_call_target="tpu_custom_call" | custom-call | flops 671088640 | bytes 6291456 | tf_op jit(solution)/shard_map/pallas_call | solution.py:88
  208.6 4.3 %all-to-all-start.4 = ((bf16[32,48,128]{2,1,0:T(8,128)(2,1)}), bf16[32,48,128]{2,1,0:T(8,128)(2,1)S(1)}, u32[]{:S(2)}, u32[]{:S(2)}) async-start(bf16[32,48,128]{2,1,0:T(8,128)(2,1)} %bitcast.20), calls=%async_computation.4 | async-start | bytes 786432 | tf_op jit(solution)/shard_map/all_to_all | solution.py:886
  212.9 2.1 collective-permute-start.6
  216.0 3.7 shard_map.197
  219.7 6.9 %all-to-all-done.4.refs_1_.refs_2_ = bf16[32,48,128]{2,1,0:T(8,128)(2,1)S(1)} async-done(((bf16[32,48,128]{2,1,0:T(8,128)(2,1)}), bf16[32,48,128]{2,1,0:T(8,128)(2,1)S(1)}, u32[]{:S(2)}, u32[]{:S(2)}) %all-to-all-start.4) | async-done | bytes 393248 | tf_op jit(solution)/shard_map/all_to_all | solution.py:886
  226.6 6.7 %all-to-all-start.5 = ((bf16[64,16,512]{2,1,0:T(8,128)(2,1)}), bf16[64,16,512]{2,1,0:T(8,128)(2,1)S(1)}, u32[]{:S(2)}, u32[]{:S(2)}) async-start(bf16[64,16,512]{2,1,0:T(8,128)(2,1)} %shard_map.198.refs_7_.refs_1_), calls=%async_computation.5 | async-start | bytes 2097152 | tf_op jit(solution)/shard_map/all_to_all | solution.py:898
  233.3 2.7 add_convert_fusion.1.refs_0_
  237.2 14.3 %shard_map.199 = (bf16[32,96,128]{2,1,0:T(8,128)(2,1)}, f32[8,128]{1,0:T(8,128)}) custom-call(s32[2]{0:T(128)S(1)} %pad_add_fusion.refs_0_, bf16[32,96,128]{2,1,0:T(8,128)(2,1)S(1)} %copy-done.4, bf16[32,48,128]{2,1,0:T(8,128)(2,1)S(1)} %all-to-all-done.4.refs_1_.refs_2_, f32[4,64,512]{2,1,0:T(8,128)} %get-tuple-element.57.refs_3_, ...), custom_call_target="tpu_custom_call" | custom-call | flops 3355443200 | bytes 3145728 | tf_op jit(solution)/shard_map/pallas_call | solution.py:88
  251.4 5.9 %shard_map.202.refs_1_ = bf16[16,80,256]{2,1,0:T(8,128)(2,1)} custom-call(s32[2]{0:T(128)S(1)} %pad_add_fusion.2.refs_0_, bf16[16,2,64,1024]{3,2,1,0:T(8,128)(2,1)} %bitcast.58, bf16[32,96,128]{2,1,0:T(8,128)(2,1)} %get-tuple-element.61.refs_2_.refs_0_, f32[8,128]{1,0:T(8,128)} %get-tuple-element.62.refs_3_), custom_call_target="tpu_custom_call" | custom-call | flops 1073741824 | bytes 6291456 | tf_op jit(solution)/shard_map/pallas_call | solution.py:88
  257.3 2.0 copy.35.refs_0_
  259.3 11.0 %all-to-all-start.6 = ((bf16[16,80,256]{2,1,0:T(8,128)(2,1)}), bf16[16,80,256]{2,1,0:T(8,128)(2,1)S(1)}, u32[]{:S(2)}, u32[]{:S(2)}) async-start(bf16[16,80,256]{2,1,0:T(8,128)(2,1)} %shard_map.203), calls=%async_computation.6 | async-start | bytes 1310720 | tf_op jit(solution)/shard_map/all_to_all | solution.py:974
  270.3 1.7 add_convert_fusion
  273.0 15.6 %all-to-all-done.6.refs_0_ = bf16[16,80,256]{2,1,0:T(8,128)(2,1)S(1)} async-done(((bf16[16,80,256]{2,1,0:T(8,128)(2,1)}), bf16[16,80,256]{2,1,0:T(8,128)(2,1)S(1)}, u32[]{:S(2)}, u32[]{:S(2)}) %all-to-all-start.6) | async-done | bytes 655392 | tf_op jit(solution)/shard_map/all_to_all | solution.py:974
  288.6 2.0 shard_map.206
  290.6 7.5 %all-to-all-start.7 = ((bf16[64,96,256]{2,1,0:T(8,128)(2,1)}), bf16[64,96,256]{2,1,0:T(8,128)(2,1)S(1)}, u32[]{:S(2)}, u32[]{:S(2)}) async-start(bf16[64,96,256]{2,1,0:T(8,128)(2,1)} %get-tuple-element.63), calls=%async_computation.7 | async-start | bytes 6291456 | tf_op jit(solution)/shard_map/all_to_all | solution.py:898
  300.9 3.0 collective-permute-done.8.refs_2_
  304.0 3.8 %shard_map.207 = (f32[1024,1024]{1,0:T(8,128)}, f32[512,1024]{1,0:T(8,128)}) custom-call(s32[1]{0:T(128)} %bitcast.7.refs_0_, bf16[768,1024]{1,0:T(8,128)(2,1)S(1)} %pad_maximum_fusion.refs_1_, bf16[768,1024]{1,0:T(8,128)(2,1)S(1)} %collective-permute-done.8.refs_2_), custom_call_target="tpu_custom_call" | custom-call | bytes 9437184 | tf_op jit(solution)/shard_map/pallas_call | solution.py:88
  307.8 29.7 %all-to-all-done.7.refs_0_ = bf16[64,96,256]{2,1,0:T(8,128)(2,1)S(1)} async-done(((bf16[64,96,256]{2,1,0:T(8,128)(2,1)}), bf16[64,96,256]{2,1,0:T(8,128)(2,1)S(1)}, u32[]{:S(2)}, u32[]{:S(2)}) %all-to-all-start.7) | async-done | bytes 3145760 | tf_op jit(solution)/shard_map/all_to_all | solution.py:898
  337.5 5.2 %collective-permute-start.10 = (bf16[64,96,256]{2,1,0:T(8,128)(2,1)S(1)}, bf16[64,96,256]{2,1,0:T(8,128)(2,1)}, u32[]{:S(2)}, u32[]{:S(2)}) collective-permute-start(bf16[64,96,256]{2,1,0:T(8,128)(2,1)S(1)} %shard_map.208), channel_id=1, source_target_pairs={{0,32},{32,0},{1,33},{33,1},{2,34},{34,2},{3,35},{35,3},{4,36},{36... | collective-permute-start | bytes 9437192 | tf_op jit(solution)/shard_map/ppermute | solution.py:920
  342.7 6.1 %all-to-all-start.8 = ((bf16[32,96,128]{2,1,0:T(8,128)(2,1)}), bf16[32,96,128]{2,1,0:T(8,128)(2,1)}, u32[]{:S(2)}, u32[]{:S(2)}) async-start(bf16[32,96,128]{2,1,0:T(8,128)(2,1)} %shard_map.209), calls=%async_computation.8 | async-start | bytes 1572864 | tf_op jit(solution)/shard_map/all_to_all | solution.py:886
  348.8 1.7 slice.63
  350.5 3.5 collective-permute-start.9
  354.0 5.1 %shard_map.211 = (f32[1024,2048]{1,0:T(8,128)}, f32[4,8,2,16,1024]{4,3,2,1,0:T(8,128)}, f32[8,128]{1,0:T(8,128)}) custom-call(s32[1]{0:T(128)} %bitcast.7.refs_0_, bf16[2,2,8,2,96,256]{5,4,3,2,1,0:T(8,128)(2,1)S(1)} %bitcast.44, bf16[1024,2048]{1,0:T(8,128)(2,1)} %refs_4_.5, f32[8,128]{1,0:T(8,128)} %bitcast.73), custom_call_target="tpu_custom_call" | custom-call | bytes 16777216 | tf_op jit(solution)/shard_map/pallas_call | solution.py:88
  359.2 6.0 %shard_map.212 = (f32[1024,2048]{1,0:T(8,128)}, f32[4,8,2,16,1024]{4,3,2,1,0:T(8,128)}, f32[8,128]{1,0:T(8,128)}) custom-call(s32[1]{0:T(128)S(6)} %sub.7.refs_0_, bf16[2,2,8,2,96,256]{5,4,3,2,1,0:T(8,128)(2,1)} %bitcast.30.refs_1_, bf16[1024,2048]{1,0:T(8,128)(2,1)} %refs_4_.5, f32[8,128]{1,0:T(8,128)} %bitcast.74, ...), custom_call_target="tpu_custom_call", output_to_operand_aliasing={{0}: (5, {}), {1}: (6, {})} | custom-call | bytes 16777216 | tf_op jit(solution)/shard_map/pallas_call | solution.py:88
  365.2 2.7 collective-permute-done.9.refs_10_
  367.9 5.3 %shard_map.213 = (f32[128,1024]{1,0:T(8,128)}, bf16[128,1024]{1,0:T(8,128)(2,1)}) custom-call(bf16[2,8,2,96,128]{4,3,2,1,0:T(8,128)(2,1)} %bitcast.27.refs_0_, bf16[1024,2048]{1,0:T(8,128)(2,1)} %refs_4_.5, bf16[1024,2048]{1,0:T(8,128)(2,1)} %refs_4_.5, bf16[1024,2048]{1,0:T(8,128)(2,1)} %refs_4_.5, bf16[1024,2048]{1,0:T(8,128)(2,1)} %refs_4_.5, ...), custom_call_target="tpu_custom_call" | custom-call | flops 536870912 | bytes 6291456 | tf_op jit(solution)/shard_map/pallas_call | solution.py:88
  (72 shorter events, 17.6 us)
Async XLA Ops:
  7.2 127.4 %all-gather.5.cloned.1.call-start = ((), (), s32[]{:S(2)}) async-start(), calls=%async_computation.11 | async-start | bytes 10027008 | tf_op jit(solution)/shard_map/all_gather | solution.py:929
  7.2 11.6 %collective-permute-start = (bf16[128,1024]{1,0:T(8,128)(2,1)}, bf16[128,1024]{1,0:T(8,128)(2,1)S(1)}, u32[]{:S(2)}, u32[]{:S(2)}) collective-permute-start(bf16[128,1024]{1,0:T(8,128)(2,1)} %bitcast.67), channel_id=1, source_target_pairs={{0,65},{1,64},{64,1},{65,0},{2,67},{3,66},{66,3},{67,2},{4,69},{5,... | collective-permute-start | bytes 786440 | tf_op jit(solution)/shard_map/ppermute | solution.py:922
  13.4 5.4 %collective-permute-start.1 = (bf16[16,1024]{1,0:T(8,128)(2,1)}, bf16[16,1024]{1,0:T(8,128)(2,1)S(1)}, u32[]{:S(2)}, u32[]{:S(2)}) collective-permute-start(bf16[16,1024]{1,0:T(8,128)(2,1)} %get-tuple-element.42.refs_8_.refs_1_), channel_id=1, source_target_pairs={{0,65},{1,64},{64,1},{65,0},{2,67},{3,66},{66,3},{67,2},{4,69},{5,... | collective-permute-start | bytes 98312 | tf_op jit(solution)/shard_map/ppermute | solution.py:924
  18.6 9.9 %copy-start.11 = (s32[2]{0:T(128)S(1)}, s32[2]{0:T(128)}, u32[]{:S(2)}) copy-start(s32[2]{0:T(128)} %param.14) | copy-start | bytes 28
  20.7 22.3 %all-to-all-start = ((bf16[32,96,128]{2,1,0:T(8,128)(2,1)}), bf16[32,96,128]{2,1,0:T(8,128)(2,1)S(1)}, u32[]{:S(2)}, u32[]{:S(2)}) async-start(bf16[32,96,128]{2,1,0:T(8,128)(2,1)} %bitcast.62), calls=%async_computation | async-start | bytes 1572864 | tf_op jit(solution)/shard_map/all_to_all | solution.py:886
  28.5 26.0 %copy-start.9 = (bf16[128,1024]{1,0:T(8,128)(2,1)S(1)}, bf16[128,1024]{1,0:T(8,128)(2,1)}, u32[]{:S(2)}) copy-start(bf16[128,1024]{1,0:T(8,128)(2,1)} %get-tuple-element.46) | copy-start | bytes 786436
  43.0 6.2 %copy-start.3 = (bf16[32,96,128]{2,1,0:T(8,128)(2,1)}, bf16[32,96,128]{2,1,0:T(8,128)(2,1)S(1)}, u32[]{:S(2)}) copy-start(bf16[32,96,128]{2,1,0:T(8,128)(2,1)S(1)} %all-to-all-done.refs_1_) | copy-start | bytes 2359300
  49.1 14.8 %all-to-all-start.1 = ((bf16[32,32,128]{2,1,0:T(8,128)(2,1)}), bf16[32,32,128]{2,1,0:T(8,128)(2,1)S(1)}, u32[]{:S(2)}, u32[]{:S(2)}) async-start(bf16[32,32,128]{2,1,0:T(8,128)(2,1)} %get-tuple-element.44.refs_1_), calls=%async_computation.1 | async-start | bytes 524288 | tf_op jit(solution)/shard_map/all_to_all | solution.py:886
  55.1 5.8 %collective-permute-start.2 = (bf16[64,1024]{1,0:T(8,128)(2,1)S(1)}, bf16[64,1024]{1,0:T(8,128)(2,1)S(1)}, u32[]{:S(2)}, u32[]{:S(2)}) collective-permute-start(bf16[64,1024]{1,0:T(8,128)(2,1)S(1)} %get-tuple-element.77), channel_id=1, source_target_pairs={{0,1},{1,0},{2,3},{3,2},{4,5},{5,4},{6,7},{7,6},{8,9},{9,8},{10,11... | collective-permute-start | bytes 393224 | tf_op jit(solution)/shard_map/ppermute | solution.py:934
  68.7 65.8 %all-to-all-start.2 = ((bf16[32,48,1024]{2,1,0:T(8,128)(2,1)}), bf16[32,48,1024]{2,1,0:T(8,128)(2,1)S(1)}, u32[]{:S(2)}, u32[]{:S(2)}) async-start(bf16[32,48,1024]{2,1,0:T(8,128)(2,1)} %get-tuple-element.47), calls=%async_computation.2 | async-start | bytes 6291456 | tf_op jit(solution)/shard_map/all_to_all | solution.py:894
  76.3 175.1 %all-gather.7.cloned.1.call-start = ((), (), s32[]{:S(2)}) async-start(), calls=%async_computation.12 | async-start | bytes 4456448 | tf_op jit(solution)/shard_map/all_gather | solution.py:944
  76.3 11.1 %collective-permute-start.3 = (bf16[128,1024]{1,0:T(8,128)(2,1)}, bf16[128,1024]{1,0:T(8,128)(2,1)S(1)}, u32[]{:S(2)}, u32[]{:S(2)}) collective-permute-start(bf16[128,1024]{1,0:T(8,128)(2,1)} %get-tuple-element.48.refs_0_), channel_id=1, source_target_pairs={{0,32},{32,0},{1,33},{33,1},{2,34},{34,2},{3,35},{35,3},{4,36},{36... | collective-permute-start | bytes 786440 | tf_op jit(solution)/shard_map/ppermute | solution.py:920
  134.4 15.5 %copy-start = (bf16[32,48,1024]{2,1,0:T(8,128)(2,1)}, bf16[32,48,1024]{2,1,0:T(8,128)(2,1)S(1)}, u32[]{:S(2)}) copy-start(bf16[32,48,1024]{2,1,0:T(8,128)(2,1)S(1)} %all-to-all-done.2) | copy-start | bytes 9437188
  150.0 54.4 %all-to-all-start.3 = ((bf16[32,48,1024]{2,1,0:T(8,128)(2,1)}), bf16[32,48,1024]{2,1,0:T(8,128)(2,1)S(1)}, u32[]{:S(2)}, u32[]{:S(2)}) async-start(bf16[32,48,1024]{2,1,0:T(8,128)(2,1)} %bitcast.61), calls=%async_computation.3 | async-start | bytes 6291456 | tf_op jit(solution)/shard_map/all_to_all | solution.py:894
  159.7 189.2 %reduce-scatter.2.cloned.1.call-start = ((), (), s32[]{:S(2)}) async-start(), calls=%async_computation.10 | async-start | bytes 8912896 | tf_op jit(solution)/shard_map/reduce_scatter | solution.py:958
  159.9 1.9 copy-start.1
  172.8 4.4 %collective-permute-start.4 = (bf16[768,1024]{1,0:T(8,128)(2,1)}, bf16[768,1024]{1,0:T(8,128)(2,1)S(1)}, u32[]{:S(2)}, u32[]{:S(2)}) collective-permute-start(bf16[768,1024]{1,0:T(8,128)(2,1)} %get-tuple-element.55), channel_id=1, source_target_pairs={{0,32},{32,0},{1,33},{33,1},{2,34},{34,2},{3,35},{35,3},{4,36},{36... | collective-permute-start | bytes 4718600 | tf_op jit(solution)/shard_map/ppermute | solution.py:920
  177.2 1.1 copy-start.8
  179.6 13.3 %collective-permute-start.5 = (bf16[256,1024]{1,0:T(8,128)(2,1)S(1)}, bf16[256,1024]{1,0:T(8,128)(2,1)S(1)}, u32[]{:S(2)}, u32[]{:S(2)}) collective-permute-start(bf16[256,1024]{1,0:T(8,128)(2,1)S(1)} %add_convert_fusion.3), channel_id=1, source_target_pairs={{0,64},{64,0},{1,65},{65,1},{2,66},{66,2},{3,67},{67,3},{4,68},{68... | collective-permute-start | bytes 1572872 | tf_op jit(solution)/shard_map/ppermute | solution.py:952
  193.1 0.8 copy-start.6
  208.6 4.3 %copy-start.10 = (bf16[128,512]{1,0:T(8,128)(2,1)S(1)}, bf16[128,512]{1,0:T(8,128)(2,1)}, u32[]{:S(2)}) copy-start(bf16[128,512]{1,0:T(8,128)(2,1)} %get-tuple-element.60) | copy-start | bytes 393220
  208.6 18.0 %all-to-all-start.4 = ((bf16[32,48,128]{2,1,0:T(8,128)(2,1)}), bf16[32,48,128]{2,1,0:T(8,128)(2,1)S(1)}, u32[]{:S(2)}, u32[]{:S(2)}) async-start(bf16[32,48,128]{2,1,0:T(8,128)(2,1)} %bitcast.20), calls=%async_computation.4 | async-start | bytes 786432 | tf_op jit(solution)/shard_map/all_to_all | solution.py:886
  212.9 20.3 %copy-start.7 = (bf16[768,1024]{1,0:T(8,128)(2,1)S(1)}, bf16[768,1024]{1,0:T(8,128)(2,1)}, u32[]{:S(2)}) copy-start(bf16[768,1024]{1,0:T(8,128)(2,1)} %get-tuple-element.54) | copy-start | bytes 4718596
  212.9 3.0 collective-permute-start.6
  226.6 32.7 %all-to-all-start.5 = ((bf16[64,16,512]{2,1,0:T(8,128)(2,1)}), bf16[64,16,512]{2,1,0:T(8,128)(2,1)S(1)}, u32[]{:S(2)}, u32[]{:S(2)}) async-start(bf16[64,16,512]{2,1,0:T(8,128)(2,1)} %shard_map.198.refs_7_.refs_1_), calls=%async_computation.5 | async-start | bytes 2097152 | tf_op jit(solution)/shard_map/all_to_all | solution.py:898
  233.3 3.9 %copy-start.4 = (bf16[32,96,128]{2,1,0:T(8,128)(2,1)S(1)}, bf16[32,96,128]{2,1,0:T(8,128)(2,1)}, u32[]{:S(2)}) copy-start(bf16[32,96,128]{2,1,0:T(8,128)(2,1)} %copy-done.3) | copy-start | bytes 2359300
  236.0 34.3 %collective-permute-start.7 = (bf16[512,1024]{1,0:T(8,128)(2,1)}, bf16[512,1024]{1,0:T(8,128)(2,1)S(1)}, u32[]{:S(2)}, u32[]{:S(2)}) collective-permute-start(bf16[512,1024]{1,0:T(8,128)(2,1)} %shard_map.204.refs_0_), channel_id=1, source_target_pairs={{0,64},{64,0},{1,65},{65,1},{2,66},{66,2},{3,67},{67,3},{4,68},{68... | collective-permute-start | bytes 3145736 | tf_op jit(solution)/shard_map/ppermute | solution.py:966
  259.3 29.3 %all-to-all-start.6 = ((bf16[16,80,256]{2,1,0:T(8,128)(2,1)}), bf16[16,80,256]{2,1,0:T(8,128)(2,1)S(1)}, u32[]{:S(2)}, u32[]{:S(2)}) async-start(bf16[16,80,256]{2,1,0:T(8,128)(2,1)} %shard_map.203), calls=%async_computation.6 | async-start | bytes 1310720 | tf_op jit(solution)/shard_map/all_to_all | solution.py:974
  272.0 1.0 copy-start.5
  290.6 46.9 %all-to-all-start.7 = ((bf16[64,96,256]{2,1,0:T(8,128)(2,1)}), bf16[64,96,256]{2,1,0:T(8,128)(2,1)S(1)}, u32[]{:S(2)}, u32[]{:S(2)}) async-start(bf16[64,96,256]{2,1,0:T(8,128)(2,1)} %get-tuple-element.63), calls=%async_computation.7 | async-start | bytes 6291456 | tf_op jit(solution)/shard_map/all_to_all | solution.py:898
  299.6 4.3 %collective-permute-start.8 = (bf16[768,1024]{1,0:T(8,128)(2,1)S(1)}, bf16[768,1024]{1,0:T(8,128)(2,1)S(1)}, u32[]{:S(2)}, u32[]{:S(2)}) collective-permute-start(bf16[768,1024]{1,0:T(8,128)(2,1)S(1)} %pad_maximum_fusion.refs_1_), channel_id=1, source_target_pairs={{0,32},{32,0},{1,33},{33,1},{2,34},{34,2},{3,35},{35,3},{4,36},{36... | collective-permute-start | bytes 4718600 | tf_op jit(solution)/shard_map/ppermute | solution.py:920
  337.5 21.7 %collective-permute-start.10 = (bf16[64,96,256]{2,1,0:T(8,128)(2,1)S(1)}, bf16[64,96,256]{2,1,0:T(8,128)(2,1)}, u32[]{:S(2)}, u32[]{:S(2)}) collective-permute-start(bf16[64,96,256]{2,1,0:T(8,128)(2,1)S(1)} %shard_map.208), channel_id=1, source_target_pairs={{0,32},{32,0},{1,33},{33,1},{2,34},{34,2},{3,35},{35,3},{4,36},{36... | collective-permute-start | bytes 9437192 | tf_op jit(solution)/shard_map/ppermute | solution.py:920
  342.7 22.5 %all-to-all-start.8 = ((bf16[32,96,128]{2,1,0:T(8,128)(2,1)}), bf16[32,96,128]{2,1,0:T(8,128)(2,1)}, u32[]{:S(2)}, u32[]{:S(2)}) async-start(bf16[32,96,128]{2,1,0:T(8,128)(2,1)} %shard_map.209), calls=%async_computation.8 | async-start | bytes 1572864 | tf_op jit(solution)/shard_map/all_to_all | solution.py:886
  350.5 17.4 %collective-permute-start.9 = (bf16[128,1024]{1,0:T(8,128)(2,1)}, bf16[128,1024]{1,0:T(8,128)(2,1)S(1)}, u32[]{:S(2)}, u32[]{:S(2)}) collective-permute-start(bf16[128,1024]{1,0:T(8,128)(2,1)} %slice.63), channel_id=1, source_target_pairs={{0,65},{1,64},{64,1},{65,0},{2,67},{3,66},{66,3},{67,2},{4,69},{5,... | collective-permute-start | bytes 786440 | tf_op jit(solution)/shard_map/ppermute | solution.py:959
  359.2 8.7 %copy-start.2 = (bf16[256,1024]{1,0:T(8,128)(2,1)S(1)}, bf16[256,1024]{1,0:T(8,128)(2,1)}, u32[]{:S(2)}) copy-start(bf16[256,1024]{1,0:T(8,128)(2,1)} %reduce-scatter.2.cloned.1.call-done) | copy-start | bytes 1572868
Sparse Core Ops, SparseCore 0:
  20.8 113.7 all-gather.4
  150.1 83.3 all-gather.6
  237.5 109.3 reduce-scatter.1

commit v6 on v5

--- a/solution.py
+++ b/solution.py
@@ -319,17 +319,16 @@
         lse = lse_ref[tile][0:1]
         limit = limits(tile, info)
 
-        def step(c, acc):
-            at = pl.ds(pl.multiple_of(c * 256, 256), 256)
+        acc = jnp.zeros((64, 512), F32)
+        for c in range(tile + 1):
+            at = slice(c * 512, c * 512 + 512)
             part = kv[at, :]
             s = dot(part, q2, NT)
-            place = c * 256 + lax.broadcasted_iota(jnp.int32, (256, 1), 0)
+            place = c * 512 + lax.broadcasted_iota(jnp.int32, (512, 1), 0)
             p = jnp.exp(jnp.where(place <= limit, s, -1e30) - lse)
             ds = (p * (dot(part, do2, NT) - inner)).astype(BF16)
             total[at, :] += dot(ds, q2) + dot(p.astype(BF16), do2)
-            return acc + dot(kvt[0:64, at], ds)
-
-        acc = lax.fori_loop(0, 2 * tile + 2, step, jnp.zeros((64, 512), F32))
+            acc = acc + dot(kvt[0:64, at], ds)
         dq = jnp.concatenate([acc[:, :256], acc[:, 256:]], 0).T
         at = (slice(tile * 8, tile * 8 + 8), pl.ds(pl.multiple_of(info[1] * 32, 32), 32))
         c, s = cos[at].reshape(256, 128), sin[at].reshape(256, 128)
@@ -956,7 +955,6 @@
 
     sums = after(outputs.reshape(4096, 1024), hold(dbr_own))
     sums = lax.psum_scatter(sums, PLANE, tiled=True).reshape(2, 128, 1024)
-    far = lax.ppermute(sums[1], ("zl", "zh"), Z_PAIRS)
 
 
     do_recv = exchange(do.reshape(32, 48, 128))
@@ -980,6 +978,8 @@
     own = await_all(among_chips(copies), hold(grad_gate_up))
     dqkv_recv = exchange(after(dqkv, corner(own))).reshape(2, 8, 2, 96, 128)
     rows = final(which, own, w_qkv, gain_attn.reshape(8, 128))
+    sums = await_all(sums, hold(rows[0]))
+    far = lax.ppermute(sums[1], ("zl", "zh"), Z_PAIRS)
     grad_qkv, grad_out, grad_gain_attn = final(
         1 - which, to_partner(own), w_qkv, gain_attn.reshape(8, 128), (rows[2], rows[0], rows[1])
     )

time: 382 us -> 387 us (1.013)
  waiting for transfers between devices: 143 us -> 155 us
  Pallas kernels: 104 us -> 100 us
  starting transfers between devices: 97.6 us -> 93.7 us
    reduce_scatter x1, waiting for transfers between devices: 0.02 us -> 12.4 us  [shards(): sums = lax.psum_scatter(sums, PLANE, tiled=True).reshape(2, 128, 1024)]
    pallas_call x17, Pallas kernels: 104 us -> 99.9 us  [call(): built(*[place(i, x) for i, x in enumerate(operands)], *deps)]
    unnamed x25 -> x29, local copies, waits for them, and re-layouts: 6.88 us -> 8.71 us
  transfers between devices with their start and end apart: 23 -> 23, of which waited for: 15 -> 16; matrix products, arithmetic and copies ran while one was open for 4% -> 4% of each run, Pallas kernels for 22% -> 20%
where the time goes in v6:
time: 387 us; the launch traced here: 385 us
  waiting for transfers between devices  155 us (40%)
  Pallas kernels  100 us (26%)
  starting transfers between devices  93.7 us (24%)
  between operations  14 us (4%)
  local copies, waits for them, and re-layouts  12.6 us (3%)
  other arithmetic  9.79 us (3%)
    pallas_call x17, Pallas kernels, call(): built(*[place(i, x) for i, x in enumerate(operands)], *deps)  99.9 us
    all_to_all x2, waiting for transfers between devices, among_experts(): lax.all_to_all(x, CHIPS, 0, 0, tiled=True, axis_index_groups=EXPERT_GROUPS)  57.4 us
    all_to_all x2, waiting for transfers between devices, among_chips(): return lax.all_to_all(x, CHIPS, 0, 0, tiled=True)  31.3 us
    all_to_all x4, starting transfers between devices, exchange(): return lax.all_to_all(x, BLK, 0, 0, tiled=True)  23.2 us
    all_to_all x4, waiting for transfers between devices, exchange(): return lax.all_to_all(x, BLK, 0, 0, tiled=True)  22.1 us
    all_to_all x2, starting transfers between devices, among_experts(): lax.all_to_all(x, CHIPS, 0, 0, tiled=True, axis_index_groups=EXPERT_GROUPS)  17.3 us
    ppermute x5, starting transfers between devices, to_partner(): return lax.ppermute(part, 'core', SWAP)  15.9 us
    all_to_all x2, starting transfers between devices, among_chips(): return lax.all_to_all(x, CHIPS, 0, 0, tiled=True)  14.2 us
  transfers between devices with their start and end apart: 23, of which 16 were waited for; matrix products, arithmetic and copies ran while one was open for 4% of the time, Pallas kernels for 20%

profile of v6, /device:TPU:1, one launch (start us, length us, event | category | flops | bytes accessed | tf_op | source)
XLA Modules:
  0.0 384.8 jit_solution(10977524646643345397)
XLA Ops:
  7.2 4.7 %collective-permute-start = (bf16[128,1024]{1,0:T(8,128)(2,1)}, bf16[128,1024]{1,0:T(8,128)(2,1)S(1)}, u32[]{:S(2)}, u32[]{:S(2)}) collective-permute-start(bf16[128,1024]{1,0:T(8,128)(2,1)} %bitcast.69), channel_id=1, source_target_pairs={{0,65},{1,64},{64,1},{65,0},{2,67},{3,66},{66,3},{67,2},{4,69},{5,... | collective-permute-start | bytes 786440 | tf_op jit(solution)/shard_map/ppermute | solution.py:921
  13.4 5.2 %shard_map.189 = (bf16[128,1024]{1,0:T(8,128)(2,1)}, bf16[2,8,2,96,128]{4,3,2,1,0:T(8,128)(2,1)}) custom-call(s32[1]{0:T(128)} %bitcast.1.refs_0_, bf16[128,1024]{1,0:T(8,128)(2,1)} %bitcast.65, f32[1,1024]{1,0:T(1,128)} %bitcast.74, bf16[1024,2048]{1,0:T(8,128)(2,1)} %refs_4_.5, bf16[1024,2048]{1,0:T(8,128)(2,1)} %refs_4_.5, bf16[1024,2048]{1,0:T(8,128)(2,1)} %refs_4_.5, ...), custom_call_target="tpu_custom_call" | custom-call | flops 536870912 | bytes 5242880 | tf_op jit(solution)/shard_map/pallas_call | solution.py:88
  18.8 1.8 shard_map.190
  20.7 7.8 %all-to-all-start = ((bf16[32,96,128]{2,1,0:T(8,128)(2,1)}), bf16[32,96,128]{2,1,0:T(8,128)(2,1)S(1)}, u32[]{:S(2)}, u32[]{:S(2)}) async-start(bf16[32,96,128]{2,1,0:T(8,128)(2,1)} %bitcast.64), calls=%async_computation | async-start | bytes 1572864 | tf_op jit(solution)/shard_map/all_to_all | solution.py:885
  30.8 12.1 %all-to-all-done.refs_1_ = bf16[32,96,128]{2,1,0:T(8,128)(2,1)S(1)} async-done(((bf16[32,96,128]{2,1,0:T(8,128)(2,1)}), bf16[32,96,128]{2,1,0:T(8,128)(2,1)S(1)}, u32[]{:S(2)}, u32[]{:S(2)}) %all-to-all-start) | async-done | bytes 786464 | tf_op jit(solution)/shard_map/all_to_all | solution.py:885
  43.0 6.2 %shard_map.191 = (bf16[32,32,128]{2,1,0:T(8,128)(2,1)}, f32[4,64,512]{2,1,0:T(8,128)}, f32[4,8,512]{2,1,0:T(8,128)}) custom-call(s32[2]{0:T(128)S(1)} %pad_add_fusion.refs_0_, bf16[32,96,128]{2,1,0:T(8,128)(2,1)S(1)} %all-to-all-done.refs_1_, bf16[8,128]{1,0:T(8,128)(2,1)S(1)} %slice.53.refs_2_), custom_call_target="tpu_custom_call" | custom-call | flops 1342177280 | bytes 2097152 | tf_op jit(solution)/shard_map/pallas_call | solution.py:88
  49.1 5.3 %all-to-all-start.1 = ((bf16[32,32,128]{2,1,0:T(8,128)(2,1)}), bf16[32,32,128]{2,1,0:T(8,128)(2,1)S(1)}, u32[]{:S(2)}, u32[]{:S(2)}) async-start(bf16[32,32,128]{2,1,0:T(8,128)(2,1)} %get-tuple-element.44.refs_1_), calls=%async_computation.1 | async-start | bytes 524288 | tf_op jit(solution)/shard_map/all_to_all | solution.py:885
  55.1 2.7 collective-permute-start.2
  57.9 3.0 collective-permute-done.2
  60.9 3.1 all-to-all-done.1
  64.0 4.7 %shard_map.192 = (bf16[128,1024]{1,0:T(8,128)(2,1)}, f32[128,1024]{1,0:T(8,128)}, bf16[32,48,1024]{2,1,0:T(8,128)(2,1)}) custom-call(bf16[2,8,2,32,128]{4,3,2,1,0:T(8,128)(2,1)S(1)} %bitcast.50, bf16[1024,1024]{1,0:T(8,128)(2,1)} %refs_9_.1, bf16[1024,1024]{1,0:T(8,128)(2,1)} %refs_9_.1, bf16[1024,1024]{1,0:T(8,128)(2,1)} %refs_9_.1, ...), custom_call_target="tpu_custom_call" | custom-call | flops 671088640 | bytes 6291456 | tf_op jit(solution)/shard_map/pallas_call | solution.py:88
  68.7 7.6 %all-to-all-start.2 = ((bf16[32,48,1024]{2,1,0:T(8,128)(2,1)}), bf16[32,48,1024]{2,1,0:T(8,128)(2,1)S(1)}, u32[]{:S(2)}, u32[]{:S(2)}) async-start(bf16[32,48,1024]{2,1,0:T(8,128)(2,1)} %get-tuple-element.47), calls=%async_computation.2 | async-start | bytes 6291456 | tf_op jit(solution)/shard_map/all_to_all | solution.py:893
  76.3 9.4 %collective-permute-start.3 = (bf16[128,1024]{1,0:T(8,128)(2,1)}, bf16[128,1024]{1,0:T(8,128)(2,1)S(1)}, u32[]{:S(2)}, u32[]{:S(2)}) collective-permute-start(bf16[128,1024]{1,0:T(8,128)(2,1)} %get-tuple-element.48.refs_0_), channel_id=1, source_target_pairs={{0,32},{32,0},{1,33},{33,1},{2,34},{34,2},{3,35},{35,3},{4,36},{36... | collective-permute-start | bytes 786440 | tf_op jit(solution)/shard_map/ppermute | solution.py:919
  87.5 46.9 %all-to-all-done.2 = bf16[32,48,1024]{2,1,0:T(8,128)(2,1)S(1)} async-done(((bf16[32,48,1024]{2,1,0:T(8,128)(2,1)}), bf16[32,48,1024]{2,1,0:T(8,128)(2,1)S(1)}, u32[]{:S(2)}, u32[]{:S(2)}) %all-to-all-start.2) | async-done | bytes 3145760 | tf_op jit(solution)/shard_map/all_to_all | solution.py:893
  134.6 15.3 %shard_map.193 = (bf16[1536,1024]{1,0:T(8,128)(2,1)}, bf16[1536,1024]{1,0:T(8,128)(2,1)}, bf16[1536,1024]{1,0:T(8,128)(2,1)}, bf16[1536,512]{1,0:T(8,128)(2,1)}) custom-call(s32[2]{0:T(128)S(1)} %pad_add_fusion.1.refs_0_, bf16[1536,1024]{1,0:T(8,128)(2,1)S(1)} %bitcast.48, bf16[16,2,144,1024]{3,2,1,0:T(8,128)(2,1)} %bitcast.53, ...), custom_call_target="tpu_custom_call" | custom-call | flops 8858370048 | bytes 27262976 | tf_op jit(solution)/shard_map/pallas_call | solution.py:88
  150.0 9.6 %all-to-all-start.3 = ((bf16[32,48,1024]{2,1,0:T(8,128)(2,1)}), bf16[32,48,1024]{2,1,0:T(8,128)(2,1)S(1)}, u32[]{:S(2)}, u32[]{:S(2)}) async-start(bf16[32,48,1024]{2,1,0:T(8,128)(2,1)} %bitcast.63), calls=%async_computation.3 | async-start | bytes 6291456 | tf_op jit(solution)/shard_map/all_to_all | solution.py:893
  159.9 1.9 copy-done.4
  161.8 11.0 %shard_map.194 = (bf16[768,1024]{1,0:T(8,128)(2,1)}, bf16[768,1024]{1,0:T(8,128)(2,1)}) custom-call(s32[1]{0:T(128)} %bitcast.7.refs_0_, bf16[1536,1024]{1,0:T(8,128)(2,1)S(1)} %bitcast.49, bf16[1536,1024]{1,0:T(8,128)(2,1)} %get-tuple-element.51.refs_2_.refs_1_, bf16[1536,512]{1,0:T(8,128)(2,1)} %get-tuple-element.52.refs_3_.refs_2_, ...), custom_call_target="tpu_custom_call" | custom-call | flops 4831838208 | bytes 16777216 | tf_op jit(solution)/shard_map/pallas_call | solution.py:88
  173.9 3.2 collective-permute-done.4
  179.6 8.2 %shard_map.195.refs_11_ = bf16[16,2,128,1024]{3,2,1,0:T(8,128)(2,1)} custom-call(s32[2]{0:T(128)S(1)} %pad_add_fusion.1.refs_0_, bf16[16,2,144,1024]{3,2,1,0:T(8,128)(2,1)} %bitcast.55, bf16[1536,512]{1,0:T(8,128)(2,1)} %get-tuple-element.52.refs_3_.refs_2_, bf16[512,1024]{1,0:T(8,128)(2,1)} %bitcast.58, bf16[512,1024]{1,0:T(8,128)(2,1)} %bitcast.59), custom_call_target="tpu_custom_call" | custom-call | flops 2415919104 | bytes 12582912 | tf_op jit(solution)/shard_map/pallas_call | solution.py:88
  187.8 5.0 %collective-permute-done.5 = bf16[256,1024]{1,0:T(8,128)(2,1)S(1)} collective-permute-done((bf16[256,1024]{1,0:T(8,128)(2,1)S(1)}, bf16[256,1024]{1,0:T(8,128)(2,1)S(1)}, u32[]{:S(2)}, u32[]{:S(2)}) %collective-permute-start.5) | collective-permute-done | bytes 524320 | tf_op jit(solution)/shard_map/ppermute | solution.py:951
  193.9 10.5 %all-to-all-done.3.refs_1_ = bf16[32,48,1024]{2,1,0:T(8,128)(2,1)S(1)} async-done(((bf16[32,48,1024]{2,1,0:T(8,128)(2,1)}), bf16[32,48,1024]{2,1,0:T(8,128)(2,1)S(1)}, u32[]{:S(2)}, u32[]{:S(2)}) %all-to-all-start.3) | async-done | bytes 3145760 | tf_op jit(solution)/shard_map/all_to_all | solution.py:893
  204.4 4.2 %shard_map.196 = (f32[128,1024]{1,0:T(8,128)}, bf16[128,512]{1,0:T(8,128)(2,1)}, bf16[128,512]{1,0:T(8,128)(2,1)}, bf16[2,8,2,48,128]{4,3,2,1,0:T(8,128)(2,1)}) custom-call(s32[1]{0:T(128)} %bitcast.7.refs_0_, bf16[32,48,1024]{2,1,0:T(8,128)(2,1)S(1)} %all-to-all-done.3.refs_1_, s32[32,128]{1,0:T(8,128)} %get-tuple-element.45.refs_7_.refs_2_, ...), custom_call_target="tpu_custom_call" | custom-call | flops 671088640 | bytes 6291456 | tf_op jit(solution)/shard_map/pallas_call | solution.py:88
  208.6 4.3 %all-to-all-start.4 = ((bf16[32,48,128]{2,1,0:T(8,128)(2,1)}), bf16[32,48,128]{2,1,0:T(8,128)(2,1)S(1)}, u32[]{:S(2)}, u32[]{:S(2)}) async-start(bf16[32,48,128]{2,1,0:T(8,128)(2,1)} %bitcast.20), calls=%async_computation.4 | async-start | bytes 786432 | tf_op jit(solution)/shard_map/all_to_all | solution.py:885
  212.9 2.1 collective-permute-start.6
  216.0 3.7 shard_map.197
  219.7 6.9 %all-to-all-done.4.refs_1_.refs_2_ = bf16[32,48,128]{2,1,0:T(8,128)(2,1)S(1)} async-done(((bf16[32,48,128]{2,1,0:T(8,128)(2,1)}), bf16[32,48,128]{2,1,0:T(8,128)(2,1)S(1)}, u32[]{:S(2)}, u32[]{:S(2)}) %all-to-all-start.4) | async-done | bytes 393248 | tf_op jit(solution)/shard_map/all_to_all | solution.py:885
  226.6 6.7 %all-to-all-start.5 = ((bf16[64,16,512]{2,1,0:T(8,128)(2,1)}), bf16[64,16,512]{2,1,0:T(8,128)(2,1)S(1)}, u32[]{:S(2)}, u32[]{:S(2)}) async-start(bf16[64,16,512]{2,1,0:T(8,128)(2,1)} %shard_map.198.refs_7_.refs_1_), calls=%async_computation.5 | async-start | bytes 2097152 | tf_op jit(solution)/shard_map/all_to_all | solution.py:897
  233.3 2.7 add_convert_fusion.1.refs_0_
  237.2 9.9 %shard_map.199 = (bf16[32,96,128]{2,1,0:T(8,128)(2,1)}, f32[8,128]{1,0:T(8,128)}) custom-call(s32[2]{0:T(128)S(1)} %pad_add_fusion.refs_0_, bf16[32,96,128]{2,1,0:T(8,128)(2,1)S(1)} %copy-done.6, bf16[32,48,128]{2,1,0:T(8,128)(2,1)S(1)} %all-to-all-done.4.refs_1_.refs_2_, f32[4,64,512]{2,1,0:T(8,128)} %get-tuple-element.57.refs_3_, ...), custom_call_target="tpu_custom_call" | custom-call | flops 3355443200 | bytes 3145728 | tf_op jit(solution)/shard_map/pallas_call | solution.py:88
  247.1 5.8 %shard_map.202.refs_1_ = bf16[16,80,256]{2,1,0:T(8,128)(2,1)} custom-call(s32[2]{0:T(128)S(1)} %pad_add_fusion.2.refs_0_, bf16[16,2,64,1024]{3,2,1,0:T(8,128)(2,1)} %bitcast.60, bf16[32,96,128]{2,1,0:T(8,128)(2,1)} %get-tuple-element.61.refs_2_.refs_0_, f32[8,128]{1,0:T(8,128)} %get-tuple-element.62.refs_3_), custom_call_target="tpu_custom_call" | custom-call | flops 1073741824 | bytes 6291456 | tf_op jit(solution)/shard_map/pallas_call | solution.py:88
  252.9 2.0 copy.36.refs_0_
  254.9 11.0 %all-to-all-start.6 = ((bf16[16,80,256]{2,1,0:T(8,128)(2,1)}), bf16[16,80,256]{2,1,0:T(8,128)(2,1)S(1)}, u32[]{:S(2)}, u32[]{:S(2)}) async-start(bf16[16,80,256]{2,1,0:T(8,128)(2,1)} %shard_map.203), calls=%async_computation.6 | async-start | bytes 1310720 | tf_op jit(solution)/shard_map/all_to_all | solution.py:972
  265.9 3.9 %collective-permute-done.7 = bf16[512,1024]{1,0:T(8,128)(2,1)S(1)} collective-permute-done((bf16[512,1024]{1,0:T(8,128)(2,1)}, bf16[512,1024]{1,0:T(8,128)(2,1)S(1)}, u32[]{:S(2)}, u32[]{:S(2)}) %collective-permute-start.7) | collective-permute-done | bytes 1048608 | tf_op jit(solution)/shard_map/ppermute | solution.py:964
  269.7 1.7 add_convert_fusion
  272.4 11.9 %all-to-all-done.6.refs_0_ = bf16[16,80,256]{2,1,0:T(8,128)(2,1)S(1)} async-done(((bf16[16,80,256]{2,1,0:T(8,128)(2,1)}), bf16[16,80,256]{2,1,0:T(8,128)(2,1)S(1)}, u32[]{:S(2)}, u32[]{:S(2)}) %all-to-all-start.6) | async-done | bytes 655392 | tf_op jit(solution)/shard_map/all_to_all | solution.py:972
  284.3 2.0 shard_map.206
  286.3 7.5 %all-to-all-start.7 = ((bf16[64,96,256]{2,1,0:T(8,128)(2,1)}), bf16[64,96,256]{2,1,0:T(8,128)(2,1)S(1)}, u32[]{:S(2)}, u32[]{:S(2)}) async-start(bf16[64,96,256]{2,1,0:T(8,128)(2,1)} %get-tuple-element.63), calls=%async_computation.7 | async-start | bytes 6291456 | tf_op jit(solution)/shard_map/all_to_all | solution.py:897
  296.2 3.0 collective-permute-done.8.refs_2_
  299.2 3.8 shard_map.207
  303.1 31.3 %all-to-all-done.7.refs_0_ = bf16[64,96,256]{2,1,0:T(8,128)(2,1)S(1)} async-done(((bf16[64,96,256]{2,1,0:T(8,128)(2,1)}), bf16[64,96,256]{2,1,0:T(8,128)(2,1)S(1)}, u32[]{:S(2)}, u32[]{:S(2)}) %all-to-all-start.7) | async-done | bytes 3145760 | tf_op jit(solution)/shard_map/all_to_all | solution.py:897
  334.3 2.4 collective-permute-start.10
  336.7 5.8 %all-to-all-start.8 = ((bf16[32,96,128]{2,1,0:T(8,128)(2,1)}), bf16[32,96,128]{2,1,0:T(8,128)(2,1)}, u32[]{:S(2)}, u32[]{:S(2)}) async-start(bf16[32,96,128]{2,1,0:T(8,128)(2,1)} %shard_map.209), calls=%async_computation.8 | async-start | bytes 1572864 | tf_op jit(solution)/shard_map/all_to_all | solution.py:885
  342.5 5.2 %shard_map.211 = (f32[1024,2048]{1,0:T(8,128)}, f32[4,8,2,16,1024]{4,3,2,1,0:T(8,128)}, f32[8,128]{1,0:T(8,128)}) custom-call(s32[1]{0:T(128)} %bitcast.7.refs_0_, bf16[2,2,8,2,96,256]{5,4,3,2,1,0:T(8,128)(2,1)S(1)} %bitcast.46, bf16[1024,2048]{1,0:T(8,128)(2,1)} %refs_4_.5, f32[8,128]{1,0:T(8,128)} %bitcast.75), custom_call_target="tpu_custom_call" | custom-call | bytes 16777216 | tf_op jit(solution)/shard_map/pallas_call | solution.py:88
  347.7 12.4 %reduce-scatter.2.cloned.1.call-done = bf16[256,1024]{1,0:T(8,128)(2,1)} async-done(((bf16[4096,1024]{1,0:T(8,128)(2,1)}), bf16[256,1024]{1,0:T(8,128)(2,1)}) %reduce-scatter.2.cloned.1.call-update) | async-done | bytes 524304 | tf_op jit(solution)/shard_map/reduce_scatter | solution.py:957
  363.6 3.3 collective-permute-start.9
  366.9 6.0 %shard_map.213 = (f32[1024,2048]{1,0:T(8,128)}, f32[4,8,2,16,1024]{4,3,2,1,0:T(8,128)}, f32[8,128]{1,0:T(8,128)}) custom-call(s32[1]{0:T(128)S(6)} %sub.7.refs_0_, bf16[2,2,8,2,96,256]{5,4,3,2,1,0:T(8,128)(2,1)} %bitcast.33.refs_1_, bf16[1024,2048]{1,0:T(8,128)(2,1)} %refs_4_.5, f32[8,128]{1,0:T(8,128)} %bitcast.76, ...), custom_call_target="tpu_custom_call", output_to_operand_aliasing={{0}: (5, {}), {1}: (6, {})} | custom-call | bytes 16777216 | tf_op jit(solution)/shard_map/pallas_call | solution.py:88
  372.9 5.3 %shard_map.214 = (f32[128,1024]{1,0:T(8,128)}, bf16[128,1024]{1,0:T(8,128)(2,1)}) custom-call(bf16[2,8,2,96,128]{4,3,2,1,0:T(8,128)(2,1)} %bitcast.27.refs_0_, bf16[1024,2048]{1,0:T(8,128)(2,1)} %refs_4_.5, bf16[1024,2048]{1,0:T(8,128)(2,1)} %refs_4_.5, bf16[1024,2048]{1,0:T(8,128)(2,1)} %refs_4_.5, bf16[1024,2048]{1,0:T(8,128)(2,1)} %refs_4_.5, ...), custom_call_target="tpu_custom_call" | custom-call | flops 536870912 | bytes 6291456 | tf_op jit(solution)/shard_map/pallas_call | solution.py:88
  (77 shorter events, 20.7 us)
Async XLA Ops:
  7.2 127.4 %all-gather.5.cloned.1.call-start = ((), (), s32[]{:S(2)}) async-start(), calls=%async_computation.11 | async-start | bytes 10027008 | tf_op jit(solution)/shard_map/all_gather | solution.py:928
  7.2 11.6 %collective-permute-start = (bf16[128,1024]{1,0:T(8,128)(2,1)}, bf16[128,1024]{1,0:T(8,128)(2,1)S(1)}, u32[]{:S(2)}, u32[]{:S(2)}) collective-permute-start(bf16[128,1024]{1,0:T(8,128)(2,1)} %bitcast.69), channel_id=1, source_target_pairs={{0,65},{1,64},{64,1},{65,0},{2,67},{3,66},{66,3},{67,2},{4,69},{5,... | collective-permute-start | bytes 786440 | tf_op jit(solution)/shard_map/ppermute | solution.py:921
  13.4 5.4 %collective-permute-start.1 = (bf16[16,1024]{1,0:T(8,128)(2,1)}, bf16[16,1024]{1,0:T(8,128)(2,1)S(1)}, u32[]{:S(2)}, u32[]{:S(2)}) collective-permute-start(bf16[16,1024]{1,0:T(8,128)(2,1)} %get-tuple-element.42.refs_8_.refs_1_), channel_id=1, source_target_pairs={{0,65},{1,64},{64,1},{65,0},{2,67},{3,66},{66,3},{67,2},{4,69},{5,... | collective-permute-start | bytes 98312 | tf_op jit(solution)/shard_map/ppermute | solution.py:923
  18.6 9.9 %copy-start.13 = (s32[2]{0:T(128)S(1)}, s32[2]{0:T(128)}, u32[]{:S(2)}) copy-start(s32[2]{0:T(128)} %param.14) | copy-start | bytes 28
  20.7 22.3 %all-to-all-start = ((bf16[32,96,128]{2,1,0:T(8,128)(2,1)}), bf16[32,96,128]{2,1,0:T(8,128)(2,1)S(1)}, u32[]{:S(2)}, u32[]{:S(2)}) async-start(bf16[32,96,128]{2,1,0:T(8,128)(2,1)} %bitcast.64), calls=%async_computation | async-start | bytes 1572864 | tf_op jit(solution)/shard_map/all_to_all | solution.py:885
  28.5 26.0 %copy-start.11 = (bf16[128,1024]{1,0:T(8,128)(2,1)S(1)}, bf16[128,1024]{1,0:T(8,128)(2,1)}, u32[]{:S(2)}) copy-start(bf16[128,1024]{1,0:T(8,128)(2,1)} %get-tuple-element.46) | copy-start | bytes 786436
  43.0 6.2 %copy-start.5 = (bf16[32,96,128]{2,1,0:T(8,128)(2,1)}, bf16[32,96,128]{2,1,0:T(8,128)(2,1)S(1)}, u32[]{:S(2)}) copy-start(bf16[32,96,128]{2,1,0:T(8,128)(2,1)S(1)} %all-to-all-done.refs_1_) | copy-start | bytes 2359300
  49.1 14.8 %all-to-all-start.1 = ((bf16[32,32,128]{2,1,0:T(8,128)(2,1)}), bf16[32,32,128]{2,1,0:T(8,128)(2,1)S(1)}, u32[]{:S(2)}, u32[]{:S(2)}) async-start(bf16[32,32,128]{2,1,0:T(8,128)(2,1)} %get-tuple-element.44.refs_1_), calls=%async_computation.1 | async-start | bytes 524288 | tf_op jit(solution)/shard_map/all_to_all | solution.py:885
  55.1 5.8 %collective-permute-start.2 = (bf16[64,1024]{1,0:T(8,128)(2,1)S(1)}, bf16[64,1024]{1,0:T(8,128)(2,1)S(1)}, u32[]{:S(2)}, u32[]{:S(2)}) collective-permute-start(bf16[64,1024]{1,0:T(8,128)(2,1)S(1)} %get-tuple-element.77), channel_id=1, source_target_pairs={{0,1},{1,0},{2,3},{3,2},{4,5},{5,4},{6,7},{7,6},{8,9},{9,8},{10,11... | collective-permute-start | bytes 393224 | tf_op jit(solution)/shard_map/ppermute | solution.py:933
  68.7 65.8 %all-to-all-start.2 = ((bf16[32,48,1024]{2,1,0:T(8,128)(2,1)}), bf16[32,48,1024]{2,1,0:T(8,128)(2,1)S(1)}, u32[]{:S(2)}, u32[]{:S(2)}) async-start(bf16[32,48,1024]{2,1,0:T(8,128)(2,1)} %get-tuple-element.47), calls=%async_computation.2 | async-start | bytes 6291456 | tf_op jit(solution)/shard_map/all_to_all | solution.py:893
  76.3 170.8 %all-gather.7.cloned.1.call-start = ((), (), s32[]{:S(2)}) async-start(), calls=%async_computation.12 | async-start | bytes 4456448 | tf_op jit(solution)/shard_map/all_gather | solution.py:943
  76.3 11.1 %collective-permute-start.3 = (bf16[128,1024]{1,0:T(8,128)(2,1)}, bf16[128,1024]{1,0:T(8,128)(2,1)S(1)}, u32[]{:S(2)}, u32[]{:S(2)}) collective-permute-start(bf16[128,1024]{1,0:T(8,128)(2,1)} %get-tuple-element.48.refs_0_), channel_id=1, source_target_pairs={{0,32},{32,0},{1,33},{33,1},{2,34},{34,2},{3,35},{35,3},{4,36},{36... | collective-permute-start | bytes 786440 | tf_op jit(solution)/shard_map/ppermute | solution.py:919
  134.4 15.5 %copy-start.3 = (bf16[32,48,1024]{2,1,0:T(8,128)(2,1)}, bf16[32,48,1024]{2,1,0:T(8,128)(2,1)S(1)}, u32[]{:S(2)}) copy-start(bf16[32,48,1024]{2,1,0:T(8,128)(2,1)S(1)} %all-to-all-done.2) | copy-start | bytes 9437188
  150.0 54.4 %all-to-all-start.3 = ((bf16[32,48,1024]{2,1,0:T(8,128)(2,1)}), bf16[32,48,1024]{2,1,0:T(8,128)(2,1)S(1)}, u32[]{:S(2)}, u32[]{:S(2)}) async-start(bf16[32,48,1024]{2,1,0:T(8,128)(2,1)} %bitcast.63), calls=%async_computation.3 | async-start | bytes 6291456 | tf_op jit(solution)/shard_map/all_to_all | solution.py:893
  159.7 200.4 %reduce-scatter.2.cloned.1.call-start = ((), (), s32[]{:S(2)}) async-start(), calls=%async_computation.10 | async-start | bytes 8912896 | tf_op jit(solution)/shard_map/reduce_scatter | solution.py:957
  159.9 1.9 copy-start.4
  172.8 4.3 %collective-permute-start.4 = (bf16[768,1024]{1,0:T(8,128)(2,1)}, bf16[768,1024]{1,0:T(8,128)(2,1)S(1)}, u32[]{:S(2)}, u32[]{:S(2)}) collective-permute-start(bf16[768,1024]{1,0:T(8,128)(2,1)} %get-tuple-element.55), channel_id=1, source_target_pairs={{0,32},{32,0},{1,33},{33,1},{2,34},{34,2},{3,35},{35,3},{4,36},{36... | collective-permute-start | bytes 4718600 | tf_op jit(solution)/shard_map/ppermute | solution.py:919
  177.2 1.1 copy-start.10
  179.5 13.3 %collective-permute-start.5 = (bf16[256,1024]{1,0:T(8,128)(2,1)S(1)}, bf16[256,1024]{1,0:T(8,128)(2,1)S(1)}, u32[]{:S(2)}, u32[]{:S(2)}) collective-permute-start(bf16[256,1024]{1,0:T(8,128)(2,1)S(1)} %add_convert_fusion.3), channel_id=1, source_target_pairs={{0,64},{64,0},{1,65},{65,1},{2,66},{66,2},{3,67},{67,3},{4,68},{68... | collective-permute-start | bytes 1572872 | tf_op jit(solution)/shard_map/ppermute | solution.py:951
  193.1 0.8 copy-start.8
  208.6 4.3 %copy-start.12 = (bf16[128,512]{1,0:T(8,128)(2,1)S(1)}, bf16[128,512]{1,0:T(8,128)(2,1)}, u32[]{:S(2)}) copy-start(bf16[128,512]{1,0:T(8,128)(2,1)} %get-tuple-element.60) | copy-start | bytes 393220
  208.6 18.0 %all-to-all-start.4 = ((bf16[32,48,128]{2,1,0:T(8,128)(2,1)}), bf16[32,48,128]{2,1,0:T(8,128)(2,1)S(1)}, u32[]{:S(2)}, u32[]{:S(2)}) async-start(bf16[32,48,128]{2,1,0:T(8,128)(2,1)} %bitcast.20), calls=%async_computation.4 | async-start | bytes 786432 | tf_op jit(solution)/shard_map/all_to_all | solution.py:885
  212.9 20.3 %copy-start.9 = (bf16[768,1024]{1,0:T(8,128)(2,1)S(1)}, bf16[768,1024]{1,0:T(8,128)(2,1)}, u32[]{:S(2)}) copy-start(bf16[768,1024]{1,0:T(8,128)(2,1)} %get-tuple-element.54) | copy-start | bytes 4718596
  212.9 3.0 collective-permute-start.6
  226.6 28.3 %all-to-all-start.5 = ((bf16[64,16,512]{2,1,0:T(8,128)(2,1)}), bf16[64,16,512]{2,1,0:T(8,128)(2,1)S(1)}, u32[]{:S(2)}, u32[]{:S(2)}) async-start(bf16[64,16,512]{2,1,0:T(8,128)(2,1)} %shard_map.198.refs_7_.refs_1_), calls=%async_computation.5 | async-start | bytes 2097152 | tf_op jit(solution)/shard_map/all_to_all | solution.py:897
  233.3 3.9 %copy-start.6 = (bf16[32,96,128]{2,1,0:T(8,128)(2,1)S(1)}, bf16[32,96,128]{2,1,0:T(8,128)(2,1)}, u32[]{:S(2)}) copy-start(bf16[32,96,128]{2,1,0:T(8,128)(2,1)} %copy-done.5) | copy-start | bytes 2359300
  236.0 33.8 %collective-permute-start.7 = (bf16[512,1024]{1,0:T(8,128)(2,1)}, bf16[512,1024]{1,0:T(8,128)(2,1)S(1)}, u32[]{:S(2)}, u32[]{:S(2)}) collective-permute-start(bf16[512,1024]{1,0:T(8,128)(2,1)} %shard_map.204.refs_0_), channel_id=1, source_target_pairs={{0,64},{64,0},{1,65},{65,1},{2,66},{66,2},{3,67},{67,3},{4,68},{68... | collective-permute-start | bytes 3145736 | tf_op jit(solution)/shard_map/ppermute | solution.py:964
  254.9 29.4 %all-to-all-start.6 = ((bf16[16,80,256]{2,1,0:T(8,128)(2,1)}), bf16[16,80,256]{2,1,0:T(8,128)(2,1)S(1)}, u32[]{:S(2)}, u32[]{:S(2)}) async-start(bf16[16,80,256]{2,1,0:T(8,128)(2,1)} %shard_map.203), calls=%async_computation.6 | async-start | bytes 1310720 | tf_op jit(solution)/shard_map/all_to_all | solution.py:972
  271.4 1.0 copy-start.7
  286.3 48.1 %all-to-all-start.7 = ((bf16[64,96,256]{2,1,0:T(8,128)(2,1)}), bf16[64,96,256]{2,1,0:T(8,128)(2,1)S(1)}, u32[]{:S(2)}, u32[]{:S(2)}) async-start(bf16[64,96,256]{2,1,0:T(8,128)(2,1)} %get-tuple-element.63), calls=%async_computation.7 | async-start | bytes 6291456 | tf_op jit(solution)/shard_map/all_to_all | solution.py:897
  295.3 3.9 %collective-permute-start.8 = (bf16[768,1024]{1,0:T(8,128)(2,1)S(1)}, bf16[768,1024]{1,0:T(8,128)(2,1)S(1)}, u32[]{:S(2)}, u32[]{:S(2)}) collective-permute-start(bf16[768,1024]{1,0:T(8,128)(2,1)S(1)} %pad_maximum_fusion.refs_1_), channel_id=1, source_target_pairs={{0,32},{32,0},{1,33},{33,1},{2,34},{34,2},{3,35},{35,3},{4,36},{36... | collective-permute-start | bytes 4718600 | tf_op jit(solution)/shard_map/ppermute | solution.py:919
  334.3 32.6 %collective-permute-start.10 = (bf16[64,96,256]{2,1,0:T(8,128)(2,1)S(1)}, bf16[64,96,256]{2,1,0:T(8,128)(2,1)}, u32[]{:S(2)}, u32[]{:S(2)}) collective-permute-start(bf16[64,96,256]{2,1,0:T(8,128)(2,1)S(1)} %shard_map.208), channel_id=1, source_target_pairs={{0,32},{32,0},{1,33},{33,1},{2,34},{34,2},{3,35},{35,3},{4,36},{36... | collective-permute-start | bytes 9437192 | tf_op jit(solution)/shard_map/ppermute | solution.py:919
  336.7 36.2 %all-to-all-start.8 = ((bf16[32,96,128]{2,1,0:T(8,128)(2,1)}), bf16[32,96,128]{2,1,0:T(8,128)(2,1)}, u32[]{:S(2)}, u32[]{:S(2)}) async-start(bf16[32,96,128]{2,1,0:T(8,128)(2,1)} %shard_map.209), calls=%async_computation.8 | async-start | bytes 1572864 | tf_op jit(solution)/shard_map/all_to_all | solution.py:885
  360.1 1.0 copy-start
  361.1 0.8 copy-start.1
  363.6 9.3 %collective-permute-start.9 = (bf16[128,1024]{1,0:T(8,128)(2,1)}, bf16[128,1024]{1,0:T(8,128)(2,1)S(1)}, u32[]{:S(2)}, u32[]{:S(2)}) collective-permute-start(bf16[128,1024]{1,0:T(8,128)(2,1)} %slice_bitcast_fusion.1), channel_id=1, source_target_pairs={{0,65},{1,64},{64,1},{65,0},{2,67},{3,66},{66,3},{67,2},{4,69},{5,... | collective-permute-start | bytes 786440 | tf_op jit(solution)/shard_map/ppermute | solution.py:982
  366.9 6.0 %copy-start.2 = (bf16[2,128,1024]{2,1,0:T(8,128)(2,1)S(1)}, bf16[2,128,1024]{2,1,0:T(8,128)(2,1)}, u32[]{:S(2)}) copy-start(bf16[2,128,1024]{2,1,0:T(8,128)(2,1)} %copy-done.1) | copy-start | bytes 1572868
Sparse Core Ops, SparseCore 0:
  20.8 113.7 all-gather.4
  150.1 83.3 all-gather.6
  236.9 123.1 reduce-scatter.1
